TPU v7x, 32 devices: a whole 2x2x4 slice. The times are simulated.
32 devices in a mesh: fsdp: 4 (over y, core), ctx: 8 (over z, x).
Axes of the slice: x: 2, y: 2, z: 4, core: 2. Of those that a mesh axis runs over, the one named last changes fastest.
Arguments:
- tokens: bfloat16 [4, 1024, 4096], P('fsdp', 'ctx'), may hold values from -6 to 6
- segments: int32 [4, 1024], P(None, 'ctx'), may hold values from 0 to 7, never falling along the last dimension, each value on 1 to 512 neighbouring positions
- gate_weight: bfloat16 [4096, 4096], P(None, 'fsdp'), may hold values from -0.09375 to 0.09375
- value_weight: bfloat16 [4096, 4096], P(None, 'fsdp'), may hold values from -0.09375 to 0.09375
- coupling_weight: bfloat16 [4096, 2048], P(None, 'fsdp'), may hold values from -0.09375 to 0.09375
- step_weight: bfloat16 [4096, 64], P(None, 'fsdp'), may hold values from -0.09375 to 0.09375
- value_conv: bfloat16 [4, 4096], P(None, 'fsdp'), may hold values from -3 to 3
- coupling_conv: bfloat16 [4, 2048], P(None, 'fsdp'), may hold values from -3 to 3
- value_shift: float32 [4096], P('fsdp'), may hold values from -3 to 3
- coupling_shift: float32 [2048], P('fsdp'), may hold values from -3 to 3
- step_bias: float32 [64], P('fsdp'), may hold values from -4.5 to -1.5
- decay_log: float32 [64], P('fsdp'), may hold values from -4.6 to 2.3
- skip_gain: float32 [64], P('fsdp'), may hold values from 0.5 to 1.5
- norm_gain: float32 [4096], P('fsdp'), may hold values from 0.1 to 1.9
- out_weight: bfloat16 [4096, 4096], P('fsdp'), may hold values from -0.09375 to 0.09375
- rezero: float32 [1], replicated, may hold values from 0.5 to 1.5
Outputs:
- mixed: bfloat16 [4, 1024, 4096], P('fsdp', 'ctx')
Inputs may be any that keep to these rules, and one draw needn't show every extreme that they name: `segments`: along each stream the ids never fall; every document has 1 to 512 tokens and one of them exactly 512.
All inputs are finite; a program needn't handle non-finite values.
Results may differ from a plain program's by a relative error of at most 0.0064.
Values may be sent and summed in bfloat16 or wider, within the bound.
No kernel may reach another device: no remote copies, remote signals or barrier semaphores. Data moves between devices by JAX's collectives and lax.ppermute only.
A program may use at most 128 MiB of HBM per device.

v0:
```python
import jax
import jax.numpy as jnp
from jax import lax
from jax.sharding import PartitionSpec as P

P_SIZE = 64
N = 128
CH = 128


epsilon = 1e-05
highest = lax.Precision.HIGHEST


def shifted(block, axis, distance):
    devices = range(lax.axis_size(axis))
    route = [(i - distance, i) for i in devices if i - distance in devices]
    return lax.ppermute(block, axis, route)


def carried_in(part, axis, combine, identity):
    place = lax.axis_index(axis)
    gathered = jax.tree.map(lambda a: lax.all_gather(a, axis), part)
    state = jax.tree.map(lambda a, e: jnp.zeros_like(a) + jnp.asarray(e, a.dtype), part, identity)

    def one(step, state):
        return combine(
            state, jax.tree.map(lambda a: lax.dynamic_index_in_dim(a, step, 0, False), gathered)
        )

    return lax.fori_loop(0, place, one, state)


def stretch_update(
    state, previous, values, couple_in, couple_out, steps, decays, stretch_ids, per_group
):
    length = values.shape[0]
    cumulative = jnp.cumsum(decays, axis=0)
    position = lax.broadcasted_iota(jnp.int32, (length, length), 0)
    source = lax.broadcasted_iota(jnp.int32, (length, length), 1)
    visible = jnp.logical_and(stretch_ids[:, None] == stretch_ids[None, :], position >= source)[
        :, :, None
    ]
    spread = cumulative[:, None, :] - cumulative[None, :, :]
    damping = jnp.where(visible, jnp.exp(jnp.where(visible, spread, 0.0)), 0.0)
    scores = jnp.einsum("tgn,sgn->tsg", couple_out, couple_in, precision=highest)
    scores = jnp.repeat(scores, per_group, axis=2)
    mixing = scores * damping * steps[None, :, :]
    result = jnp.einsum("tsh,shp->thp", mixing, values, precision=highest)
    kept = (stretch_ids == previous).astype(jnp.float32)
    growth = kept[:, None] * jnp.exp(cumulative)
    query_heads = jnp.repeat(couple_out, per_group, axis=1)
    result = result + growth[:, :, None] * jnp.einsum(
        "thn,hpn->thp", query_heads, state, precision=highest
    )
    tail_weight = (
        (stretch_ids == stretch_ids[-1]).astype(jnp.float32)[:, None]
        * jnp.exp(cumulative[-1][None, :] - cumulative)
        * steps
    )
    key_heads = jnp.repeat(couple_in, per_group, axis=1)
    renewed = growth[-1][:, None, None] * state + jnp.einsum(
        "sh,shp,shn->hpn", tail_weight, values, key_heads, precision=highest
    )
    return (renewed, result, growth)


def causal_mix(padded, padded_ids, weight, shift_term):
    reach = weight.shape[0] - 1
    length = padded.shape[-2] - reach
    own_ids = padded_ids[..., reach:]
    running = jnp.zeros(padded[..., reach:, :].shape, jnp.float32) + shift_term
    for offset in range(reach + 1):
        window = padded[..., offset : offset + length, :].astype(jnp.float32)
        matching = (padded_ids[..., offset : offset + length] == own_ids).astype(jnp.float32)
        running = running + weight[offset].astype(jnp.float32) * window * matching[..., None]
    return jax.nn.silu(running).astype(jnp.bfloat16)


def on_device(
    tokens,
    segments,
    gate_weight,
    value_weight,
    coupling_weight,
    step_weight,
    value_conv,
    coupling_conv,
    value_shift,
    coupling_shift,
    step_bias,
    decay_log,
    skip_gain,
    norm_gain,
    out_weight,
    rezero,
):
    inner_width = gate_weight.shape[1]
    coupling_width = coupling_weight.shape[1]
    head_count = step_weight.shape[1]
    group_count = coupling_width // (2 * N)
    per_group = head_count // group_count
    reach = value_conv.shape[0] - 1
    stream_count, token_count = segments.shape
    block_rows = lax.all_gather(tokens, "fsdp", axis=0, tiled=True)
    flat_rows = block_rows.reshape(-1, block_rows.shape[-1])
    projected_parts = [
        jnp.dot(flat_rows, matrix, preferred_element_type=jnp.float32).astype(jnp.bfloat16)
        for matrix in (gate_weight, value_weight, coupling_weight, step_weight)
    ]
    projected = jnp.concatenate(projected_parts, axis=1).reshape(
        block_rows.shape[0], block_rows.shape[1], -1
    )
    gate_proj = projected[:, :, :inner_width]
    value_proj = projected[:, :, inner_width : 2 * inner_width]
    coupling_proj = projected[:, :, 2 * inner_width : 2 * inner_width + coupling_width]
    step_proj = projected[:, :, 2 * inner_width + coupling_width :]
    prior_value, prior_coupling, prior_ids = shifted(
        (
            value_proj[:, -reach:],
            coupling_proj[:, -reach:],
            segments[:, -reach:].astype(jnp.bfloat16),
        ),
        "ctx",
        1,
    )
    padded_ids = jnp.concatenate([prior_ids.astype(jnp.int32), segments], axis=1)
    value_mixed = causal_mix(
        jnp.concatenate([prior_value, value_proj], axis=1), padded_ids, value_conv, value_shift
    )
    coupling_mixed = causal_mix(
        jnp.concatenate([prior_coupling, coupling_proj], axis=1),
        padded_ids,
        coupling_conv,
        coupling_shift,
    )
    step_sizes = jax.nn.softplus(step_proj.astype(jnp.float32) + step_bias)
    decays = step_sizes * -jnp.exp(decay_log)
    values = value_mixed.astype(jnp.float32).reshape(stream_count, token_count, head_count, P_SIZE)
    coupled = coupling_mixed.astype(jnp.float32).reshape(
        stream_count, token_count, group_count, 2, N
    )
    couple_in = coupled[:, :, :, 0]
    couple_out = coupled[:, :, :, 1]
    stretches = token_count // CH

    def local_stream(
        stream_values, stream_in, stream_out, stream_steps, stream_decays, stream_ids, previous
    ):

        def advance(carried, inputs):
            state, prior, leading = carried
            stretch_values, stretch_in, stretch_out, stretch_steps, stretch_decays, stretch_ids = (
                inputs
            )
            renewed, result, growth = stretch_update(
                state,
                prior,
                stretch_values,
                stretch_in,
                stretch_out,
                stretch_steps,
                stretch_decays,
                stretch_ids,
                per_group,
            )
            return (
                (renewed, stretch_ids[-1], leading * growth[-1]),
                (result, leading[None, :] * growth),
            )

        inputs = (
            stream_values.reshape(stretches, CH, head_count, P_SIZE),
            stream_in.reshape(stretches, CH, group_count, N),
            stream_out.reshape(stretches, CH, group_count, N),
            stream_steps.reshape(stretches, CH, head_count),
            stream_decays.reshape(stretches, CH, head_count),
            stream_ids.reshape(stretches, CH),
        )
        initial = (
            jnp.zeros((head_count, P_SIZE, N), jnp.float32),
            previous,
            jnp.ones((head_count,), jnp.float32),
        )
        (end_state, latest, leading), (results, factors) = lax.scan(advance, initial, inputs)
        return (
            end_state,
            leading,
            results.reshape(token_count, head_count, P_SIZE),
            factors.reshape(token_count, head_count),
        )

    end_states, lead_factors, local_heads, entry_factors = jax.vmap(local_stream)(
        values, couple_in, couple_out, step_sizes, decays, segments, padded_ids[:, reach - 1]
    )

    def chain(earlier, later):
        return (earlier[0] * later[0], later[0][:, :, None, None] * earlier[1] + later[1])

    carried_lead, entry_state = carried_in(
        (lead_factors, end_states),
        "ctx",
        chain,
        (jnp.ones_like(lead_factors), jnp.zeros_like(end_states)),
    )
    query_heads = jnp.repeat(couple_out, per_group, axis=2)
    scanned = (
        local_heads
        + entry_factors[..., None]
        * jnp.einsum("bthn,bhpn->bthp", query_heads, entry_state, precision=highest)
        + skip_gain[None, None, :, None] * values
    )
    gated = scanned * jax.nn.silu(gate_proj.astype(jnp.float32)).reshape(
        stream_count, token_count, head_count, P_SIZE
    )
    grouped = gated.reshape(stream_count, token_count, group_count, per_group * P_SIZE)
    scale = lax.rsqrt(jnp.mean(grouped * grouped, axis=-1, keepdims=True) + epsilon)
    normed = ((grouped * scale).reshape(stream_count, token_count, inner_width) * norm_gain).astype(
        jnp.bfloat16
    )
    branch = lax.psum_scatter(
        jnp.einsum("btk,kd->btd", normed, out_weight, preferred_element_type=jnp.float32),
        "fsdp",
        scatter_dimension=0,
        tiled=True,
    )
    return (tokens.astype(jnp.float32) + rezero[0] * branch).astype(jnp.bfloat16)


def solution(mesh):
    return jax.shard_map(
        on_device,
        mesh=mesh,
        in_specs=(
            P("fsdp", "ctx", None),
            P(None, "ctx"),
            P(None, "fsdp"),
            P(None, "fsdp"),
            P(None, "fsdp"),
            P(None, "fsdp"),
            P(None, "fsdp"),
            P(None, "fsdp"),
            P("fsdp"),
            P("fsdp"),
            P("fsdp"),
            P("fsdp"),
            P("fsdp"),
            P("fsdp"),
            P("fsdp", None),
            P(),
        ),
        out_specs=P("fsdp", "ctx", None),
        check_vma=False,
    )
```

profile of v0, /device:TPU:0, one launch (start us, length us, event | category | flops | bytes accessed | tf_op | source)
XLA Modules:
  0.0 452.1 jit_solution(6012988512100327844)
XLA Ops:
  8.1 4.8 %collective-permute-start.1 = (bf16[4,3]{1,0:T(4,128)(2,1)S(1)}, bf16[4,3]{1,0:T(4,128)(2,1)S(1)}, u32[]{:S(2)}, u32[]{:S(2)}) collective-permute-start(bf16[4,3]{1,0:T(4,128)(2,1)S(1)} %slice.109), channel_id=1, source_target_pairs={{0,1},{1,2},{2,3},{3,4},{4,5},{5,6},{6,7},{8,9},{9,10},{10,11},{11... | collective-permute-start | bytes 80 | tf_op jit(solution)/shard_map/ppermute | solution.py:18
  12.9 0.9 slice_reduce_fusion
  16.4 0.9 fusion.39
  17.3 28.9 %all-gather.5.cloned.1.call-done = bf16[4,128,4096]{2,1,0:T(8,128)(2,1)} async-done(((bf16[1,128,4096]{2,1,0:T(8,128)(2,1)}), bf16[4,128,4096]{2,1,0:T(8,128)(2,1)}) %all-gather.5.cloned.1.call-update) | async-done | bytes 4194320 | tf_op jit(solution)/shard_map/all_gather | solution.py:105
  46.2 3.4 convolution_convert_fusion.3
  49.7 5.9 %convolution_convert_fusion.2 = bf16[512,512]{1,0:T(8,128)(2,1)S(1)} fusion(bf16[512,4096]{1,0:T(8,128)(2,1)} %bitcast.96, bf16[4096,512]{1,0:T(8,128)(2,1)} %param.22), kind=kOutput, calls=%fused_computation.40 | convolution fusion | flops 2147745792 | bytes 8912896 | tf_op jit(solution)/shard_map/dot_general | solution.py:108
  55.6 7.2 %convolution_convert_fusion = bf16[512,1024]{1,0:T(8,128)(2,1)S(1)} fusion(bf16[512,4096]{1,0:T(8,128)(2,1)S(1)} %bitcast.97, bf16[4096,1024]{1,0:T(8,128)(2,1)} %param.21), kind=kOutput, calls=%fused_computation.38 | convolution fusion | flops 4295491584 | bytes 13631488 | tf_op jit(solution)/shard_map/dot_general | solution.py:108
  62.8 4.5 convolution_convert_fusion.1
  68.6 3.4 collective-permute-start
  72.1 3.6 collective-permute-start.2
  76.5 1.1 slice.138
  77.7 1.8 multiply_convert_fusion.3
  79.4 1.3 copy.79
  80.8 1.1 slice_bitcast_fusion
  81.9 2.0 copy.90
  84.0 5.7 %multiply_convert_fusion.1 = bf16[4,128,1024]{2,1,0:T(8,128)(2,1)} fusion(bf16[4,128,1024]{2,1,0:T(8,128)(2,1)} %slice.138, bf16[4,3,1024]{2,1,0:T(4,128)(2,1)S(1)} %collective-permute-done, f32[1024]{0:T(1024)S(1)} %bitcast.102, f32[4,128]{1,0:T(4,128)S(1)} %get-tuple-element.111, f32[1024]{0:T(1024)S(1)} %bitcast.103, f32[4,128]{1,0:T(4,128)S(1)} %get-tuple-element.112, ...), kind=kLoop, calls=%fused_computation.33 | loop fusion | flops 15204352 | bytes 2148352 | tf_op jit(solution)/shard_map/convert_element_type | solution.py:77
  89.7 2.3 copy.78
  92.0 1.6 broadcast_in_dim.92
  93.6 5.4 %fusion.22 = f32[4,16,64,128]{3,2,1,0:T(8,128)} fusion(f32[4,128,16,128]{3,1,2,0:T(8,128)S(1)} %bitcast.79, bf16[4,128,16,64]{1,3,2,0:T(8,128)(2,1)S(1)} %bitcast.86, f32[4,128,16]{1,2,0:T(8,128)S(1)} %get-tuple-element.100, f32[4,16]{1,0:T(4,128)S(1)} %bitcast.109), kind=kOutput, calls=%fused_computation.35 | convolution fusion | flops 806879232 | bytes 7373056 | tf_op jit(solution)/shard_map/vmap()/while/body/eval_jaxpr/sh,shp,shn->hpn/dot_general | solution.py:62
  99.8 1.0 copy.87
  100.9 1.9 convert_multiply_fusion
  102.8 3.0 copy.91
  105.8 27.9 %all-gather = f32[32,1,16]{2,1,0:T(1,128)S(1)} all-gather(f32[4,1,16]{2,1,0:T(1,128)S(1)} %get-tuple-element.99), channel_id=2, replica_groups=mesh['fsdp'=4,'ctx'=8] {'ctx'}, dimensions={0}, use_global_device_ids=true | all-gather | bytes 2304 | tf_op jit(solution)/shard_map/all_gather | solution.py:23
  134.9 9.6 %fusion.27 = f32[4,16,64,128]{3,2,1,0:T(8,128)} fusion(f32[4,128,16,128]{3,1,2,0:T(8,128)S(1)} %bitcast.77), kind=kOutput, calls=%fused_computation.48 | convolution fusion | flops 805306368 | bytes 6291456 | tf_op jit(solution)/shard_map/vmap()/while/body/eval_jaxpr/thn,hpn->thp/dot_general | solution.py:53
  145.8 6.1 %fusion.2 = f32[4,16,64,128]{3,2,1,0:T(8,128)} fusion(bf16[4,128,16,64]{1,3,2,0:T(8,128)(2,1)S(1)} %bitcast.87, f32[4,128,128,16]{2,1,3,0:T(8,128)S(1)} %bitcast.94, f32[4,128,16]{1,2,0:T(8,128)S(1)} %get-tuple-element.101, f32[4,128,16]{1,2,0:T(8,128)S(1)} %copy.85, pred[4,128,128]{2,1,0:T(8,128)(4,1)S(1)} %compare_and_fusion), kind=kOutput, calls=%fused_computation.4 | convolution fusion | flops 810549248 | bytes 7471104 | tf_op jit(solution)/shard_map/vmap()/while/body/eval_jaxpr/tsh,shp->thp/dot_general | solution.py:49
  151.8 175.3 %all-gather.7.cloned.1.call-done = f32[32,16,64,128]{3,2,1,0:T(8,128)} async-done(((f32[4,16,64,128]{3,2,1,0:T(8,128)}), f32[32,16,64,128]{3,2,1,0:T(8,128)}) %all-gather.7.cloned.1.call-update) | async-done | bytes 16777232 | tf_op jit(solution)/shard_map/all_gather | solution.py:23
  328.0 11.9 %multiply_reduce_fusion = (f32[4,128,16]{1,2,0:T(8,128)S(1)}, f32[4,128,16,64]{1,3,2,0:T(8,128)}) fusion(f32[4,128,16,64]{1,3,2,0:T(8,128)} %bitcast.89, bf16[4,128,16,64]{1,3,2,0:T(8,128)(2,1)S(1)} %bitcast.88, f32[16]{0:T(128)S(1)} %copy-done.13, f32[4,16,64,128]{3,2,1,0:T(8,128)S(1)} %get-tuple-element.85, f32[4,128,16,128]{3,1,2,0:T(8,128)} %bitcast.78, ...), kind=kOutput, calls=%fused_computation.28 | convolution fusion | flops 810541056 | bytes 15794240 | tf_op jit(solution)/shard_map/bthn,bhpn->bthp/dot_general | solution.py:210
  339.9 3.0 copy.94
  343.8 2.8 mul.333
  346.6 12.4 %fusion = f32[4,128,4096]{2,1,0:T(8,128)} fusion(bf16[1024,4096]{1,0:T(8,128)(2,1)} %param.32, f32[4,128,1024]{2,1,0:T(8,128)} %copy.94, f32[4,128,1024]{2,1,0:T(8,128)} %mul.333, f32[1024]{0:T(1024)S(1)} %copy-done.14), kind=kOutput, calls=%fused_computation.2 | convolution fusion | flops 4296540160 | bytes 20975616 | tf_op jit(solution)/shard_map/btk,kd->btd/dot_general | solution.py:222
  359.8 83.0 %reduce-scatter.2.cloned.1.call-done = f32[1,128,4096]{2,1,0:T(8,128)} async-done(((f32[4,128,4096]{2,1,0:T(8,128)}), f32[1,128,4096]{2,1,0:T(8,128)}) %reduce-scatter.2.cloned.1.call-update) | async-done | bytes 2097168 | tf_op jit(solution)/shard_map/reduce_scatter | solution.py:221
  442.8 2.9 add_convert_fusion
  (80 shorter events, 11.5 us)
Async XLA Ops:
  6.5 39.6 %copy-start = (bf16[4096,16]{0,1:T(8,128)(2,1)S(1)}, bf16[4096,16]{0,1:T(8,128)(2,1)}, u32[]{:S(2)}) copy-start(bf16[4096,16]{0,1:T(8,128)(2,1)} %param.23) | copy-start | bytes 393220
  6.5 39.6 %all-gather.5.cloned.1.call-start = ((), (), s32[]{:S(2)}) async-start(), calls=%async_computation.1 | async-start | bytes 5242880 | tf_op jit(solution)/shard_map/all_gather | solution.py:105
  7.3 319.8 %all-gather.7.cloned.1.call-start = ((), (), s32[]{:S(2)}) async-start(), calls=%async_computation.3 | async-start | bytes 18874368 | tf_op jit(solution)/shard_map/all_gather | solution.py:23
  8.1 8.1 %collective-permute-start.1 = (bf16[4,3]{1,0:T(4,128)(2,1)S(1)}, bf16[4,3]{1,0:T(4,128)(2,1)S(1)}, u32[]{:S(2)}, u32[]{:S(2)}) collective-permute-start(bf16[4,3]{1,0:T(4,128)(2,1)S(1)} %slice.109), channel_id=1, source_target_pairs={{0,1},{1,2},{2,3},{3,4},{4,5},{5,6},{6,7},{8,9},{9,10},{10,11},{11... | collective-permute-start | bytes 80 | tf_op jit(solution)/shard_map/ppermute | solution.py:18
  49.7 6.0 %copy-start.6 = (bf16[4,128,4096]{2,1,0:T(8,128)(2,1)S(1)}, bf16[4,128,4096]{2,1,0:T(8,128)(2,1)}, u32[]{:S(2)}) copy-start(bf16[4,128,4096]{2,1,0:T(8,128)(2,1)} %all-gather.5.cloned.1.call-done) | copy-start | bytes 12582916
  49.7 13.1 %slice-start = ((s8[8388608]{0:T(1024)(128)(4,1)}), s8[4194304]{0:T(1024)(128)(4,1)S(1)}, s32[]{:S(2)}) async-start(s8[8388608]{0:T(1024)(128)(4,1)} %bitcast.110), calls=%async_computation.4 | async-start | bytes 8388608
  55.6 7.2 %slice-start.1 = ((s8[8388608]{0:T(1024)(128)(4,1)}), s8[4194304]{0:T(1024)(128)(4,1)S(1)}, s32[]{:S(2)}) async-start(s8[8388608]{0:T(1024)(128)(4,1)} %bitcast.110), calls=%async_computation.5 | async-start | bytes 8388608
  67.3 0.7 copy-start.12
  68.5 9.2 %copy-start.11 = (f32[512]{0:T(512)S(1)}, f32[512]{0:T(512)}, u32[]{:S(2)}) copy-start(f32[512]{0:T(512)} %param.27) | copy-start | bytes 6148
  68.6 15.4 %collective-permute-start = (bf16[4,3,1024]{2,1,0:T(4,128)(2,1)S(1)}, bf16[4,3,1024]{2,1,0:T(4,128)(2,1)S(1)}, u32[]{:S(2)}, u32[]{:S(2)}) collective-permute-start(bf16[4,3,1024]{2,1,0:T(4,128)(2,1)S(1)} %slice.137), channel_id=1, source_target_pairs={{0,1},{1,2},{2,3},{3,4},{4,5},{5,6},{6,7},{8,9},{9,10},{10,11},{11... | collective-permute-start | bytes 73736 | tf_op jit(solution)/shard_map/ppermute | solution.py:18
  72.1 4.3 copy-start.8
  72.1 5.5 %collective-permute-start.2 = (bf16[4,3,512]{2,1,0:T(4,128)(2,1)S(1)}, bf16[4,3,512]{2,1,0:T(4,128)(2,1)S(1)}, u32[]{:S(2)}, u32[]{:S(2)}) collective-permute-start(bf16[4,3,512]{2,1,0:T(4,128)(2,1)S(1)} %slice.147), channel_id=1, source_target_pairs={{0,1},{1,2},{2,3},{3,4},{4,5},{5,6},{6,7},{8,9},{9,10},{10,11},{11... | collective-permute-start | bytes 36872 | tf_op jit(solution)/shard_map/ppermute | solution.py:18
  80.7 3.2 copy-start.10
  92.0 1.6 copy-start.3
  99.0 0.7 copy-start.9
  99.0 343.7 %reduce-scatter.2.cloned.1.call-start = ((), (), s32[]{:S(2)}) async-start(), calls=%async_computation.2 | async-start | bytes 10485760 | tf_op jit(solution)/shard_map/reduce_scatter | solution.py:221
  102.8 30.9 %copy-start.7 = (f32[4,128,2,128]{1,3,2,0:T(8,128)S(1)}, f32[4,128,2,128]{1,3,2,0:T(8,128)}, u32[]{:S(2)}) copy-start(f32[4,128,2,128]{1,3,2,0:T(8,128)} %get-tuple-element.97) | copy-start | bytes 1572868
  134.9 9.7 %copy-start.2 = (f32[4,128,2,8,128]{4,1,3,2,0:T(8,128)}, f32[4,128,2,8,128]{4,1,3,2,0:T(8,128)S(1)}, u32[]{:S(2)}) copy-start(f32[4,128,2,8,128]{4,1,3,2,0:T(8,128)S(1)} %broadcast_in_dim.67) | copy-start | bytes 12582916
  144.5 1.2 copy-start.4
  327.3 0.7 copy-start.13
  343.8 2.8 copy-start.14
  359.0 83.8 %copy-start.5 = (bf16[1,128,4096]{2,1,0:T(8,128)(2,1)S(1)}, bf16[1,128,4096]{2,1,0:T(8,128)(2,1)}, u32[]{:S(2)}) copy-start(bf16[1,128,4096]{2,1,0:T(8,128)(2,1)} %param.18) | copy-start | bytes 3145732
  442.8 2.9 copy-start.1
Sparse Core Ops, SparseCore 0:
  8.9 37.1 all-gather.4
  99.2 227.8 all-gather.6
  359.2 83.5 reduce-scatter.1
where the time goes:
time: 453 us; the launch traced here: 452 us
  waiting for transfers between devices  288 us (64%)
  matrix products  66.6 us (15%)
  blocking collectives  27.9 us (6%)
  local copies, waits for them, and re-layouts  25.4 us (6%)
  other arithmetic  18 us (4%)
  between operations  14.3 us (3%)
  starting transfers between devices  11.9 us (3%)
    all_gather x1, waiting for transfers between devices, carried_in(): gathered = jax.tree.map(lambda a: lax.all_gather(a, axis), part)  175 us
    reduce_scatter x1, waiting for transfers between devices, on_device(): lax.psum_scatter(jnp.einsum('btk,kd->btd', normed, out_weight, preferred_...  83 us
    all_gather x1, waiting for transfers between devices, on_device(): block_rows = lax.all_gather(tokens, 'fsdp', axis=0, tiled=True)  28.9 us
    all_gather x1, blocking collectives, carried_in(): gathered = jax.tree.map(lambda a: lax.all_gather(a, axis), part)  27.9 us
    dot_general x4, matrix products, on_device(): jnp.dot(flat_rows, matrix, preferred_element_type=jnp.float32)  20.9 us
    dot_general x1, matrix products, on_device(): jnp.einsum('btk,kd->btd', normed, out_weight, preferred_element_type=jnp....  12.4 us
    dot_general x1, matrix products, on_device(): jnp.einsum('bthn,bhpn->bthp', query_heads, entry_state, precision=highest)  11.9 us
    ppermute x3, starting transfers between devices, shifted(): return lax.ppermute(block, axis, route)  11.8 us
  transfers between devices with their start and end apart: 6, of which 3 were waited for; matrix products, arithmetic and copies ran while one was open for 8% of the time, Pallas kernels for 0%

commit v1 on v0

v1 whole, which is shorter than its diff:
```python
import jax
import jax.numpy as jnp
from jax import lax
from jax.experimental import pallas as pl
from jax.experimental.pallas import tpu as pltpu
from jax.sharding import PartitionSpec as P

P_SIZE = 64
N = 128
CH = 128
TAIL = 8
STATE_ROWS = N + 16
OUT_STEPS = 4

epsilon = 1e-05
highest = lax.Precision.HIGHEST
f32 = jnp.float32
bf16 = jnp.bfloat16
VMEM_LIMIT = 52 * 1024 * 1024


def dot(a, b):
    return jnp.dot(a, b, preferred_element_type=f32)


def turned(rows):
    fill = jnp.zeros((N - rows.shape[0], rows.shape[1]), f32)
    return jnp.concatenate([rows, fill], axis=0).T


def per_head(columns, first, heads):
    lane = lax.broadcasted_iota(jnp.int32, (columns.shape[0], 2 * P_SIZE), 1)
    low = lane < P_SIZE
    blocks = [
        jnp.where(low, columns[:, c : c + 1], columns[:, c + 1 : c + 2])
        for c in range(first, first + heads, 2)
    ]
    return jnp.concatenate(blocks, axis=1)


def spread_heads(columns, heads_per_step, steps):
    return jnp.concatenate(
        [per_head(columns, 8 * j, heads_per_step) for j in range(steps)], axis=1
    )


def mix_kernel(
    first_ref,
    second_ref,
    tails_ref,
    rows_ref,
    value_ref,
    coupling_ref,
    step_ref,
    value_conv_ref,
    coupling_conv_ref,
    value_shift_ref,
    coupling_shift_ref,
    head_ref,
    values_ref,
    coupled_ref,
    sums_ref,
    state_ref,
    rows_scr,
    step_scr,
    mask_scr,
    pad_scr,
):
    j = pl.program_id(0)
    steps = pl.num_programs(0)
    wide, narrow = value_ref.shape[1], coupling_ref.shape[1]
    heads = step_ref.shape[0]
    reach = value_conv_ref.shape[0] - 1

    @pl.when(j == 0)
    def _():
        rows_scr[0:CH] = first_ref[...]
        rows_scr[CH : 2 * CH] = second_ref[...]
        rows_scr[2 * CH : 2 * CH + 2 * TAIL] = tails_ref[...]
        step_scr[...] = lax.dot_general(
            step_ref[...],
            rows_scr[0 : 2 * CH],
            (((1,), (1,)), ((), ())),
            preferred_element_type=f32,
        )
        for s in range(2):
            mask_scr[s] = turned(rows_ref[s])

    def convolved(projected, taps_ref, shift_ref, out_ref, offset, width):
        projected = projected.astype(bf16).astype(f32)
        for s in range(2):
            pad_scr[0:TAIL, 0:width] = projected[2 * CH + TAIL * s : 2 * CH + TAIL * (s + 1)]
            pad_scr[TAIL : TAIL + CH, 0:width] = projected[CH * s : CH * (s + 1)]
            running = shift_ref[...] + taps_ref[reach : reach + 1].astype(f32) * projected[
                CH * s : CH * (s + 1)
            ]
            for k in range(reach):
                window = pad_scr[TAIL - reach + k : TAIL - reach + k + CH, 0:width]
                running = running + taps_ref[k : k + 1].astype(f32) * window * mask_scr[
                    s, :, k : k + 1
                ]
            out_ref[s, :, pl.ds(pl.multiple_of(offset, width), width)] = jax.nn.silu(
                running
            ).astype(bf16)

    rows = rows_scr[...]
    convolved(
        dot(rows, value_ref[...]), value_conv_ref, value_shift_ref, values_ref, j * wide, wide
    )
    convolved(
        dot(rows, coupling_ref[...]),
        coupling_conv_ref,
        coupling_shift_ref,
        coupled_ref,
        j * narrow,
        narrow,
    )

    @pl.when(j == steps - 1)
    def _():
        count = sums_ref.shape[1]
        per_step = heads // count
        groups = coupled_ref.shape[2] // (2 * N)
        share = values_ref.shape[2] // groups
        source = lax.broadcasted_iota(jnp.int32, (CH, CH), 0)
        position = lax.broadcasted_iota(jnp.int32, (CH, CH), 1)
        upto = (source <= position).astype(f32)
        for s in range(2):
            step_rows = step_scr[:, s * CH : (s + 1) * CH].astype(bf16).astype(f32)
            sizes = jax.nn.softplus(step_rows + head_ref[0])
            decays = -sizes * jnp.exp(head_ref[1])
            cumulative = jnp.dot(decays, upto, precision=highest, preferred_element_type=f32)
            last = cumulative[:, CH - 1 : CH]
            kept, ending = rows_ref[s, 4:5], rows_ref[s, 5:6]
            tail_weight = ending * jnp.exp(last - cumulative) * sizes
            growth = kept * jnp.exp(cumulative)
            gap = jnp.zeros((8 - per_step, CH), f32)
            spaced_tail, spaced_growth = [], []
            for jj in range(count):
                own = slice(jj * per_step, (jj + 1) * per_step)
                sums_ref[s, jj, 0:per_step] = cumulative[own]
                sums_ref[s, jj, per_step : 2 * per_step] = sizes[own]
                if 2 * per_step < 8:
                    sums_ref[s, jj, 2 * per_step : 8] = jnp.zeros((8 - 2 * per_step, CH), f32)
                spaced_tail += [tail_weight[own], gap]
                spaced_growth += [growth[own], gap]
            weights = spread_heads(
                turned(jnp.concatenate(spaced_tail, axis=0)), per_step, count
            )
            leading = spread_heads(
                turned(jnp.concatenate(spaced_growth, axis=0))[CH - 8 : CH], per_step, count
            )[7:8]
            weighted = (weights * values_ref[s].astype(f32)).astype(bf16)
            for g in range(groups):
                keys = coupled_ref[s, :, g * 2 * N : g * 2 * N + N]
                state_ref[s, 0:N, g * share : (g + 1) * share] = lax.dot_general(
                    keys,
                    weighted[:, g * share : (g + 1) * share],
                    (((0,), (0,)), ((), ())),
                    preferred_element_type=f32,
                ).astype(bf16)
            coarse = leading.astype(bf16).astype(f32)
            line = lax.broadcasted_iota(jnp.int32, (16, leading.shape[1]), 0)
            state_ref[s, N:STATE_ROWS] = jnp.where(
                line == 0, coarse, jnp.where(line == 1, leading - coarse, 0.0)
            ).astype(bf16)


def scan_kernel(
    first_ref,
    second_ref,
    rows_ref,
    gate_ref,
    values_ref,
    coupled_ref,
    sums_ref,
    skip_ref,
    gates_ref,
    local_ref,
    rows_scr,
    score_scr,
    hidden_scr,
):
    j = pl.program_id(0)
    groups = coupled_ref.shape[2] // (2 * N)
    per_step = values_ref.shape[2] // P_SIZE

    @pl.when(j == 0)
    def _():
        rows_scr[0:CH] = first_ref[...]
        rows_scr[CH : 2 * CH] = second_ref[...]
        position = lax.broadcasted_iota(jnp.int32, (CH, CH), 0)
        source = lax.broadcasted_iota(jnp.int32, (CH, CH), 1)
        for s in range(2):
            ids = turned(rows_ref[s])[:, 3:4]
            visible = jnp.logical_and(ids == rows_ref[s, 3:4], position >= source)
            hidden_scr[s] = jnp.where(visible, 0.0, -1e30)
            for g in range(groups):
                keys = coupled_ref[s, :, g * 2 * N : g * 2 * N + N]
                queries = coupled_ref[s, :, g * 2 * N + N : (g + 1) * 2 * N]
                score_scr[s, g] = lax.dot_general(
                    queries, keys, (((1,), (1,)), ((), ())), preferred_element_type=f32
                )

    projected = dot(rows_scr[...], gate_ref[...]).astype(bf16)
    lane = lax.broadcasted_iota(jnp.int32, (CH, 2 * P_SIZE), 1)
    group = j // 2
    for s in range(2):
        gates_ref[s] = projected[s * CH : (s + 1) * CH]
        columns = turned(sums_ref[s, 0])
        scores = score_scr[s, group]
        hidden = hidden_scr[s]
        for pair in range(per_step // 2):
            mixing = []
            for h in (2 * pair, 2 * pair + 1):
                damping = jnp.exp(columns[:, h : h + 1] - sums_ref[s, 0, h : h + 1] + hidden)
                sizes = sums_ref[s, 0, per_step + h : per_step + h + 1]
                mixing.append((scores * damping * sizes).astype(bf16))
            own = slice(pair * 2 * P_SIZE, (pair + 1) * 2 * P_SIZE)
            both = values_ref[s, :, own]
            mixed = dot(jnp.concatenate(mixing, axis=0), both)
            local_ref[s, :, own] = (
                jnp.where(lane < P_SIZE, mixed[0:CH], mixed[CH : 2 * CH])
                + skip_ref[:, own] * both.astype(f32)
            )


def out_kernel(
    local_ref,
    gates_ref,
    coupled_ref,
    sums_ref,
    rows_ref,
    entry_first_ref,
    entry_second_ref,
    gain_ref,
    out_ref,
    first_ref,
    second_ref,
    normed_scr,
):
    groups = coupled_ref.shape[2] // (2 * N)
    share = local_ref.shape[2] // groups
    count = sums_ref.shape[1]
    per_step = local_ref.shape[2] // P_SIZE // count

    @pl.when(pl.program_id(0) == 0)
    def _():
        for s, entry_ref in enumerate((entry_first_ref, entry_second_ref)):
            sums = jnp.concatenate([sums_ref[s, jj] for jj in range(count)], axis=0)
            line = lax.broadcasted_iota(jnp.int32, sums.shape, 0) % 8
            growth = rows_ref[s, 4:5] * jnp.exp(jnp.where(line < per_step, sums, 0.0))
            spread = spread_heads(turned(growth), per_step, count)
            for g in range(groups):
                own = slice(g * share, (g + 1) * share)
                queries = coupled_ref[s, :, g * 2 * N + N : (g + 1) * 2 * N]
                carried = dot(queries, entry_ref[:, own])
                scanned = local_ref[s, :, own] + spread[:, own] * carried
                gated = scanned * jax.nn.silu(gates_ref[s, :, own].astype(f32))
                scale = lax.rsqrt(jnp.mean(gated * gated, axis=-1, keepdims=True) + epsilon)
                normed_scr[s * CH : (s + 1) * CH, own] = (
                    gated * scale * gain_ref[:, own]
                ).astype(bf16)

    branch = dot(normed_scr[...], out_ref[...]).astype(bf16)
    first_ref[...] = branch[0:CH]
    second_ref[...] = branch[CH : 2 * CH]


def whole(a):
    return pl.BlockSpec(a.shape, lambda j: (0,) * a.ndim)


def columns_of(a, steps):
    lead = a.shape[:-1]
    return pl.BlockSpec((*lead, a.shape[-1] // steps), lambda j: (0,) * len(lead) + (j,))


def params():
    return pltpu.CompilerParams(
        dimension_semantics=("arbitrary",), vmem_limit_bytes=VMEM_LIMIT
    )


def cost(rows, *weights):
    flops = sum(2 * rows * w.shape[0] * w.shape[1] for w in weights)
    return pl.CostEstimate(
        flops=flops, bytes_accessed=sum(2 * w.size for w in weights), transcendentals=0
    )


def mix(first, second, tails, rows, weights, convs, head):
    value_weight, coupling_weight, step_rows = weights
    value_conv, coupling_conv, value_shift, coupling_shift = convs
    width, narrow, depth = value_weight.shape[1], coupling_weight.shape[1], first.shape[1]
    steps = narrow // N
    shapes = [
        jax.ShapeDtypeStruct((2, CH, width), bf16),
        jax.ShapeDtypeStruct((2, CH, narrow), bf16),
        jax.ShapeDtypeStruct((2, steps, 8, CH), f32),
        jax.ShapeDtypeStruct((2, STATE_ROWS, width), bf16),
    ]
    return pl.pallas_call(
        mix_kernel,
        grid=(steps,),
        in_specs=[
            whole(first),
            whole(second),
            whole(tails),
            whole(rows),
            columns_of(value_weight, steps),
            columns_of(coupling_weight, steps),
            whole(step_rows),
            columns_of(value_conv, steps),
            columns_of(coupling_conv, steps),
            columns_of(value_shift, steps),
            columns_of(coupling_shift, steps),
            whole(head),
        ],
        out_specs=[whole(s) for s in shapes],
        out_shape=shapes,
        scratch_shapes=[
            pltpu.VMEM((2 * CH + 2 * TAIL, depth), bf16),
            pltpu.VMEM((step_rows.shape[0], 2 * CH), f32),
            pltpu.VMEM((2, CH, CH), f32),
            pltpu.VMEM((CH + TAIL, width // steps), f32),
        ],
        compiler_params=params(),
        cost_estimate=cost(2 * CH, value_weight, coupling_weight),
        name="mix",
    )(
        first,
        second,
        tails,
        rows,
        value_weight,
        coupling_weight,
        step_rows,
        value_conv,
        coupling_conv,
        value_shift,
        coupling_shift,
        head,
    )


def scan(first, second, rows, gate_weight, values, coupled, sums, skip):
    shapes = [
        jax.ShapeDtypeStruct(values.shape, bf16),
        jax.ShapeDtypeStruct(values.shape, f32),
    ]
    steps = coupled.shape[2] // N
    return pl.pallas_call(
        scan_kernel,
        grid=(steps,),
        in_specs=[
            whole(first),
            whole(second),
            whole(rows),
            columns_of(gate_weight, steps),
            columns_of(values, steps),
            whole(coupled),
            pl.BlockSpec((2, 1, 8, CH), lambda j: (0, j, 0, 0)),
            columns_of(skip, steps),
        ],
        out_specs=[columns_of(s, steps) for s in shapes],
        out_shape=shapes,
        scratch_shapes=[
            pltpu.VMEM((2 * CH, first.shape[1]), bf16),
            pltpu.VMEM((2, steps // 2, CH, CH), f32),
            pltpu.VMEM((2, CH, CH), f32),
        ],
        compiler_params=params(),
        cost_estimate=cost(2 * CH, gate_weight),
        name="scan",
    )(first, second, rows, gate_weight, values, coupled, sums, skip)


def project_out(local, gates, coupled, sums, rows, entry_first, entry_second, gain, out_weight):
    depth = out_weight.shape[1]
    shapes = [jax.ShapeDtypeStruct((CH, depth), bf16)] * 2
    return pl.pallas_call(
        out_kernel,
        grid=(OUT_STEPS,),
        in_specs=[
            whole(local),
            whole(gates),
            whole(coupled),
            whole(sums),
            whole(rows),
            whole(entry_first),
            whole(entry_second),
            whole(gain),
            columns_of(out_weight, OUT_STEPS),
        ],
        out_specs=[columns_of(s, OUT_STEPS) for s in shapes],
        out_shape=shapes,
        scratch_shapes=[pltpu.VMEM((2 * CH, out_weight.shape[0]), bf16)],
        compiler_params=params(),
        cost_estimate=cost(2 * CH, out_weight),
        name="project_out",
    )(local, gates, coupled, sums, rows, entry_first, entry_second, gain, out_weight)


def along(block, axis, distance):
    devices = range(lax.axis_size(axis))
    return lax.ppermute(
        block, axis, [(i, i + distance) for i in devices if i + distance in devices]
    )


def partner(block, axis):
    return lax.ppermute(block, axis, [(i, i ^ 1) for i in range(lax.axis_size(axis))])


def rows_over(block, distance):
    size = lax.axis_size("fsdp")
    route = [(i, (i + 2 * distance) % size) for i in range(size)]
    return lax.ppermute(block, "fsdp", route)


def unpacked(block):
    block = block.astype(f32)
    return block[:N], block[N : N + 1] + block[N + 1 : N + 2]


def packed(state, factor):
    coarse = factor.astype(bf16).astype(f32)
    rest = jnp.zeros((STATE_ROWS - N - 2, state.shape[1]), f32)
    return jnp.concatenate([state, coarse, factor - coarse, rest], axis=0).astype(bf16)


def entry_states(ends):
    spans = lax.axis_size("ctx")
    odd = lax.axis_index("ctx") % 2 == 1
    given, kept = jnp.where(odd, ends[1], ends[0]), jnp.where(odd, ends[0], ends[1])
    got = partner(given, "ctx")
    even_state, even_factor = unpacked(jnp.where(odd, got, kept))
    odd_state, odd_factor = unpacked(jnp.where(odd, kept, got))
    state, factor = odd_state + odd_factor * even_state, odd_factor * even_factor
    distance = 1
    while distance < spans // 4:
        earlier_state, earlier_factor = unpacked(along(packed(state, factor), "ctx", 2 * distance))
        state, factor = state + factor * earlier_state, factor * earlier_factor
        distance *= 2
    before = along(state.astype(bf16), "ctx", 2)
    between = (even_state + even_factor * before.astype(f32)).astype(bf16)
    other = partner(jnp.where(odd, before, between), "ctx")
    own = jnp.where(odd, between, before)
    return jnp.where(odd, own, other), jnp.where(odd, other, own)


def on_device(
    tokens,
    segments,
    gate_weight,
    value_weight,
    coupling_weight,
    step_weight,
    value_conv,
    coupling_conv,
    value_shift,
    coupling_shift,
    step_bias,
    decay_log,
    skip_gain,
    norm_gain,
    out_weight,
    rezero,
):
    place = lax.axis_index("fsdp")
    streams = lax.axis_size("fsdp")
    chips = streams // 2
    chip, core = place // 2, place % 2
    reach = value_conv.shape[0] - 1
    own = tokens[0]

    tail = own[CH - TAIL :]
    tails = jnp.stack([tail] + [rows_over(tail, -d) for d in range(1, chips)])
    arrived = [own] + [rows_over(own, -d) for d in range(1, chips)]
    opposite = [partner(a, "fsdp") for a in arrived]
    tails = jnp.stack([tails, partner(tails, "fsdp")], axis=1)

    which = ((chip + jnp.arange(chips)) % chips * 2)[:, None] + (core ^ jnp.arange(2))[None, :]
    chosen = which[:, :, None] == jnp.arange(streams)[None, None, :]
    ids = jnp.sum(jnp.where(chosen[..., None], segments[None, None], 0), axis=2)
    last_ids = jnp.pad(
        ids[:, :, None, CH - TAIL :].astype(bf16),
        ((0, 0), (0, 0), (0, 0), (0, own.shape[1] - TAIL)),
    )
    tails = along(jnp.concatenate([last_ids, tails[:, :, 1:]], axis=2), "ctx", 1)
    prior_ids = tails[:, :, 0, TAIL - reach : TAIL].astype(jnp.int32)
    padded_ids = jnp.concatenate([prior_ids, ids], axis=2)
    rows = jnp.stack(
        [(padded_ids[:, :, k : k + CH] == ids).astype(f32) for k in range(reach)]
        + [
            ids.astype(f32),
            (ids == prior_ids[:, :, reach - 1 :]).astype(f32),
            (ids == ids[:, :, CH - 1 :]).astype(f32),
        ]
        + [jnp.zeros(ids.shape, f32)] * (8 - reach - 3),
        axis=2,
    )

    heads = step_weight.shape[1]
    head = jnp.broadcast_to(jnp.stack([step_bias, decay_log])[:, :, None], (2, heads, CH))
    skip = jnp.repeat(skip_gain, P_SIZE)[None]
    weights = (value_weight, coupling_weight, step_weight.T)
    convs = (value_conv, coupling_conv, value_shift[None], coupling_shift[None])

    partials = []
    for d in range(chips):
        pair = (arrived[d], opposite[d])
        values, coupled, sums, ends = mix(
            *pair, tails[d].reshape(2 * TAIL, -1), rows[d], weights, convs, head
        )
        entries = entry_states(ends)
        gates, local = scan(*pair, rows[d], gate_weight, values, coupled, sums, skip)
        partials.append(
            project_out(
                local, gates, coupled, sums, rows[d], *entries, norm_gain[None], out_weight
            )
        )
    branch = 0.0
    for d, (mine, others) in enumerate(partials):
        total = mine.astype(f32) + partner(others, "fsdp").astype(f32)
        if d:
            total = rows_over(total.astype(bf16), d).astype(f32)
        branch = branch + total
    return (own.astype(f32) + rezero[0] * branch).astype(bf16)[None]


def solution(mesh):
    return jax.shard_map(
        on_device,
        mesh=mesh,
        in_specs=(
            P("fsdp", "ctx", None),
            P(None, "ctx"),
            P(None, "fsdp"),
            P(None, "fsdp"),
            P(None, "fsdp"),
            P(None, "fsdp"),
            P(None, "fsdp"),
            P(None, "fsdp"),
            P("fsdp"),
            P("fsdp"),
            P("fsdp"),
            P("fsdp"),
            P("fsdp"),
            P("fsdp"),
            P("fsdp", None),
            P(),
        ),
        out_specs=P("fsdp", "ctx", None),
        check_vma=False,
    )
```

time: 453 us -> 169 us (0.37)
  waiting for transfers between devices: 288 us -> 70.4 us
  matrix products: 66.6 us -> 0 us
  Pallas kernels: 0 us -> 55.3 us
  blocking collectives: 27.9 us -> 0 us
  local copies, waits for them, and re-layouts: 25.4 us -> 4.59 us
  starting transfers between devices: 11.9 us -> 31.1 us
  between operations: 14.3 us -> 1.06 us
  other arithmetic: 18 us -> 5.81 us
    all_gather x2 -> x0, waiting for transfers between devices: 204 us -> none  [the longest x1 175 us: carried_in(): gathered = jax.tree.map(lambda a: lax.all_gather(a, axis), part)]
    reduce_scatter x1 -> x0, waiting for transfers between devices: 83 us -> none  [on_device(): lax.psum_scatter(jnp.einsum('btk,kd->btd', normed, out_weight, preferred_...]
    ppermute x3 -> x17, waiting for transfers between devices: 0.01 us -> 70.4 us  [the longest x3 43.5 us: rows_over(): return lax.ppermute(block, 'fsdp', route)]
    dot_general x10 -> x0, matrix products: 66.6 us -> none  [the longest x4 20.9 us: on_device(): jnp.dot(flat_rows, matrix, preferred_element_type=jnp.float32)]
    pallas_call x0 -> x6, Pallas kernels: none -> 55.3 us  [the longest x2 23.8 us: mix(): pl.pallas_call(mix_kernel, grid=(steps,), in_specs=[whole(first), whole(s...]
    all_gather x1 -> x0, blocking collectives: 27.9 us -> none  [carried_in(): gathered = jax.tree.map(lambda a: lax.all_gather(a, axis), part)]
    ppermute x3 -> x17, starting transfers between devices: 11.8 us -> 31.1 us  [the longest x5 18.1 us: along(): lax.ppermute(block, axis, [(i, i + distance) for i in devices if i + dist...]
    convert_element_type x7 -> x11, other arithmetic: 13 us -> 1.63 us  [the longest x2 0.94 us: entry_states(): before = along(state.astype(bf16), 'ctx', 2)]
  transfers between devices with their start and end apart: 6 -> 17, of which waited for: 3 -> 10; matrix products, arithmetic and copies ran while one was open for 8% -> 2% of each run, Pallas kernels for 0% -> 26%
where the time goes in v1:
time: 169 us; the launch traced here: 168 us
  waiting for transfers between devices  70.4 us (42%)
  Pallas kernels  55.3 us (33%)
  starting transfers between devices  31.1 us (18%)
  other arithmetic  5.81 us (3%)
  local copies, waits for them, and re-layouts  4.59 us (3%)
    ppermute x3, waiting for transfers between devices, rows_over(): return lax.ppermute(block, 'fsdp', route)  43.5 us
    pallas_call x2, Pallas kernels, mix(): pl.pallas_call(mix_kernel, grid=(steps,), in_specs=[whole(first), whole(s...  23.8 us
    ppermute x5, starting transfers between devices, along(): lax.ppermute(block, axis, [(i, i + distance) for i in devices if i + dist...  18.1 us
    ppermute x9, waiting for transfers between devices, partner(): lax.ppermute(block, axis, [(i, i ^ 1) for i in range(lax.axis_size(axis))])  17.7 us
    pallas_call x2, Pallas kernels, project_out(): pl.pallas_call(out_kernel, grid=(OUT_STEPS,), in_specs=[whole(local), who...  16 us
    pallas_call x2, Pallas kernels, scan(): pl.pallas_call(scan_kernel, grid=(steps,), in_specs=[whole(first), whole(...  15.6 us
    ppermute x5, waiting for transfers between devices, along(): lax.ppermute(block, axis, [(i, i + distance) for i in devices if i + dist...  9.17 us
    ppermute x9, starting transfers between devices, partner(): lax.ppermute(block, axis, [(i, i ^ 1) for i in range(lax.axis_size(axis))])  6.82 us
  transfers between devices with their start and end apart: 17, of which 10 were waited for; matrix products, arithmetic and copies ran while one was open for 2% of the time, Pallas kernels for 26%

profile of v1, /device:TPU:0, one launch (start us, length us, event | category | flops | bytes accessed | tf_op | source)
XLA Modules:
  0.0 168.3 jit_solution(6894697124276922957)
XLA Ops:
  0.0 0.9 fusion.20
  1.0 3.0 %collective-permute-start.1 = (bf16[8,4096]{1,0:T(8,128)(2,1)S(1)}, bf16[8,4096]{1,0:T(8,128)(2,1)S(1)}, u32[]{:S(2)}, u32[]{:S(2)}) collective-permute-start(bf16[8,4096]{1,0:T(8,128)(2,1)S(1)} %get-tuple-element.50), channel_id=1, source_target_pairs={{0,16},{8,24},{16,0},{24,8},{1,17},{9,25},{17,1},{25,9},{2,18},{10... | collective-permute-start | bytes 196616 | tf_op jit(solution)/shard_map/ppermute | solution.py:419
  5.0 1.3 collective-permute-done.1
  6.7 1.0 collective-permute-done.2
  8.5 3.9 %collective-permute-start.3 = (bf16[2,2,8,4096]{3,1,2,0:T(2,128)(2,1)S(1)}, bf16[2,2,8,4096]{3,1,2,0:T(2,128)(2,1)S(1)}, u32[]{:S(2)}, u32[]{:S(2)}) collective-permute-start(bf16[2,2,8,4096]{3,1,2,0:T(2,128)(2,1)S(1)} %fusion.8), channel_id=1, source_target_pairs={{0,1},{1,2},{2,3},{3,4},{4,5},{5,6},{6,7},{8,9},{9,10},{10,11},{11... | collective-permute-start | bytes 786440 | tf_op jit(solution)/shard_map/ppermute | solution.py:407
  12.5 1.6 collective-permute-start.9
  14.3 3.9 %collective-permute-done.3 = bf16[2,2,8,4096]{3,1,2,0:T(2,128)(2,1)S(1)} collective-permute-done((bf16[2,2,8,4096]{3,1,2,0:T(2,128)(2,1)S(1)}, bf16[2,2,8,4096]{3,1,2,0:T(2,128)(2,1)S(1)}, u32[]{:S(2)}, u32[]{:S(2)}) %collective-permute-start.3) | collective-permute-done | bytes 262176 | tf_op jit(solution)/shard_map/ppermute | solution.py:407
  19.1 19.1 %collective-permute-done.9.first_ref = bf16[128,4096]{1,0:T(8,128)(2,1)} collective-permute-done((bf16[128,4096]{1,0:T(8,128)(2,1)S(1)}, bf16[128,4096]{1,0:T(8,128)(2,1)}, u32[]{:S(2)}, u32[]{:S(2)}) %collective-permute-start.9) | collective-permute-done | bytes 1048608 | tf_op jit(solution)/shard_map/ppermute | solution.py:419
  38.3 0.9 copy-done.10
  39.2 11.9 %mix.2 = (bf16[2,128,1024]{2,1,0:T(8,128)(2,1)S(1)}, bf16[2,128,512]{2,1,0:T(8,128)(2,1)S(1)}, f32[2,4,8,128]{3,2,1,0:T(8,128)S(1)}, bf16[2,144,1024]{2,1,0:T(8,128)(2,1)S(1)}) custom-call(bf16[128,4096]{1,0:T(8,128)(2,1)} %bitcast.79, bf16[128,4096]{1,0:T(8,128)(2,1)} %copy-done.10, bf16[16,4096]{1,0:T(8,128)(2,1)S(1)} %bitcast.71, ...), custom_call_target="tpu_custom_call" | custom-call | flops 3221225472 | bytes 12582912 | tf_op jit(solution)/shard_map/mix/pallas_call | solution.py:303
  51.2 1.6 collective-permute-start.4
  52.9 7.7 %collective-permute-done.4 = bf16[144,1024]{1,0:T(8,128)(2,1)S(1)} collective-permute-done((bf16[144,1024]{1,0:T(8,128)(2,1)S(1)}, bf16[144,1024]{1,0:T(8,128)(2,1)S(1)}, u32[]{:S(2)}, u32[]{:S(2)}) %collective-permute-start.4) | collective-permute-done | bytes 294944 | tf_op jit(solution)/shard_map/ppermute | solution.py:413
  60.8 1.0 copy-done.11
  61.9 11.9 %mix.3 = (bf16[2,128,1024]{2,1,0:T(8,128)(2,1)S(1)}, bf16[2,128,512]{2,1,0:T(8,128)(2,1)S(1)}, f32[2,4,8,128]{3,2,1,0:T(8,128)S(1)}, bf16[2,144,1024]{2,1,0:T(8,128)(2,1)S(1)}) custom-call(bf16[128,4096]{1,0:T(8,128)(2,1)} %collective-permute-done.9.first_ref, bf16[128,4096]{1,0:T(8,128)(2,1)} %copy-done.11, bf16[16,4096]{1,0:T(8,128)(2,1)S(1)} %bitcast.72, ...), custom_call_target="tpu_custom_call" | custom-call | flops 3221225472 | bytes 12582912 | tf_op jit(solution)/shard_map/mix/pallas_call | solution.py:303
  73.8 1.6 collective-permute-start.11
  75.5 7.0 %collective-permute-done.11 = bf16[144,1024]{1,0:T(8,128)(2,1)S(1)} collective-permute-done((bf16[144,1024]{1,0:T(8,128)(2,1)S(1)}, bf16[144,1024]{1,0:T(8,128)(2,1)S(1)}, u32[]{:S(2)}, u32[]{:S(2)}) %collective-permute-start.11) | collective-permute-done | bytes 294944 | tf_op jit(solution)/shard_map/ppermute | solution.py:413
  82.9 3.5 %collective-permute-start.12 = (bf16[144,1024]{1,0:T(8,128)(2,1)S(1)}, bf16[144,1024]{1,0:T(8,128)(2,1)S(1)}, u32[]{:S(2)}, u32[]{:S(2)}) collective-permute-start(bf16[144,1024]{1,0:T(8,128)(2,1)S(1)} %get-tuple-element.67), channel_id=1, source_target_pairs={{0,2},{1,3},{2,4},{3,5},{4,6},{5,7},{8,10},{9,11},{10,12},{11,13},... | collective-permute-start | bytes 884744 | tf_op jit(solution)/shard_map/ppermute | solution.py:407
  86.4 5.2 %collective-permute-done.12 = bf16[144,1024]{1,0:T(8,128)(2,1)S(1)} collective-permute-done((bf16[144,1024]{1,0:T(8,128)(2,1)S(1)}, bf16[144,1024]{1,0:T(8,128)(2,1)S(1)}, u32[]{:S(2)}, u32[]{:S(2)}) %collective-permute-start.12) | collective-permute-done | bytes 294944 | tf_op jit(solution)/shard_map/ppermute | solution.py:407
  91.6 0.8 add_convert_fusion.3
  92.4 4.4 %collective-permute-start.13 = (bf16[128,1024]{1,0:T(8,128)(2,1)}, bf16[128,1024]{1,0:T(8,128)(2,1)S(1)}, u32[]{:S(2)}, u32[]{:S(2)}) collective-permute-start(bf16[128,1024]{1,0:T(8,128)(2,1)} %add_convert_fusion.3), channel_id=1, source_target_pairs={{0,2},{1,3},{2,4},{3,5},{4,6},{5,7},{8,10},{9,11},{10,12},{11,13},... | collective-permute-start | bytes 786440 | tf_op jit(solution)/shard_map/ppermute | solution.py:407
  97.0 3.5 %collective-permute-start.5 = (bf16[144,1024]{1,0:T(8,128)(2,1)S(1)}, bf16[144,1024]{1,0:T(8,128)(2,1)S(1)}, u32[]{:S(2)}, u32[]{:S(2)}) collective-permute-start(bf16[144,1024]{1,0:T(8,128)(2,1)S(1)} %get-tuple-element.66), channel_id=1, source_target_pairs={{0,2},{1,3},{2,4},{3,5},{4,6},{5,7},{8,10},{9,11},{10,12},{11,13},... | collective-permute-start | bytes 884744 | tf_op jit(solution)/shard_map/ppermute | solution.py:407
  100.5 7.9 %scan.3 = (bf16[2,128,1024]{2,1,0:T(8,128)(2,1)S(1)}, f32[2,128,1024]{2,1,0:T(8,128)}) custom-call(bf16[128,4096]{1,0:T(8,128)(2,1)} %collective-permute-done.9.first_ref, bf16[128,4096]{1,0:T(8,128)(2,1)} %copy-done.11, f32[2,8,128]{2,1,0:T(8,128)S(1)} %get-tuple-element.60.rows_ref, bf16[4096,1024]{1,0:T(8,128)(2,1)} %gate_ref.3, ...), custom_call_target="tpu_custom_call" | custom-call | flops 2147483648 | bytes 8388608 | tf_op jit(solution)/shard_map/scan/pallas_call | solution.py:353
  108.4 1.6 collective-permute-start.14
  110.2 2.8 %collective-permute-start.6 = (bf16[128,1024]{1,0:T(8,128)(2,1)S(1)}, bf16[128,1024]{1,0:T(8,128)(2,1)S(1)}, u32[]{:S(2)}, u32[]{:S(2)}) collective-permute-start(bf16[128,1024]{1,0:T(8,128)(2,1)S(1)} %add_convert_fusion.5), channel_id=1, source_target_pairs={{0,2},{1,3},{2,4},{3,5},{4,6},{5,7},{8,10},{9,11},{10,12},{11,13},... | collective-permute-start | bytes 786440 | tf_op jit(solution)/shard_map/ppermute | solution.py:407
  113.0 1.8 %collective-permute-done.14 = bf16[128,1024]{1,0:T(8,128)(2,1)S(1)} collective-permute-done((bf16[128,1024]{1,0:T(8,128)(2,1)S(1)}, bf16[128,1024]{1,0:T(8,128)(2,1)S(1)}, u32[]{:S(2)}, u32[]{:S(2)}) %collective-permute-start.14) | collective-permute-done | bytes 262176 | tf_op jit(solution)/shard_map/ppermute | solution.py:413
  115.1 7.9 %project_out.3 = (bf16[128,4096]{1,0:T(8,128)(2,1)}, bf16[128,4096]{1,0:T(8,128)(2,1)}) custom-call(f32[2,128,1024]{2,1,0:T(8,128)} %get-tuple-element.32.local_ref, bf16[2,128,1024]{2,1,0:T(8,128)(2,1)S(1)} %get-tuple-element.33.gates_ref, bf16[2,128,512]{2,1,0:T(8,128)(2,1)S(1)} %get-tuple-element.30.coupled_ref, ...), custom_call_target="tpu_custom_call" | custom-call | flops 2147483648 | bytes 8388608 | tf_op jit(solution)/shard_map/project_out/pallas_call | solution.py:382
  123.1 1.6 collective-permute-start.7
  124.7 7.7 %scan.2 = (bf16[2,128,1024]{2,1,0:T(8,128)(2,1)S(1)}, f32[2,128,1024]{2,1,0:T(8,128)}) custom-call(bf16[128,4096]{1,0:T(8,128)(2,1)} %bitcast.80, bf16[128,4096]{1,0:T(8,128)(2,1)} %copy-done.10, f32[2,8,128]{2,1,0:T(8,128)S(1)} %get-tuple-element.59.rows_ref, bf16[4096,1024]{1,0:T(8,128)(2,1)} %gate_ref.3, ...), custom_call_target="tpu_custom_call" | custom-call | flops 2147483648 | bytes 8388608 | tf_op jit(solution)/shard_map/scan/pallas_call | solution.py:353
  132.7 8.1 %project_out.2 = (bf16[128,4096]{1,0:T(8,128)(2,1)}, bf16[128,4096]{1,0:T(8,128)(2,1)}) custom-call(f32[2,128,1024]{2,1,0:T(8,128)} %get-tuple-element.24.local_ref, bf16[2,128,1024]{2,1,0:T(8,128)(2,1)S(1)} %get-tuple-element.25.gates_ref, bf16[2,128,512]{2,1,0:T(8,128)(2,1)S(1)} %get-tuple-element.22.coupled_ref, ...), custom_call_target="tpu_custom_call" | custom-call | flops 2147483648 | bytes 8388608 | tf_op jit(solution)/shard_map/project_out/pallas_call | solution.py:382
  141.2 1.6 collective-permute-start.16
  143.6 23.0 %collective-permute-done.16 = bf16[128,4096]{1,0:T(8,128)(2,1)S(1)} collective-permute-done((bf16[128,4096]{1,0:T(8,128)(2,1)S(1)}, bf16[128,4096]{1,0:T(8,128)(2,1)S(1)}, u32[]{:S(2)}, u32[]{:S(2)}) %collective-permute-start.16) | collective-permute-done | bytes 1048608 | tf_op jit(solution)/shard_map/ppermute | solution.py:419
  166.7 1.7 fusion
  (91 shorter events, 5.6 us)
Async XLA Ops:
  0.0 12.4 %copy-start.6 = (bf16[1,128,4096]{2,1,0:T(8,128)(2,1)S(1)}, bf16[1,128,4096]{2,1,0:T(8,128)(2,1)}, u32[]{:S(2)}) copy-start(bf16[1,128,4096]{2,1,0:T(8,128)(2,1)} %param.16) | copy-start | bytes 3145732
  0.0 14.1 %copy-start.15 = (f32[16]{0:T(128)S(1)}, f32[16]{0:T(128)}, u32[]{:S(2)}) copy-start(f32[16]{0:T(128)} %param.27) | copy-start | bytes 196
  0.0 14.1 %copy-start.16 = (f32[16]{0:T(128)S(1)}, f32[16]{0:T(128)}, u32[]{:S(2)}) copy-start(f32[16]{0:T(128)} %param.26) | copy-start | bytes 196
  0.0 39.2 %copy-start.2 = (bf16[4,512]{1,0:T(4,128)(2,1)S(1)}, bf16[4,512]{1,0:T(4,128)(2,1)}, u32[]{:S(2)}) copy-start(bf16[4,512]{1,0:T(4,128)(2,1)} %coupling_conv_ref.3) | copy-start | bytes 12292
  0.0 39.2 %copy-start.1 = (bf16[4,1024]{1,0:T(4,128)(2,1)S(1)}, bf16[4,1024]{1,0:T(4,128)(2,1)}, u32[]{:S(2)}) copy-start(bf16[4,1024]{1,0:T(4,128)(2,1)} %value_conv_ref.3) | copy-start | bytes 24580
  0.0 39.2 %copy-start.5 = (f32[512]{0:T(512)S(1)}, f32[512]{0:T(512)}, u32[]{:S(2)}) copy-start(f32[512]{0:T(512)} %param.25) | copy-start | bytes 6148
  0.0 39.2 %copy-start.3 = (f32[1024]{0:T(1024)S(1)}, f32[1024]{0:T(1024)}, u32[]{:S(2)}) copy-start(f32[1024]{0:T(1024)} %param.24) | copy-start | bytes 12292
  0.0 39.2 %copy-start = (bf16[4096,16]{0,1:T(8,128)(2,1)S(1)}, bf16[4096,16]{0,1:T(8,128)(2,1)}, u32[]{:S(2)}) copy-start(bf16[4096,16]{0,1:T(8,128)(2,1)} %param.21) | copy-start | bytes 393220
  1.0 5.3 %collective-permute-start.1 = (bf16[8,4096]{1,0:T(8,128)(2,1)S(1)}, bf16[8,4096]{1,0:T(8,128)(2,1)S(1)}, u32[]{:S(2)}, u32[]{:S(2)}) collective-permute-start(bf16[8,4096]{1,0:T(8,128)(2,1)S(1)} %get-tuple-element.50), channel_id=1, source_target_pairs={{0,16},{8,24},{16,0},{24,8},{1,17},{9,25},{17,1},{25,9},{2,18},{10... | collective-permute-start | bytes 196616 | tf_op jit(solution)/shard_map/ppermute | solution.py:419
  6.3 1.4 collective-permute-start.2
  8.5 9.8 %collective-permute-start.3 = (bf16[2,2,8,4096]{3,1,2,0:T(2,128)(2,1)S(1)}, bf16[2,2,8,4096]{3,1,2,0:T(2,128)(2,1)S(1)}, u32[]{:S(2)}, u32[]{:S(2)}) collective-permute-start(bf16[2,2,8,4096]{3,1,2,0:T(2,128)(2,1)S(1)} %fusion.8), channel_id=1, source_target_pairs={{0,1},{1,2},{2,3},{3,4},{4,5},{5,6},{6,7},{8,9},{9,10},{10,11},{11... | collective-permute-start | bytes 786440 | tf_op jit(solution)/shard_map/ppermute | solution.py:407
  12.4 25.8 %collective-permute-start = (bf16[128,4096]{1,0:T(8,128)(2,1)S(1)}, bf16[128,4096]{1,0:T(8,128)(2,1)S(1)}, u32[]{:S(2)}, u32[]{:S(2)}) collective-permute-start(bf16[128,4096]{1,0:T(8,128)(2,1)S(1)} %bitcast.81), channel_id=1, source_target_pairs={{0,8},{8,0},{16,24},{24,16},{1,9},{9,1},{17,25},{25,17},{2,10},{10... | collective-permute-start | bytes 3145736 | tf_op jit(solution)/shard_map/ppermute | solution.py:413
  12.5 25.7 %collective-permute-start.9 = (bf16[128,4096]{1,0:T(8,128)(2,1)S(1)}, bf16[128,4096]{1,0:T(8,128)(2,1)}, u32[]{:S(2)}, u32[]{:S(2)}) collective-permute-start(bf16[128,4096]{1,0:T(8,128)(2,1)S(1)} %bitcast.82), channel_id=1, source_target_pairs={{0,16},{8,24},{16,0},{24,8},{1,17},{9,25},{17,1},{25,9},{2,18},{10... | collective-permute-start | bytes 3145736 | tf_op jit(solution)/shard_map/ppermute | solution.py:419
  38.2 22.6 %collective-permute-start.10 = (bf16[128,4096]{1,0:T(8,128)(2,1)}, bf16[128,4096]{1,0:T(8,128)(2,1)S(1)}, u32[]{:S(2)}, u32[]{:S(2)}) collective-permute-start(bf16[128,4096]{1,0:T(8,128)(2,1)} %collective-permute-done.9.first_ref), channel_id=1, source_target_pairs={{0,8},{8,0},{16,24},{24,16},{1,9},{9,1},{17,25},{25,17},{2,10},{10... | collective-permute-start | bytes 3145736 | tf_op jit(solution)/shard_map/ppermute | solution.py:413
  51.2 9.5 %collective-permute-start.4 = (bf16[144,1024]{1,0:T(8,128)(2,1)S(1)}, bf16[144,1024]{1,0:T(8,128)(2,1)S(1)}, u32[]{:S(2)}, u32[]{:S(2)}) collective-permute-start(bf16[144,1024]{1,0:T(8,128)(2,1)S(1)} %select_bitcast_fusion.1), channel_id=1, source_target_pairs={{0,1},{1,0},{2,3},{3,2},{4,5},{5,4},{6,7},{7,6},{8,9},{9,8},{10,11... | collective-permute-start | bytes 884744 | tf_op jit(solution)/shard_map/ppermute | solution.py:413
  60.8 14.6 %copy-start.8 = (f32[144,1024]{1,0:T(8,128)}, f32[144,1024]{1,0:T(8,128)S(1)}, u32[]{:S(2)}) copy-start(f32[144,1024]{1,0:T(8,128)S(1)} %get-tuple-element.51) | copy-start | bytes 1769476
  73.8 8.7 %collective-permute-start.11 = (bf16[144,1024]{1,0:T(8,128)(2,1)S(1)}, bf16[144,1024]{1,0:T(8,128)(2,1)S(1)}, u32[]{:S(2)}, u32[]{:S(2)}) collective-permute-start(bf16[144,1024]{1,0:T(8,128)(2,1)S(1)} %select_bitcast_fusion), channel_id=1, source_target_pairs={{0,1},{1,0},{2,3},{3,2},{4,5},{5,4},{6,7},{7,6},{8,9},{9,8},{10,11... | collective-permute-start | bytes 884744 | tf_op jit(solution)/shard_map/ppermute | solution.py:413
  82.6 14.3 %copy-start.14 = (f32[16]{0:T(128)S(1)}, f32[16]{0:T(128)}, u32[]{:S(2)}) copy-start(f32[16]{0:T(128)} %param.28) | copy-start | bytes 196
  82.9 8.7 %collective-permute-start.12 = (bf16[144,1024]{1,0:T(8,128)(2,1)S(1)}, bf16[144,1024]{1,0:T(8,128)(2,1)S(1)}, u32[]{:S(2)}, u32[]{:S(2)}) collective-permute-start(bf16[144,1024]{1,0:T(8,128)(2,1)S(1)} %get-tuple-element.67), channel_id=1, source_target_pairs={{0,2},{1,3},{2,4},{3,5},{4,6},{5,7},{8,10},{9,11},{10,12},{11,13},... | collective-permute-start | bytes 884744 | tf_op jit(solution)/shard_map/ppermute | solution.py:407
  92.4 15.9 %collective-permute-start.13 = (bf16[128,1024]{1,0:T(8,128)(2,1)}, bf16[128,1024]{1,0:T(8,128)(2,1)S(1)}, u32[]{:S(2)}, u32[]{:S(2)}) collective-permute-start(bf16[128,1024]{1,0:T(8,128)(2,1)} %add_convert_fusion.3), channel_id=1, source_target_pairs={{0,2},{1,3},{2,4},{3,5},{4,6},{5,7},{8,10},{9,11},{10,12},{11,13},... | collective-permute-start | bytes 786440 | tf_op jit(solution)/shard_map/ppermute | solution.py:407
  97.0 13.1 %collective-permute-start.5 = (bf16[144,1024]{1,0:T(8,128)(2,1)S(1)}, bf16[144,1024]{1,0:T(8,128)(2,1)S(1)}, u32[]{:S(2)}, u32[]{:S(2)}) collective-permute-start(bf16[144,1024]{1,0:T(8,128)(2,1)S(1)} %get-tuple-element.66), channel_id=1, source_target_pairs={{0,2},{1,3},{2,4},{3,5},{4,6},{5,7},{8,10},{9,11},{10,12},{11,13},... | collective-permute-start | bytes 884744 | tf_op jit(solution)/shard_map/ppermute | solution.py:407
  100.5 9.6 %copy-start.9 = (f32[144,1024]{1,0:T(8,128)S(1)}, f32[144,1024]{1,0:T(8,128)}, u32[]{:S(2)}) copy-start(f32[144,1024]{1,0:T(8,128)} %copy-done.8) | copy-start | bytes 1769476
  108.4 6.6 %copy-start.4 = (f32[1024]{0:T(1024)S(1)}, f32[1024]{0:T(1024)}, u32[]{:S(2)}) copy-start(f32[1024]{0:T(1024)} %param.29) | copy-start | bytes 12292
  108.4 6.4 %collective-permute-start.14 = (bf16[128,1024]{1,0:T(8,128)(2,1)S(1)}, bf16[128,1024]{1,0:T(8,128)(2,1)S(1)}, u32[]{:S(2)}, u32[]{:S(2)}) collective-permute-start(bf16[128,1024]{1,0:T(8,128)(2,1)S(1)} %broadcast_select_fusion.4), channel_id=1, source_target_pairs={{0,1},{1,0},{2,3},{3,2},{4,5},{5,4},{6,7},{7,6},{8,9},{9,8},{10,11... | collective-permute-start | bytes 786440 | tf_op jit(solution)/shard_map/ppermute | solution.py:413
  110.2 12.8 %collective-permute-start.6 = (bf16[128,1024]{1,0:T(8,128)(2,1)S(1)}, bf16[128,1024]{1,0:T(8,128)(2,1)S(1)}, u32[]{:S(2)}, u32[]{:S(2)}) collective-permute-start(bf16[128,1024]{1,0:T(8,128)(2,1)S(1)} %add_convert_fusion.5), channel_id=1, source_target_pairs={{0,2},{1,3},{2,4},{3,5},{4,6},{5,7},{8,10},{9,11},{10,12},{11,13},... | collective-permute-start | bytes 786440 | tf_op jit(solution)/shard_map/ppermute | solution.py:407
  123.0 18.0 %collective-permute-start.15 = (bf16[128,4096]{1,0:T(8,128)(2,1)}, bf16[128,4096]{1,0:T(8,128)(2,1)S(1)}, u32[]{:S(2)}, u32[]{:S(2)}) collective-permute-start(bf16[128,4096]{1,0:T(8,128)(2,1)} %get-tuple-element.36), channel_id=1, source_target_pairs={{0,8},{8,0},{16,24},{24,16},{1,9},{9,1},{17,25},{25,17},{2,10},{10... | collective-permute-start | bytes 3145736 | tf_op jit(solution)/shard_map/ppermute | solution.py:413
  123.1 9.4 %collective-permute-start.7 = (bf16[128,1024]{1,0:T(8,128)(2,1)S(1)}, bf16[128,1024]{1,0:T(8,128)(2,1)S(1)}, u32[]{:S(2)}, u32[]{:S(2)}) collective-permute-start(bf16[128,1024]{1,0:T(8,128)(2,1)S(1)} %broadcast_select_fusion.8), channel_id=1, source_target_pairs={{0,1},{1,0},{2,3},{3,2},{4,5},{5,4},{6,7},{7,6},{8,9},{9,8},{10,11... | collective-permute-start | bytes 786440 | tf_op jit(solution)/shard_map/ppermute | solution.py:413
  132.7 8.3 %copy-start.12 = (bf16[128,4096]{1,0:T(8,128)(2,1)S(1)}, bf16[128,4096]{1,0:T(8,128)(2,1)}, u32[]{:S(2)}) copy-start(bf16[128,4096]{1,0:T(8,128)(2,1)} %get-tuple-element.35) | copy-start | bytes 3145732
  140.7 25.9 %copy-start.7 = (bf16[1,128,4096]{2,1,0:T(8,128)(2,1)S(1)}, bf16[1,128,4096]{2,1,0:T(8,128)(2,1)}, u32[]{:S(2)}) copy-start(bf16[1,128,4096]{2,1,0:T(8,128)(2,1)} %param.16) | copy-start | bytes 3145732
  140.7 25.9 %copy-start.13 = (bf16[128,4096]{1,0:T(8,128)(2,1)S(1)}, bf16[128,4096]{1,0:T(8,128)(2,1)}, u32[]{:S(2)}) copy-start(bf16[128,4096]{1,0:T(8,128)(2,1)} %get-tuple-element.27) | copy-start | bytes 3145732
  140.7 2.9 %collective-permute-start.8 = (bf16[128,4096]{1,0:T(8,128)(2,1)}, bf16[128,4096]{1,0:T(8,128)(2,1)S(1)}, u32[]{:S(2)}, u32[]{:S(2)}) collective-permute-start(bf16[128,4096]{1,0:T(8,128)(2,1)} %get-tuple-element.28), channel_id=1, source_target_pairs={{0,8},{8,0},{16,24},{24,16},{1,9},{9,1},{17,25},{25,17},{2,10},{10... | collective-permute-start | bytes 3145736 | tf_op jit(solution)/shard_map/ppermute | solution.py:413
  141.2 25.4 %collective-permute-start.16 = (bf16[128,4096]{1,0:T(8,128)(2,1)S(1)}, bf16[128,4096]{1,0:T(8,128)(2,1)S(1)}, u32[]{:S(2)}, u32[]{:S(2)}) collective-permute-start(bf16[128,4096]{1,0:T(8,128)(2,1)S(1)} %add_convert_fusion.1), channel_id=1, source_target_pairs={{0,16},{8,24},{16,0},{24,8},{1,17},{9,25},{17,1},{25,9},{2,18},{10... | collective-permute-start | bytes 3145736 | tf_op jit(solution)/shard_map/ppermute | solution.py:419
  (2 other events, 2.1 us)

commit v2 on v0

v2 whole, which is shorter than its diff:
```python
import functools

import jax
import jax.numpy as jnp
from jax import lax
from jax.experimental import pallas as pl
from jax.experimental.pallas import tpu as pltpu
from jax.sharding import PartitionSpec as P

P_SIZE = 64
N = 128
CH = 128
HALF = CH // 2
TAIL = 8
TAILS = 16
WIDE = 256
PIECES = 4
STATE_ROWS = N + 16

epsilon = 1e-05
highest = lax.Precision.HIGHEST
f32 = jnp.float32
bf16 = jnp.bfloat16


def dot(a, b):
    return jnp.dot(a, b, preferred_element_type=f32)


def turned(rows):
    fill = jnp.zeros((N - rows.shape[0], rows.shape[1]), f32)
    return jnp.concatenate([rows, fill], axis=0).T


def per_head(columns, first, heads):
    lane = lax.broadcasted_iota(jnp.int32, (columns.shape[0], 2 * P_SIZE), 1)
    low = lane < P_SIZE
    blocks = [
        jnp.where(low, columns[:, c : c + 1], columns[:, c + 1 : c + 2])
        for c in range(first, first + heads, 2)
    ]
    return jnp.concatenate(blocks, axis=1)


def spread_heads(columns, heads_per_step, steps):
    return jnp.concatenate(
        [per_head(columns, 8 * j, heads_per_step) for j in range(steps)], axis=1
    )


def fill_rows(rows_scr, sources, core, flip):
    if flip is None:
        rows_scr[0:CH] = sources[0][...]
        rows_scr[CH : 2 * CH] = sources[1][...]
        return
    for ref, taken in zip(sources, (core == flip, core != flip)):

        @pl.when(taken)
        def _(ref=ref):
            rows_scr[0:CH] = ref[...]


def ids_row(flags_ref, segments_ref, at):
    ids = segments_ref[...].astype(f32)
    line = lax.broadcasted_iota(jnp.int32, ids.shape, 0)
    return jnp.sum(jnp.where(line == flags_ref[at], ids, 0.0), axis=0, keepdims=True)


def tail_kernel(flags_ref, own_ref, segments_ref, after_ref, tail_ref):
    del after_ref
    tail_ref[...] = own_ref[CH - TAILS : CH]
    line = lax.broadcasted_iota(jnp.int32, (TAILS, CH), 0)
    tail_ref[:, 0:CH] = jnp.where(
        line == 0,
        ids_row(flags_ref, segments_ref, 3),
        own_ref[CH - TAILS : CH, 0:CH].astype(f32),
    ).astype(bf16)


def facts(rows_ref, s, ids, prior, reach):
    lane = lax.broadcasted_iota(jnp.int32, (8, CH), 1)
    line = lax.broadcasted_iota(jnp.int32, (8, CH), 0)
    ids, prior = (jnp.broadcast_to(a, (8, CH)) for a in (ids, prior))
    found = jnp.zeros((8, CH), f32)
    for k in range(reach):
        back = reach - k
        earlier = jnp.where(lane < back, pltpu.roll(prior, back, 1), pltpu.roll(ids, back, 1))
        found = jnp.where(line == k, jnp.where(earlier == ids, 1.0, 0.0), found)
    found = jnp.where(line == 3, ids, found)
    found = jnp.where(line == 4, jnp.where(ids == prior[:, CH - 1 : CH], 1.0, 0.0), found)
    found = jnp.where(line == 5, jnp.where(ids == ids[:, CH - 1 : CH], 1.0, 0.0), found)
    rows_ref[s] = found


def mix_kernel(slots, streams, flip, flags_ref, *refs):
    sources, refs = refs[:2], refs[2:]
    tail_refs, refs = refs[:2], refs[-(12 + slots) :]
    segments_ref, value_ref, coupling_ref, step_ref, taps_ref, head_ref = refs[:6]
    refs = refs[6:]
    values_ref, coupled_ref, sums_ref, rows_ref = refs[:4]
    state_refs, (rows_scr, pad_scr) = refs[4 : 4 + slots], refs[4 + slots :]
    odd = flags_ref[0] == 1
    heads = step_ref.shape[0]
    reach = 3
    count = sums_ref.shape[1]
    per_step = heads // count
    width = values_ref.shape[2]
    groups = coupled_ref.shape[2] // (2 * N)
    share = width // groups
    held = slots * CH

    work = []
    for g in range(groups):
        work.append((coupling_ref, coupled_ref, width, g))
        for piece in range(share // WIDE):
            work.append((value_ref, values_ref, 0, g * (share // WIDE) + piece))
    fill_rows(rows_scr, sources, flags_ref[1], flip)
    later = flags_ref[2] > 0
    tails = [ref[...].astype(f32) for ref in tail_refs]
    if slots == 1:
        tails = [jnp.where(flags_ref[1] == flip, tails[0], tails[1])]
    for s, tail in enumerate(tails):
        tail = jnp.where(later, tail, 0.0)
        rows_scr[held + TAILS * s : held + TAILS * (s + 1)] = tail.astype(bf16)
        facts(rows_ref, s, ids_row(flags_ref, segments_ref, streams[s]), tail[0:1, 0:CH], reach)
    masks = [turned(rows_ref[s]) for s in range(slots)]
    rows = rows_scr[...]
    step_rows = lax.dot_general(
        step_ref[...], rows_scr[0:held], (((1,), (1,)), ((), ())), preferred_element_type=f32
    )

    def convolved(projected, out_ref, base, at, slot):
        projected = projected.astype(bf16).astype(f32)
        taps = taps_ref[:, base + at * WIDE : base + (at + 1) * WIDE]
        for s in range(slots):
            body = projected[CH * s : CH * (s + 1)]
            start = held + TAILS * (s + 1) - TAIL
            pad_scr[slot, s, 0:TAIL] = projected[start : start + TAIL]
            pad_scr[slot, s, TAIL : TAIL + CH] = body
            running = taps[reach + 1 : reach + 2] + taps[reach : reach + 1] * body
            for k in range(reach):
                window = pad_scr[slot, s, TAIL - reach + k : TAIL - reach + k + CH]
                running = running + taps[k : k + 1] * window * masks[s][:, k : k + 1]
            out_ref[s, :, at * WIDE : (at + 1) * WIDE] = jax.nn.silu(running).astype(bf16)

    source = lax.broadcasted_iota(jnp.int32, (CH, CH), 0)
    position = lax.broadcasted_iota(jnp.int32, (CH, CH), 1)
    upto = (source <= position).astype(f32)

    def put_states(parts, lines, columns):
        if slots == 2:
            parts = [jnp.where(odd, parts[1], parts[0]), jnp.where(odd, parts[0], parts[1])]
        for ref, part in zip(state_refs, parts):
            ref[lines, columns] = part.astype(bf16)

    def weighed(s):
        sizes = jax.nn.softplus(
            step_rows[:, s * CH : (s + 1) * CH].astype(bf16).astype(f32) + head_ref[0]
        )
        decays = -sizes * jnp.exp(head_ref[1])
        cumulative = jnp.dot(decays, upto, precision=highest, preferred_element_type=f32)
        last = cumulative[:, CH - 1 : CH]
        kept, ending = rows_ref[s, 4:5], rows_ref[s, 5:6]
        tail_weight = ending * jnp.exp(last - cumulative) * sizes
        growth = kept * jnp.exp(cumulative)
        gap = jnp.zeros((8 - per_step, CH), f32)
        spaced_tail, spaced_growth = [], []
        for jj in range(count):
            own = slice(jj * per_step, (jj + 1) * per_step)
            sums_ref[s, jj, 0:per_step] = cumulative[own]
            sums_ref[s, jj, per_step : 2 * per_step] = sizes[own]
            spaced_tail += [tail_weight[own], gap]
            spaced_growth += [growth[own], gap]
        leading = spread_heads(
            turned(jnp.concatenate(spaced_growth, axis=0))[CH - 8 : CH], per_step, count
        )[7:8]
        coarse = leading.astype(bf16).astype(f32)
        line = lax.broadcasted_iota(jnp.int32, (STATE_ROWS - N, width), 0)
        factor = jnp.where(line == 0, coarse, jnp.where(line == 1, leading - coarse, 0.0))
        return turned(jnp.concatenate(spaced_tail, axis=0)), factor

    def ended(g):
        own = slice(g * share, (g + 1) * share)
        parts = []
        for s in range(slots):
            part = spread_heads(
                weights[s][0][:, g * 8 * count // groups : (g + 1) * 8 * count // groups],
                per_step,
                count // groups,
            )
            weighted = (part * values_ref[s, :, own].astype(f32)).astype(bf16)
            keys = coupled_ref[s, :, g * 2 * N : g * 2 * N + N]
            parts.append(
                lax.dot_general(
                    keys, weighted, (((0,), (0,)), ((), ())), preferred_element_type=f32
                )
            )
        put_states(parts, slice(0, N), own)

    weights = [weighed(s) for s in range(slots)]
    put_states([w[1] for w in weights], slice(N, STATE_ROWS), slice(0, width))
    per_group = len(work) // groups
    waiting = None
    for i in range(len(work) + 1):
        following = None
        if i < len(work):
            weight_ref, out_ref, base, at = work[i]
            following = (
                dot(rows, weight_ref[:, at * WIDE : (at + 1) * WIDE]),
                out_ref,
                base,
                at,
                i % 2,
            )
        if waiting is not None:
            convolved(*waiting)
            if i % per_group == 0:
                ended(i // per_group - 1)
        waiting = following


def scan_kernel(slots, flip, flags_ref, *refs):
    sources, refs = refs[:2], refs[2:]
    (
        rows_ref,
        gate_ref,
        values_ref,
        coupled_ref,
        sums_ref,
        skip_ref,
        gates_ref,
        local_ref,
        rows_scr,
    ) = refs
    count = sums_ref.shape[1]
    groups = coupled_ref.shape[2] // (2 * N)
    per_step = WIDE // P_SIZE
    fill_rows(rows_scr, sources, flags_ref[1], flip)
    rows = rows_scr[...]
    position = lax.broadcasted_iota(jnp.int32, (CH, CH), 0)
    source = lax.broadcasted_iota(jnp.int32, (CH, CH), 1)
    lane = lax.broadcasted_iota(jnp.int32, (CH, 2 * P_SIZE), 1)
    hidden = []
    for s in range(slots):
        ids = turned(rows_ref[s])[:, 3:4]
        visible = jnp.logical_and(ids == rows_ref[s, 3:4], position >= source)
        hidden.append(jnp.where(visible, 0.0, -1e30))
    scores = None
    for j in range(count):
        if j % (count // groups) == 0:
            g = j // (count // groups)
            scores = [
                lax.dot_general(
                    coupled_ref[s, :, g * 2 * N + N : (g + 1) * 2 * N],
                    coupled_ref[s, :, g * 2 * N : g * 2 * N + N],
                    (((1,), (1,)), ((), ())),
                    preferred_element_type=f32,
                )
                for s in range(slots)
            ]
        for s in range(slots):
            columns = turned(sums_ref[s, j])
            for pair in range(per_step // 2):
                mixing = []
                for h in (2 * pair, 2 * pair + 1):
                    damping = jnp.exp(
                        columns[:, h : h + 1] - sums_ref[s, j, h : h + 1] + hidden[s]
                    )
                    sizes = sums_ref[s, j, per_step + h : per_step + h + 1]
                    mixing.append((scores[s] * damping * sizes).astype(bf16))
                own = slice(j * WIDE + pair * 2 * P_SIZE, j * WIDE + (pair + 1) * 2 * P_SIZE)
                both = values_ref[s, :, own]
                mixed = dot(jnp.concatenate(mixing, axis=0), both)
                local_ref[s, :, own] = (
                    jnp.where(lane < P_SIZE, mixed[0:CH], mixed[CH : 2 * CH])
                    + per_head(skip_ref[...], j * per_step + 2 * pair, 2) * both.astype(f32)
                )
        own = slice(j * WIDE, (j + 1) * WIDE)
        projected = dot(rows, gate_ref[:, own]).astype(bf16)
        for s in range(slots):
            gates_ref[s, :, own] = projected[s * CH : (s + 1) * CH]


def unpacked(state, tail):
    tail = tail.astype(f32)
    return state.astype(f32), tail[0:1] + tail[1:2]


def paired(odd, mine_ref, got_ref):
    lines = (slice(0, N), slice(N, STATE_ROWS))
    mine, got = [[ref[line] for line in lines] for ref in (mine_ref, got_ref)]
    even = [jnp.where(odd, g.astype(f32), m.astype(f32)) for m, g in zip(mine, got)]
    later = [jnp.where(odd, m.astype(f32), g.astype(f32)) for m, g in zip(mine, got)]
    return unpacked(*even), unpacked(*later)


def put_packed(out_ref, state, factor):
    out_ref[0:N] = state.astype(bf16)
    if out_ref.shape[0] > N:
        coarse = factor.astype(bf16).astype(f32)
        line = lax.broadcasted_iota(jnp.int32, (STATE_ROWS - N, state.shape[1]), 0)
        out_ref[N:STATE_ROWS] = jnp.where(
            line == 0, coarse, jnp.where(line == 1, factor - coarse, 0.0)
        ).astype(bf16)


def join_kernel(flags_ref, mine_ref, got_ref, out_ref):
    even, later = paired(flags_ref[0] == 1, mine_ref, got_ref)
    put_packed(out_ref, later[0] + later[1] * even[0], later[1] * even[1])


def chain_kernel(distance, flags_ref, mine_ref, got_ref, out_ref):
    state, factor = unpacked(mine_ref[0:N], mine_ref[N:STATE_ROWS])
    earlier, leading = unpacked(got_ref[0:N], got_ref[N:STATE_ROWS])
    reached = jnp.where(flags_ref[2] >= distance, factor, 0.0)
    put_packed(out_ref, state + reached * earlier, reached * leading)


def entered(flags_ref, mine_ref, got_ref, before_ref):
    even, _ = paired(flags_ref[0] == 1, mine_ref, got_ref)
    before = jnp.where(flags_ref[2] >= 2, before_ref[...].astype(f32), 0.0)
    return before, even[0] + even[1] * before


def finish_kernel(flags_ref, mine_ref, got_ref, before_ref, own_ref, other_ref):
    odd = flags_ref[0] == 1
    before, between = entered(flags_ref, mine_ref, got_ref, before_ref)
    own_ref[...] = jnp.where(odd, between, before).astype(bf16)
    other_ref[...] = jnp.where(odd, before, between).astype(bf16)


def out_kernel(slots, blocks, flags_ref, *refs):
    entry_refs, refs = refs[: 4 - slots], refs[4 - slots :]
    (
        local_ref,
        gates_ref,
        coupled_ref,
        sums_ref,
        rows_ref,
        gain_ref,
        out_ref,
        first_ref,
        *second_refs,
        normed_scr,
    ) = refs
    wide = out_ref.shape[1] // blocks
    odd = flags_ref[0] == 1
    groups = coupled_ref.shape[2] // (2 * N)
    share = local_ref.shape[2] // groups
    count = sums_ref.shape[1]
    per_step = WIDE // P_SIZE
    if slots == 1:
        before, between = entered(flags_ref, *entry_refs)
        entries = [jnp.where(odd, between, before).astype(bf16)]
    else:
        own, other = [ref[...].astype(f32) for ref in entry_refs]
        entries = [jnp.where(odd, own, other).astype(bf16), jnp.where(odd, other, own).astype(bf16)]
    for s in range(slots):
        sums = jnp.concatenate([sums_ref[s, jj] for jj in range(count)], axis=0)
        line = lax.broadcasted_iota(jnp.int32, sums.shape, 0) % 8
        growth = rows_ref[s, 4:5] * jnp.exp(jnp.where(line < per_step, sums, 0.0))
        spread = spread_heads(turned(growth), per_step, count)
        for g in range(groups):
            own = slice(g * share, (g + 1) * share)
            queries = coupled_ref[s, :, g * 2 * N + N : (g + 1) * 2 * N]
            carried = dot(queries, entries[s][:, own])
            scanned = local_ref[s, :, own] + spread[:, own] * carried
            gated = scanned * jax.nn.silu(gates_ref[s, :, own].astype(f32))
            scale = lax.rsqrt(jnp.mean(gated * gated, axis=-1, keepdims=True) + epsilon)
            normed_scr[s * CH : (s + 1) * CH, own] = (gated * scale * gain_ref[:, own]).astype(
                bf16
            )

    normed = normed_scr[...]
    low = flags_ref[1] == 0
    for j in range(blocks):
        own = slice(j * wide, (j + 1) * wide)
        branch = dot(normed, out_ref[:, own])
        if slots == 2:
            first_ref[:, own] = branch[0:CH].astype(bf16)
            second_refs[0][:, own] = branch[CH : 2 * CH].astype(bf16)
        else:
            upper, lower = branch[0:HALF], branch[HALF:CH]
            first_ref[:, own] = jnp.where(low, upper, lower).astype(bf16)
            per_piece = blocks // len(second_refs)
            at = j % per_piece
            second_refs[j // per_piece][:, at * wide : (at + 1) * wide] = jnp.where(
                low, lower, upper
            ).astype(bf16)


def summed(refs):
    return sum(ref[...].astype(f32) for ref in refs)


def add_kernel(flags_ref, mine_ref, *refs):
    del flags_ref
    *other_refs, out_ref = refs
    wide = out_ref.shape[1] // len(other_refs)
    for j, ref in enumerate(other_refs):
        own = slice(j * wide, (j + 1) * wide)
        out_ref[:, own] = (mine_ref[:, own].astype(f32) + ref[...].astype(f32)).astype(bf16)


def give_kernel(flags_ref, *refs):
    *back, out_ref = refs
    chips = len(back) // 2
    out_ref[...] = jnp.where(
        flags_ref[1] == 0, summed(back[chips:]), summed(back[:chips])
    ).astype(bf16)


def close_kernel(flags_ref, rezero_ref, own_ref, mine_ref, others_ref, theirs_ref, *refs):
    *back, out_ref = refs
    chips = len(back) // 2
    core = flags_ref[1]
    ours = jnp.where(core == 0, summed(back[:chips]), summed(back[chips:]))
    for at, far in ((core, ours), (1 - core, theirs_ref[...].astype(f32))):
        lines = pl.ds(pl.multiple_of(at * HALF, HALF), HALF)
        branch = mine_ref[lines].astype(f32) + others_ref[lines].astype(f32) + far
        out_ref[lines] = (own_ref[lines].astype(f32) + rezero_ref[0] * branch).astype(bf16)


IN_VMEM = pl.BlockSpec(memory_space=pltpu.VMEM)
IN_SMEM = pl.BlockSpec(memory_space=pltpu.SMEM)
FLOPS_PER_US = 1_150_000_000


class Sequence:
    def __init__(self, flags):
        self.flags, self.token = flags, None

    def run(self, kernel, name, shapes, scratch, *operands, mib=2, us=1, scalars=()):
        tokens = [] if self.token is None else [self.token]
        given = 1 + len(scalars) + len(operands)

        def ordered(*refs):
            outs = refs[given + len(tokens) :]
            mark_ref = outs[len(shapes)]
            mark_ref[...] = jnp.zeros_like(mark_ref)
            kernel(*refs[:given], *outs[: len(shapes)], *outs[len(shapes) + 1 :])

        *results, self.token = pl.pallas_call(
            ordered,
            in_specs=[IN_SMEM] * (1 + len(scalars)) + [IN_VMEM] * (len(operands) + len(tokens)),
            out_specs=[IN_VMEM] * (len(shapes) + 1),
            out_shape=[*shapes, shape(f32, 8, CH)],
            scratch_shapes=scratch,
            compiler_params=pltpu.CompilerParams(vmem_limit_bytes=mib << 20),
            cost_estimate=pl.CostEstimate(
                flops=int(us * FLOPS_PER_US), bytes_accessed=0, transcendentals=0
            ),
            name=name,
        )(self.flags, *scalars, *operands, *tokens)
        return results

    def held(self, block):
        def hold(block_ref, token_ref, out_ref):
            del block_ref, token_ref, out_ref

        return pl.pallas_call(
            hold,
            in_specs=[IN_VMEM] * 2,
            out_specs=IN_VMEM,
            out_shape=shape(block.dtype, *block.shape),
            input_output_aliases={0: 0},
            compiler_params=pltpu.CompilerParams(vmem_limit_bytes=1 << 20),
            name="hold",
        )(block, self.token)


def shape(dtype, *sizes):
    return jax.ShapeDtypeStruct(sizes, dtype)


def mix(run, slots, streams, flip, sources, tails, segments, weights, small):
    value_weight, coupling_weight = weights
    width, narrow, depth = value_weight.shape[1], coupling_weight.shape[1], tails[0].shape[1]
    shapes = [
        shape(bf16, slots, CH, width),
        shape(bf16, slots, CH, narrow),
        shape(f32, slots, narrow // N, 8, CH),
        shape(f32, slots, 8, CH),
    ] + [shape(bf16, STATE_ROWS, width)] * slots
    scratch = [
        pltpu.VMEM((slots * (CH + TAILS), depth), bf16),
        pltpu.VMEM((2, slots, CH + TAIL, WIDE), f32),
    ]
    kernel = functools.partial(mix_kernel, slots, streams, flip)
    operands = (*sources, *tails, segments, *weights, *small)
    return run(kernel, f"mix{slots}", shapes, scratch, *operands, mib=8, us=4 * slots)


def scan(run, slots, flip, sources, rows, gate_weight, values, coupled, sums, skip):
    shapes = [shape(bf16, *values.shape), shape(f32, *values.shape)]
    scratch = [pltpu.VMEM((slots * CH, gate_weight.shape[0]), bf16)]
    kernel = functools.partial(scan_kernel, slots, flip)
    operands = (*sources, rows, gate_weight, values, coupled, sums, skip)
    return run(kernel, f"scan{slots}", shapes, scratch, *operands, mib=6, us=2 * slots)


def project_out(run, slots, entries, local, gates, coupled, sums, rows, gain, out_weight):
    width, depth = out_weight.shape
    lines = CH if slots == 2 else HALF
    scratch = [pltpu.VMEM((slots * CH, width), bf16)]
    kernel = functools.partial(out_kernel, slots, 8)
    operands = (*entries, local, gates, coupled, sums, rows, gain, out_weight)
    pieces = 1 if slots == 2 else PIECES
    shapes = [shape(bf16, lines, depth)] + [shape(bf16, lines, depth // pieces)] * pieces
    return run(kernel, f"out{slots}", shapes, scratch, *operands, mib=6, us=0.1)


def along(block, distance):
    spans = lax.axis_size("ctx")
    return lax.ppermute(block, "ctx", [(i, (i + distance) % spans) for i in range(spans)])


def tail_from(block, chips_on, flip):
    places, spans = lax.axis_size("fsdp"), lax.axis_size("ctx")
    route = [
        (((f + 2 * chips_on) % places ^ flip) * spans + c, f * spans + (c + 1) % spans)
        for f in range(places)
        for c in range(spans)
    ]
    return lax.ppermute(block, ("fsdp", "ctx"), route)


def partner(block, axis):
    return lax.ppermute(block, axis, [(i, i ^ 1) for i in range(lax.axis_size(axis))])


def over(block, distance):
    size = lax.axis_size("fsdp")
    return lax.ppermute(block, "fsdp", [(i, (i + 2 * distance) % size) for i in range(size)])


def joined(run, mine, got):
    return run(join_kernel, "join", [shape(bf16, *mine.shape)], [], mine, got, us=0.1)[0]


def chained(run, block):
    spans, width = lax.axis_size("ctx"), block.shape[1]
    distance = 2
    while distance < spans // 2:
        last = 2 * distance >= spans // 2
        out = [shape(bf16, N if last else STATE_ROWS, width)]
        kernel = functools.partial(chain_kernel, distance)
        block = run(kernel, "chain", out, [], block, along(block, distance), us=0.1)[0]
        distance *= 2
    return block


def on_device(
    tokens,
    segments,
    gate_weight,
    value_weight,
    coupling_weight,
    step_weight,
    value_conv,
    coupling_conv,
    value_shift,
    coupling_shift,
    step_bias,
    decay_log,
    skip_gain,
    norm_gain,
    out_weight,
    rezero,
):
    place = lax.axis_index("fsdp")
    span = lax.axis_index("ctx")
    chips = lax.axis_size("fsdp") // 2
    chip, core = place // 2, place % 2
    reach = value_conv.shape[0] - 1
    own = tokens[0]
    phases = [(d, j) for d in range(1, chips) for j in range(2)]
    far_streams = [(chip + d) % chips * 2 + j for d, j in phases]
    flags = jnp.stack([span % 2, core, span, place, place ^ 1] + far_streams).astype(jnp.int32)

    sequence = Sequence(flags)
    run = sequence.run

    arrived = {d: over(own, -d) for d in range(1, chips)}
    opposite = partner(own, "fsdp")
    half_shape = shape(bf16, HALF, own.shape[1])
    tail_shape = shape(bf16, TAILS, own.shape[1])
    tail = run(tail_kernel, "tail", [tail_shape], [], own, segments, opposite, us=8)[0]

    heads = step_weight.shape[1]
    head = jnp.broadcast_to(jnp.stack([step_bias, decay_log])[:, :, None], (2, heads, CH))
    skip = skip_gain[None]
    taps = jnp.concatenate([value_conv, coupling_conv], axis=1).astype(f32)
    shifts = jnp.concatenate([value_shift, coupling_shift])[None]
    taps = jnp.concatenate([taps, shifts, jnp.zeros((4 - reach, taps.shape[1]), f32)], axis=0)
    small = (step_weight.T, taps, head)
    gain = norm_gain[None]

    weights = (value_weight, coupling_weight)
    near = [tail_from(tail, 0, flip) for flip in range(2)]
    far = {d: [tail_from(tail, d, flip) for flip in range(2)] for d in range(1, chips)}
    near_sources = (own, opposite)
    values, coupled, near_sums, near_rows, given, kept = mix(
        run, 2, (3, 4), None, near_sources, near + sum(far.values(), []), segments, weights, small
    )
    near_mixed = (values, coupled, near_sums)
    near_got = partner(given, "ctx")

    far_mixed = []
    for i, (d, j) in enumerate(phases):
        if j == 0:
            arrival = sequence.held(arrived[d])
            sources = (arrival, partner(arrival, "fsdp"))
        *mixed, state = mix(run, 1, (5 + i,), j, sources, far[d], segments, weights, small)
        far_mixed.append((sources, *mixed, state, partner(state, "ctx")))
        if i == 0:
            near_block = joined(run, kept, near_got)

    far_scans, blocks = [], []
    for (d, j), (sources, values, coupled, sums, rows, state, got) in zip(phases, far_mixed):
        blocks.append(joined(run, state, got))
        far_scans.append(
            scan(run, 1, j, sources, rows, gate_weight, values, coupled, sums, skip)
        )
        if len(blocks) == 1:
            near_before = along(chained(run, near_block), 2)
    near_gates, near_local = scan(
        run, 2, None, near_sources, near_rows, gate_weight, *near_mixed, skip
    )
    entry_shape = shape(bf16, N, kept.shape[1])
    befores = []
    for block in blocks:
        befores.append(along(chained(run, block), 2))
        if len(befores) == 1:
            entry, other_entry = run(
                finish_kernel, "finish", [entry_shape] * 2, [], kept, near_got, near_before, us=0.1
            )
    near_entries = (entry, partner(other_entry, "ctx"))

    back = {}
    for (d, j), before, (gates, local), (_, _, coupled, sums, rows, state, got) in zip(
        phases, befores, far_scans, far_mixed
    ):
        mine, *others = project_out(
            run, 1, (state, got, before), local, gates, coupled, sums, rows, gain, out_weight
        )
        others = [partner(piece, "fsdp") for piece in others]
        total = run(add_kernel, "add", [half_shape], [], mine, *others, us=0.1)[0]
        back[d, j] = over(total, d)

    mine, others = project_out(
        run,
        2,
        near_entries,
        near_local,
        near_gates,
        near_mixed[1],
        near_sums,
        near_rows,
        gain,
        out_weight,
    )
    others = partner(others, "fsdp")
    returned = [back[d, j] for j in range(2) for d in range(1, chips)]
    given = run(give_kernel, "give", [half_shape], [], *returned, us=0.1)[0]
    return run(
        close_kernel,
        "close",
        [shape(bf16, *own.shape)],
        [],
        own,
        mine,
        others,
        partner(given, "fsdp"),
        *returned,
        mib=4,
        scalars=(rezero,),
    )[0][None]


def solution(mesh):
    return jax.shard_map(
        on_device,
        mesh=mesh,
        in_specs=(
            P("fsdp", "ctx", None),
            P(None, "ctx"),
            P(None, "fsdp"),
            P(None, "fsdp"),
            P(None, "fsdp"),
            P(None, "fsdp"),
            P(None, "fsdp"),
            P(None, "fsdp"),
            P("fsdp"),
            P("fsdp"),
            P("fsdp"),
            P("fsdp"),
            P("fsdp"),
            P("fsdp"),
            P("fsdp", None),
            P(),
        ),
        out_specs=P("fsdp", "ctx", None),
        check_vma=False,
    )
```

time: 453 us -> 121 us (0.27)
  waiting for transfers between devices: 288 us -> 42.2 us
  matrix products: 66.6 us -> 0 us
  Pallas kernels: 0 us -> 45.5 us
  blocking collectives: 27.9 us -> 0 us
  local copies, waits for them, and re-layouts: 25.4 us -> 2.2 us
  other arithmetic: 18 us -> 1.51 us
  starting transfers between devices: 11.9 us -> 28 us
  between operations: 14.3 us -> 0.99 us
    all_gather x2 -> x0, waiting for transfers between devices: 204 us -> none  [the longest x1 175 us: carried_in(): gathered = jax.tree.map(lambda a: lax.all_gather(a, axis), part)]
    reduce_scatter x1 -> x0, waiting for transfers between devices: 83 us -> none  [on_device(): lax.psum_scatter(jnp.einsum('btk,kd->btd', normed, out_weight, preferred_...]
    dot_general x10 -> x0, matrix products: 66.6 us -> none  [the longest x4 20.9 us: on_device(): jnp.dot(flat_rows, matrix, preferred_element_type=jnp.float32)]
    pallas_call x0 -> x22, Pallas kernels: none -> 45.5 us  [the longest x21 45.5 us: run(): pl.pallas_call(ordered, in_specs=[IN_SMEM] * (1 + len(scalars)) + [IN_VME...]
    ppermute x3 -> x29, waiting for transfers between devices: 0.01 us -> 42.2 us  [the longest x3 18.6 us: over(): lax.ppermute(block, 'fsdp', [(i, (i + 2 * distance) % size) for i in rang...]
    all_gather x1 -> x0, blocking collectives: 27.9 us -> none  [carried_in(): gathered = jax.tree.map(lambda a: lax.all_gather(a, axis), part)]
    ppermute x3 -> x29, starting transfers between devices: 11.8 us -> 28 us  [the longest x16 8.34 us: partner(): lax.ppermute(block, axis, [(i, i ^ 1) for i in range(lax.axis_size(axis))])]
    convert_element_type x7 -> x1, other arithmetic: 13 us -> 0.72 us  [on_device(): taps = jnp.concatenate([value_conv, coupling_conv], axis=1).astype(f32)]
  transfers between devices with their start and end apart: 6 -> 29, of which waited for: 3 -> 15; matrix products, arithmetic and copies ran while one was open for 8% -> 1% of each run, Pallas kernels for 0% -> 36%
where the time goes in v2:
time: 121 us; the launch traced here: 120 us
  Pallas kernels  45.5 us (38%)
  waiting for transfers between devices  42.2 us (35%)
  starting transfers between devices  28 us (23%)
  local copies, waits for them, and re-layouts  2.2 us (2%)
  other arithmetic  1.51 us (1%)
    pallas_call x21, Pallas kernels, run(): pl.pallas_call(ordered, in_specs=[IN_SMEM] * (1 + len(scalars)) + [IN_VME...  45.5 us
    ppermute x3, waiting for transfers between devices, over(): lax.ppermute(block, 'fsdp', [(i, (i + 2 * distance) % size) for i in rang...  18.6 us
    ppermute x4, waiting for transfers between devices, tail_from(): return lax.ppermute(block, ('fsdp', 'ctx'), route)  10.3 us
    ppermute x6, waiting for transfers between devices, along(): lax.ppermute(block, 'ctx', [(i, (i + distance) % spans) for i in range(sp...  9.86 us
    ppermute x16, starting transfers between devices, partner(): lax.ppermute(block, axis, [(i, i ^ 1) for i in range(lax.axis_size(axis))])  8.34 us
    ppermute x6, starting transfers between devices, along(): lax.ppermute(block, 'ctx', [(i, (i + distance) % spans) for i in range(sp...  8.26 us
    ppermute x4, starting transfers between devices, tail_from(): return lax.ppermute(block, ('fsdp', 'ctx'), route)  6.47 us
    ppermute x3, starting transfers between devices, over(): lax.ppermute(block, 'fsdp', [(i, (i + 2 * distance) % size) for i in rang...  4.92 us
  transfers between devices with their start and end apart: 29, of which 15 were waited for; matrix products, arithmetic and copies ran while one was open for 1% of the time, Pallas kernels for 36%

profile of v2, /device:TPU:0, one launch (start us, length us, event | category | flops | bytes accessed | tf_op | source)
XLA Modules:
  0.0 120.4 jit_solution(17981292893459683602)
XLA Ops:
  0.5 2.5 %collective-permute-start.6 = (bf16[128,4096]{1,0:T(8,128)(2,1)}, bf16[128,4096]{1,0:T(8,128)(2,1)S(1)}, u32[]{:S(2)}, u32[]{:S(2)}) collective-permute-start(bf16[128,4096]{1,0:T(8,128)(2,1)} %bitcast.20), channel_id=1, source_target_pairs={{0,16},{8,24},{16,0},{24,8},{1,17},{9,25},{17,1},{25,9},{2,18},{10... | collective-permute-start | bytes 3145736 | tf_op jit(solution)/shard_map/ppermute | solution.py:534
  7.1 1.5 %collective-permute-start.1 = (bf16[16,4096]{1,0:T(8,128)(2,1)S(1)}, bf16[16,4096]{1,0:T(8,128)(2,1)S(1)}, u32[]{:S(2)}, u32[]{:S(2)}) collective-permute-start(bf16[16,4096]{1,0:T(8,128)(2,1)S(1)} %get-tuple-element.72), channel_id=1, source_target_pairs={{0,1},{1,2},{2,3},{3,4},{4,5},{5,6},{6,7},{7,0},{8,9},{9,10},{10,1... | collective-permute-start | bytes 393224 | tf_op jit(solution)/shard_map/ppermute | solution.py:525
  9.8 2.1 %collective-permute-start.3 = (bf16[16,4096]{1,0:T(8,128)(2,1)S(1)}, bf16[16,4096]{1,0:T(8,128)(2,1)S(1)}, u32[]{:S(2)}, u32[]{:S(2)}) collective-permute-start(bf16[16,4096]{1,0:T(8,128)(2,1)S(1)} %get-tuple-element.72), channel_id=1, source_target_pairs={{16,1},{17,2},{18,3},{19,4},{20,5},{21,6},{22,7},{23,0},{24,9},{25... | collective-permute-start | bytes 393224 | tf_op jit(solution)/shard_map/ppermute | solution.py:525
  11.8 1.7 %collective-permute-start.4 = (bf16[16,4096]{1,0:T(8,128)(2,1)S(1)}, bf16[16,4096]{1,0:T(8,128)(2,1)S(1)}, u32[]{:S(2)}, u32[]{:S(2)}) collective-permute-start(bf16[16,4096]{1,0:T(8,128)(2,1)S(1)} %get-tuple-element.72), channel_id=1, source_target_pairs={{24,1},{25,2},{26,3},{27,4},{28,5},{29,6},{30,7},{31,0},{16,9},{17... | collective-permute-start | bytes 393224 | tf_op jit(solution)/shard_map/ppermute | solution.py:525
  13.7 2.5 %collective-permute-done.1.refs_3_ = bf16[16,4096]{1,0:T(8,128)(2,1)S(1)} collective-permute-done((bf16[16,4096]{1,0:T(8,128)(2,1)S(1)}, bf16[16,4096]{1,0:T(8,128)(2,1)S(1)}, u32[]{:S(2)}, u32[]{:S(2)}) %collective-permute-start.1) | collective-permute-done | bytes 131104 | tf_op jit(solution)/shard_map/ppermute | solution.py:525
  16.2 1.6 %collective-permute-done.2.refs_4_ = bf16[16,4096]{1,0:T(8,128)(2,1)S(1)} collective-permute-done((bf16[16,4096]{1,0:T(8,128)(2,1)S(1)}, bf16[16,4096]{1,0:T(8,128)(2,1)S(1)}, u32[]{:S(2)}, u32[]{:S(2)}) %collective-permute-start.2) | collective-permute-done | bytes 131104 | tf_op jit(solution)/shard_map/ppermute | solution.py:525
  17.8 4.8 %collective-permute-done.3.refs_5_.refs_3_ = bf16[16,4096]{1,0:T(8,128)(2,1)S(1)} collective-permute-done((bf16[16,4096]{1,0:T(8,128)(2,1)S(1)}, bf16[16,4096]{1,0:T(8,128)(2,1)S(1)}, u32[]{:S(2)}, u32[]{:S(2)}) %collective-permute-start.3) | collective-permute-done | bytes 131104 | tf_op jit(solution)/shard_map/ppermute | solution.py:525
  22.6 1.4 %collective-permute-done.4.refs_6_.refs_4_ = bf16[16,4096]{1,0:T(8,128)(2,1)S(1)} collective-permute-done((bf16[16,4096]{1,0:T(8,128)(2,1)S(1)}, bf16[16,4096]{1,0:T(8,128)(2,1)S(1)}, u32[]{:S(2)}, u32[]{:S(2)}) %collective-permute-start.4) | collective-permute-done | bytes 131104 | tf_op jit(solution)/shard_map/ppermute | solution.py:525
  24.1 7.7 %mix2.1 = (bf16[2,128,1024]{2,1,0:T(8,128)(2,1)S(1)}, bf16[2,128,512]{2,1,0:T(8,128)(2,1)S(1)}, f32[2,4,8,128]{3,2,1,0:T(8,128)S(1)}, f32[2,8,128]{2,1,0:T(8,128...) custom-call(s32[7]{0:T(128)S(1)} %stack.40.refs_0_, ...), custom_call_target="tpu_custom_call" | custom-call | flops 9200000000 | tf_op jit(solution)/shard_map/mix2/pallas_call | solution.py:443
  32.6 1.7 %collective-permute-start.5 = (bf16[144,1024]{1,0:T(8,128)(2,1)S(1)}, bf16[144,1024]{1,0:T(8,128)(2,1)S(1)}, u32[]{:S(2)}, u32[]{:S(2)}) collective-permute-start(bf16[144,1024]{1,0:T(8,128)(2,1)S(1)} %get-tuple-element.75), channel_id=1, source_target_pairs={{0,1},{1,0},{2,3},{3,2},{4,5},{5,4},{6,7},{7,6},{8,9},{9,8},{10,11... | collective-permute-start | bytes 884744 | tf_op jit(solution)/shard_map/ppermute | solution.py:529
  35.3 4.6 %mix1.2 = (bf16[1,128,1024]{2,1,0:T(8,128)(2,1)S(1)}, bf16[1,128,512]{2,1,0:T(8,128)(2,1)S(1)}, f32[1,4,8,128]{3,2,1,0:T(8,128)S(1)}, f32[1,8,128]{2,1,0:T(8,128...) custom-call(s32[7]{0:T(128)S(1)} %stack.40.refs_0_, bf16[128,4096]{1,0:T(8,128)(2,1)S(1)} %hold.1.refs_1_, ...), custom_call_target="tpu_custom_call" | custom-call | flops 4600000000 | tf_op jit(solution)/shard_map/mix1/pallas_call | solution.py:443
  39.9 1.8 %collective-permute-start.9 = (bf16[144,1024]{1,0:T(8,128)(2,1)S(1)}, bf16[144,1024]{1,0:T(8,128)(2,1)S(1)}, u32[]{:S(2)}, u32[]{:S(2)}) collective-permute-start(bf16[144,1024]{1,0:T(8,128)(2,1)S(1)} %get-tuple-element.83.refs_1_), channel_id=1, source_target_pairs={{0,1},{1,0},{2,3},{3,2},{4,5},{5,4},{6,7},{7,6},{8,9},{9,8},{10,11... | collective-permute-start | bytes 884744 | tf_op jit(solution)/shard_map/ppermute | solution.py:529
  42.7 1.9 %collective-permute-start.8 = (bf16[144,1024]{1,0:T(8,128)(2,1)S(1)}, bf16[144,1024]{1,0:T(8,128)(2,1)S(1)}, u32[]{:S(2)}, u32[]{:S(2)}) collective-permute-start(bf16[144,1024]{1,0:T(8,128)(2,1)S(1)} %get-tuple-element.78.refs_1_), channel_id=1, source_target_pairs={{0,2},{1,3},{2,4},{3,5},{4,6},{5,7},{6,0},{7,1},{8,10},{9,11},{10,... | collective-permute-start | bytes 884744 | tf_op jit(solution)/shard_map/ppermute | solution.py:515
  44.6 4.7 %mix1.3 = (bf16[1,128,1024]{2,1,0:T(8,128)(2,1)S(1)}, bf16[1,128,512]{2,1,0:T(8,128)(2,1)S(1)}, f32[1,4,8,128]{3,2,1,0:T(8,128)S(1)}, f32[1,8,128]{2,1,0:T(8,128...) custom-call(s32[7]{0:T(128)S(1)} %stack.40.refs_0_, bf16[128,4096]{1,0:T(8,128)(2,1)S(1)} %hold.1.refs_1_, ...), custom_call_target="tpu_custom_call" | custom-call | flops 4600000000 | tf_op jit(solution)/shard_map/mix1/pallas_call | solution.py:443
  49.3 1.6 %collective-permute-start.12 = (bf16[144,1024]{1,0:T(8,128)(2,1)S(1)}, bf16[144,1024]{1,0:T(8,128)(2,1)S(1)}, u32[]{:S(2)}, u32[]{:S(2)}) collective-permute-start(bf16[144,1024]{1,0:T(8,128)(2,1)S(1)} %get-tuple-element.98.refs_1_), channel_id=1, source_target_pairs={{0,1},{1,0},{2,3},{3,2},{4,5},{5,4},{6,7},{7,6},{8,9},{9,8},{10,11... | collective-permute-start | bytes 884744 | tf_op jit(solution)/shard_map/ppermute | solution.py:529
  51.6 1.6 %collective-permute-start.11 = (bf16[144,1024]{1,0:T(8,128)(2,1)S(1)}, bf16[144,1024]{1,0:T(8,128)(2,1)S(1)}, u32[]{:S(2)}, u32[]{:S(2)}) collective-permute-start(bf16[144,1024]{1,0:T(8,128)(2,1)S(1)} %get-tuple-element.89.refs_1_), channel_id=1, source_target_pairs={{0,2},{1,3},{2,4},{3,5},{4,6},{5,7},{6,0},{7,1},{8,10},{9,11},{10,... | collective-permute-start | bytes 884744 | tf_op jit(solution)/shard_map/ppermute | solution.py:515
  53.2 2.6 %scan1.2 = (bf16[1,128,1024]{2,1,0:T(8,128)(2,1)S(1)}, f32[1,128,1024]{2,1,0:T(8,128)S(1)}, f32[8,128]{1,0:T(8,128)S(1)}) custom-call(s32[7]{0:T(128)S(1)} %stack.40.refs_0_, bf16[128,4096]{1,0:T(8,128)(2,1)S(1)} %hold.1.refs_1_, bf16[128,4096]{1,0:T(8,128)(2,1)S(1)} %collective-permute-done.7.refs_2_, f32[1,8,128]{2,1,0:T(8,128)S(1)} %get-tuple-element.79.refs_3_.refs_8_, ...), custom_call_target="tpu_custom_call" | custom-call | flops 2300000000 | tf_op jit(solution)/shard_map/scan1/pallas_call | solution.py:443
  56.5 1.6 %collective-permute-start.10 = (bf16[128,1024]{1,0:T(8,128)(2,1)S(1)}, bf16[128,1024]{1,0:T(8,128)(2,1)S(1)}, u32[]{:S(2)}, u32[]{:S(2)}) collective-permute-start(bf16[128,1024]{1,0:T(8,128)(2,1)S(1)} %get-tuple-element.88), channel_id=1, source_target_pairs={{0,2},{1,3},{2,4},{3,5},{4,6},{5,7},{6,0},{7,1},{8,10},{9,11},{10,... | collective-permute-start | bytes 786440 | tf_op jit(solution)/shard_map/ppermute | solution.py:515
  58.9 1.2 %collective-permute-start.14 = (bf16[144,1024]{1,0:T(8,128)(2,1)S(1)}, bf16[144,1024]{1,0:T(8,128)(2,1)S(1)}, u32[]{:S(2)}, u32[]{:S(2)}) collective-permute-start(bf16[144,1024]{1,0:T(8,128)(2,1)S(1)} %get-tuple-element.108.refs_1_), channel_id=1, source_target_pairs={{0,2},{1,3},{2,4},{3,5},{4,6},{5,7},{6,0},{7,1},{8,10},{9,11},{10,... | collective-permute-start | bytes 884744 | tf_op jit(solution)/shard_map/ppermute | solution.py:515
  60.1 2.7 %scan1.3 = (bf16[1,128,1024]{2,1,0:T(8,128)(2,1)S(1)}, f32[1,128,1024]{2,1,0:T(8,128)S(1)}, f32[8,128]{1,0:T(8,128)S(1)}) custom-call(s32[7]{0:T(128)S(1)} %stack.40.refs_0_, bf16[128,4096]{1,0:T(8,128)(2,1)S(1)} %hold.1.refs_1_, bf16[128,4096]{1,0:T(8,128)(2,1)S(1)} %collective-permute-done.7.refs_2_, f32[1,8,128]{2,1,0:T(8,128)S(1)} %get-tuple-element.94.refs_3_.refs_8_, ...), custom_call_target="tpu_custom_call" | custom-call | flops 2300000000 | tf_op jit(solution)/shard_map/scan1/pallas_call | solution.py:443
  62.8 4.1 %scan2.1 = (bf16[2,128,1024]{2,1,0:T(8,128)(2,1)S(1)}, f32[2,128,1024]{2,1,0:T(8,128)S(1)}, f32[8,128]{1,0:T(8,128)S(1)}) custom-call(s32[7]{0:T(128)S(1)} %stack.40.refs_0_, bf16[128,4096]{1,0:T(8,128)(2,1)S(1)} %bitcast.23, bf16[128,4096]{1,0:T(8,128)(2,1)S(1)} %collective-permute-done.refs_3_.refs_2_, f32[2,8,128]{2,1,0:T(8,128)S(1)} %get-tuple-element.90.refs_3_.refs_7_, ...), custom_call_target="tpu_custom_call" | custom-call | flops 4600000000 | tf_op jit(solution)/shard_map/scan2/pallas_call | solution.py:443
  67.5 1.6 %collective-permute-start.16 = (bf16[128,1024]{1,0:T(8,128)(2,1)S(1)}, bf16[128,1024]{1,0:T(8,128)(2,1)S(1)}, u32[]{:S(2)}, u32[]{:S(2)}) collective-permute-start(bf16[128,1024]{1,0:T(8,128)(2,1)S(1)} %get-tuple-element.113), channel_id=1, source_target_pairs={{0,2},{1,3},{2,4},{3,5},{4,6},{5,7},{6,0},{7,1},{8,10},{9,11},{10,... | collective-permute-start | bytes 786440 | tf_op jit(solution)/shard_map/ppermute | solution.py:515
  69.9 5.2 %collective-permute-done.14.refs_2_ = bf16[144,1024]{1,0:T(8,128)(2,1)S(1)} collective-permute-done((bf16[144,1024]{1,0:T(8,128)(2,1)S(1)}, bf16[144,1024]{1,0:T(8,128)(2,1)S(1)}, u32[]{:S(2)}, u32[]{:S(2)}) %collective-permute-start.14) | collective-permute-done | bytes 294944 | tf_op jit(solution)/shard_map/ppermute | solution.py:515
  76.0 4.7 %collective-permute-done.16.refs_3_ = bf16[128,1024]{1,0:T(8,128)(2,1)S(1)} collective-permute-done((bf16[128,1024]{1,0:T(8,128)(2,1)S(1)}, bf16[128,1024]{1,0:T(8,128)(2,1)S(1)}, u32[]{:S(2)}, u32[]{:S(2)}) %collective-permute-start.16) | collective-permute-done | bytes 262176 | tf_op jit(solution)/shard_map/ppermute | solution.py:515
  80.7 2.6 %out1.2 = (bf16[64,4096]{1,0:T(8,128)(2,1)S(1)}, bf16[64,1024]{1,0:T(8,128)(2,1)S(1)}, bf16[64,1024]{1,0:T(8,128)(2,1)S(1)}, bf16[64,1024]{1,0:T(8,128)(2,1)S(1)...) custom-call(s32[7]{0:T(128)S(1)} %stack.40.refs_0_, bf16[144,1024]{1,0:T(8,128)(2,1)S(1)} %get-tuple-element.83.refs_1_, ...), custom_call_target="tpu_custom_call" | custom-call | flops 115000000 | tf_op jit(solution)/shard_map/out1/pallas_call | solution.py:443
  86.1 2.6 %out1.3 = (bf16[64,4096]{1,0:T(8,128)(2,1)S(1)}, bf16[64,1024]{1,0:T(8,128)(2,1)S(1)}, bf16[64,1024]{1,0:T(8,128)(2,1)S(1)}, bf16[64,1024]{1,0:T(8,128)(2,1)S(1)...) custom-call(s32[7]{0:T(128)S(1)} %stack.40.refs_0_, bf16[144,1024]{1,0:T(8,128)(2,1)S(1)} %get-tuple-element.98.refs_1_, ...), custom_call_target="tpu_custom_call" | custom-call | flops 115000000 | tf_op jit(solution)/shard_map/out1/pallas_call | solution.py:443
  90.1 1.5 %collective-permute-start.26 = (bf16[64,4096]{1,0:T(8,128)(2,1)S(1)}, bf16[64,4096]{1,0:T(8,128)(2,1)S(1)}, u32[]{:S(2)}, u32[]{:S(2)}) collective-permute-start(bf16[64,4096]{1,0:T(8,128)(2,1)S(1)} %get-tuple-element.133), channel_id=1, source_target_pairs={{0,16},{8,24},{16,0},{24,8},{1,17},{9,25},{17,1},{25,9},{2,18},{10... | collective-permute-start | bytes 1572872 | tf_op jit(solution)/shard_map/ppermute | solution.py:534
  93.2 4.5 %out2.1 = (bf16[128,4096]{1,0:T(8,128)(2,1)S(1)}, bf16[128,4096]{1,0:T(8,128)(2,1)S(1)}, f32[8,128]{1,0:T(8,128)S(1)}) custom-call(s32[7]{0:T(128)S(1)} %stack.40.refs_0_, bf16[128,1024]{1,0:T(8,128)(2,1)S(1)} %get-tuple-element.104.refs_1_, bf16[128,1024]{1,0:T(8,128)(2,1)S(1)} %collective-permute-done.13.refs_2_, ...), custom_call_target="tpu_custom_call" | custom-call | flops 115000000 | tf_op jit(solution)/shard_map/out2/pallas_call | solution.py:443
  97.8 7.0 %collective-permute-done.26.refs_1_.refs_6_ = bf16[64,4096]{1,0:T(8,128)(2,1)S(1)} collective-permute-done((bf16[64,4096]{1,0:T(8,128)(2,1)S(1)}, bf16[64,4096]{1,0:T(8,128)(2,1)S(1)}, u32[]{:S(2)}, u32[]{:S(2)}) %collective-permute-start.26) | collective-permute-done | bytes 524320 | tf_op jit(solution)/shard_map/ppermute | solution.py:534
  104.9 10.6 %collective-permute-done.27.refs_2_.refs_7_ = bf16[64,4096]{1,0:T(8,128)(2,1)S(1)} collective-permute-done((bf16[64,4096]{1,0:T(8,128)(2,1)S(1)}, bf16[64,4096]{1,0:T(8,128)(2,1)S(1)}, u32[]{:S(2)}, u32[]{:S(2)}) %collective-permute-start.27) | collective-permute-done | bytes 524320 | tf_op jit(solution)/shard_map/ppermute | solution.py:534
  116.9 1.2 %collective-permute-done.28.refs_5_ = bf16[64,4096]{1,0:T(8,128)(2,1)S(1)} collective-permute-done((bf16[64,4096]{1,0:T(8,128)(2,1)S(1)}, bf16[64,4096]{1,0:T(8,128)(2,1)S(1)}, u32[]{:S(2)}, u32[]{:S(2)}) %collective-permute-start.28) | collective-permute-done | bytes 524320 | tf_op jit(solution)/shard_map/ppermute | solution.py:529
  118.2 2.2 %close.1 = (bf16[128,4096]{1,0:T(8,128)(2,1)}, f32[8,128]{1,0:T(8,128)}) custom-call(s32[7]{0:T(128)S(1)} %stack.40.refs_0_, f32[1]{0:T(128)S(6)} %copy.19.refs_1_, bf16[128,4096]{1,0:T(8,128)(2,1)S(1)} %bitcast.24, bf16[128,4096]{1,0:T(8,128)(2,1)S(1)} %get-tuple-element.131.refs_3_, bf16[128,4096]{1,0:T(8,128)(2,1)S(1)} %collective-permute-done.25.refs_4_, ...), custom_call_target="tpu_custom_call" | custom-call | flops 1150000000 | tf_op jit(solution)/shard_map/close/pallas_call | solution.py:443
  (88 shorter events, 19.5 us)
Async XLA Ops:
  0.0 4.6 %collective-permute-start = (bf16[128,4096]{1,0:T(8,128)(2,1)}, bf16[128,4096]{1,0:T(8,128)(2,1)S(1)}, u32[]{:S(2)}, u32[]{:S(2)}) collective-permute-start(bf16[128,4096]{1,0:T(8,128)(2,1)} %bitcast.19), channel_id=1, source_target_pairs={{0,8},{8,0},{16,24},{24,16},{1,9},{9,1},{17,25},{25,17},{2,10},{10... | collective-permute-start | bytes 3145736 | tf_op jit(solution)/shard_map/ppermute | solution.py:529
  0.5 32.2 %collective-permute-start.6 = (bf16[128,4096]{1,0:T(8,128)(2,1)}, bf16[128,4096]{1,0:T(8,128)(2,1)S(1)}, u32[]{:S(2)}, u32[]{:S(2)}) collective-permute-start(bf16[128,4096]{1,0:T(8,128)(2,1)} %bitcast.20), channel_id=1, source_target_pairs={{0,16},{8,24},{16,0},{24,8},{1,17},{9,25},{17,1},{25,9},{2,18},{10... | collective-permute-start | bytes 3145736 | tf_op jit(solution)/shard_map/ppermute | solution.py:534
  7.1 9.1 %collective-permute-start.1 = (bf16[16,4096]{1,0:T(8,128)(2,1)S(1)}, bf16[16,4096]{1,0:T(8,128)(2,1)S(1)}, u32[]{:S(2)}, u32[]{:S(2)}) collective-permute-start(bf16[16,4096]{1,0:T(8,128)(2,1)S(1)} %get-tuple-element.72), channel_id=1, source_target_pairs={{0,1},{1,2},{2,3},{3,4},{4,5},{5,6},{6,7},{7,0},{8,9},{9,10},{10,1... | collective-permute-start | bytes 393224 | tf_op jit(solution)/shard_map/ppermute | solution.py:525
  8.7 9.1 %collective-permute-start.2 = (bf16[16,4096]{1,0:T(8,128)(2,1)S(1)}, bf16[16,4096]{1,0:T(8,128)(2,1)S(1)}, u32[]{:S(2)}, u32[]{:S(2)}) collective-permute-start(bf16[16,4096]{1,0:T(8,128)(2,1)S(1)} %get-tuple-element.72), channel_id=1, source_target_pairs={{8,1},{9,2},{10,3},{11,4},{12,5},{13,6},{14,7},{15,0},{0,9},{1,10}... | collective-permute-start | bytes 393224 | tf_op jit(solution)/shard_map/ppermute | solution.py:525
  9.8 12.8 %collective-permute-start.3 = (bf16[16,4096]{1,0:T(8,128)(2,1)S(1)}, bf16[16,4096]{1,0:T(8,128)(2,1)S(1)}, u32[]{:S(2)}, u32[]{:S(2)}) collective-permute-start(bf16[16,4096]{1,0:T(8,128)(2,1)S(1)} %get-tuple-element.72), channel_id=1, source_target_pairs={{16,1},{17,2},{18,3},{19,4},{20,5},{21,6},{22,7},{23,0},{24,9},{25... | collective-permute-start | bytes 393224 | tf_op jit(solution)/shard_map/ppermute | solution.py:525
  11.8 12.2 %collective-permute-start.4 = (bf16[16,4096]{1,0:T(8,128)(2,1)S(1)}, bf16[16,4096]{1,0:T(8,128)(2,1)S(1)}, u32[]{:S(2)}, u32[]{:S(2)}) collective-permute-start(bf16[16,4096]{1,0:T(8,128)(2,1)S(1)} %get-tuple-element.72), channel_id=1, source_target_pairs={{24,1},{25,2},{26,3},{27,4},{28,5},{29,6},{30,7},{31,0},{16,9},{17... | collective-permute-start | bytes 393224 | tf_op jit(solution)/shard_map/ppermute | solution.py:525
  32.6 2.7 %collective-permute-start.7 = (bf16[128,4096]{1,0:T(8,128)(2,1)S(1)}, bf16[128,4096]{1,0:T(8,128)(2,1)S(1)}, u32[]{:S(2)}, u32[]{:S(2)}) collective-permute-start(bf16[128,4096]{1,0:T(8,128)(2,1)S(1)} %hold.1.refs_1_), channel_id=1, source_target_pairs={{0,8},{8,0},{16,24},{24,16},{1,9},{9,1},{17,25},{25,17},{2,10},{10... | collective-permute-start | bytes 3145736 | tf_op jit(solution)/shard_map/ppermute | solution.py:529
  32.6 9.4 %collective-permute-start.5 = (bf16[144,1024]{1,0:T(8,128)(2,1)S(1)}, bf16[144,1024]{1,0:T(8,128)(2,1)S(1)}, u32[]{:S(2)}, u32[]{:S(2)}) collective-permute-start(bf16[144,1024]{1,0:T(8,128)(2,1)S(1)} %get-tuple-element.75), channel_id=1, source_target_pairs={{0,1},{1,0},{2,3},{3,2},{4,5},{5,4},{6,7},{7,6},{8,9},{9,8},{10,11... | collective-permute-start | bytes 884744 | tf_op jit(solution)/shard_map/ppermute | solution.py:529
  35.3 17.9 %slice-start.2 = ((s8[8388608]{0:T(1024)(128)(4,1)}), s8[4194304]{0:T(1024)(128)(4,1)S(1)}, s32[]{:S(2)}) async-start(s8[8388608]{0:T(1024)(128)(4,1)} %bitcast.17), calls=%async_computation.2 | async-start | bytes 8388608
  39.9 11.0 %collective-permute-start.9 = (bf16[144,1024]{1,0:T(8,128)(2,1)S(1)}, bf16[144,1024]{1,0:T(8,128)(2,1)S(1)}, u32[]{:S(2)}, u32[]{:S(2)}) collective-permute-start(bf16[144,1024]{1,0:T(8,128)(2,1)S(1)} %get-tuple-element.83.refs_1_), channel_id=1, source_target_pairs={{0,1},{1,0},{2,3},{3,2},{4,5},{5,4},{6,7},{7,6},{8,9},{9,8},{10,11... | collective-permute-start | bytes 884744 | tf_op jit(solution)/shard_map/ppermute | solution.py:529
  42.7 13.2 %collective-permute-start.8 = (bf16[144,1024]{1,0:T(8,128)(2,1)S(1)}, bf16[144,1024]{1,0:T(8,128)(2,1)S(1)}, u32[]{:S(2)}, u32[]{:S(2)}) collective-permute-start(bf16[144,1024]{1,0:T(8,128)(2,1)S(1)} %get-tuple-element.78.refs_1_), channel_id=1, source_target_pairs={{0,2},{1,3},{2,4},{3,5},{4,6},{5,7},{6,0},{7,1},{8,10},{9,11},{10,... | collective-permute-start | bytes 884744 | tf_op jit(solution)/shard_map/ppermute | solution.py:515
  49.3 8.8 %collective-permute-start.12 = (bf16[144,1024]{1,0:T(8,128)(2,1)S(1)}, bf16[144,1024]{1,0:T(8,128)(2,1)S(1)}, u32[]{:S(2)}, u32[]{:S(2)}) collective-permute-start(bf16[144,1024]{1,0:T(8,128)(2,1)S(1)} %get-tuple-element.98.refs_1_), channel_id=1, source_target_pairs={{0,1},{1,0},{2,3},{3,2},{4,5},{5,4},{6,7},{7,6},{8,9},{9,8},{10,11... | collective-permute-start | bytes 884744 | tf_op jit(solution)/shard_map/ppermute | solution.py:529
  51.6 15.3 %collective-permute-start.11 = (bf16[144,1024]{1,0:T(8,128)(2,1)S(1)}, bf16[144,1024]{1,0:T(8,128)(2,1)S(1)}, u32[]{:S(2)}, u32[]{:S(2)}) collective-permute-start(bf16[144,1024]{1,0:T(8,128)(2,1)S(1)} %get-tuple-element.89.refs_1_), channel_id=1, source_target_pairs={{0,2},{1,3},{2,4},{3,5},{4,6},{5,7},{6,0},{7,1},{8,10},{9,11},{10,... | collective-permute-start | bytes 884744 | tf_op jit(solution)/shard_map/ppermute | solution.py:515
  56.5 12.6 %collective-permute-start.10 = (bf16[128,1024]{1,0:T(8,128)(2,1)S(1)}, bf16[128,1024]{1,0:T(8,128)(2,1)S(1)}, u32[]{:S(2)}, u32[]{:S(2)}) collective-permute-start(bf16[128,1024]{1,0:T(8,128)(2,1)S(1)} %get-tuple-element.88), channel_id=1, source_target_pairs={{0,2},{1,3},{2,4},{3,5},{4,6},{5,7},{6,0},{7,1},{8,10},{9,11},{10,... | collective-permute-start | bytes 786440 | tf_op jit(solution)/shard_map/ppermute | solution.py:515
  58.9 16.2 %collective-permute-start.14 = (bf16[144,1024]{1,0:T(8,128)(2,1)S(1)}, bf16[144,1024]{1,0:T(8,128)(2,1)S(1)}, u32[]{:S(2)}, u32[]{:S(2)}) collective-permute-start(bf16[144,1024]{1,0:T(8,128)(2,1)S(1)} %get-tuple-element.108.refs_1_), channel_id=1, source_target_pairs={{0,2},{1,3},{2,4},{3,5},{4,6},{5,7},{6,0},{7,1},{8,10},{9,11},{10,... | collective-permute-start | bytes 884744 | tf_op jit(solution)/shard_map/ppermute | solution.py:515
  60.1 20.6 %slice-start = ((s8[8388608]{0:T(1024)(128)(4,1)}), s8[4194304]{0:T(1024)(128)(4,1)S(1)}, s32[]{:S(2)}) async-start(s8[8388608]{0:T(1024)(128)(4,1)} %bitcast.15), calls=%async_computation | async-start | bytes 8388608
  62.8 17.9 %slice-start.1 = ((s8[8388608]{0:T(1024)(128)(4,1)}), s8[4194304]{0:T(1024)(128)(4,1)S(1)}, s32[]{:S(2)}) async-start(s8[8388608]{0:T(1024)(128)(4,1)} %bitcast.15), calls=%async_computation.1 | async-start | bytes 8388608
  67.5 13.1 %collective-permute-start.16 = (bf16[128,1024]{1,0:T(8,128)(2,1)S(1)}, bf16[128,1024]{1,0:T(8,128)(2,1)S(1)}, u32[]{:S(2)}, u32[]{:S(2)}) collective-permute-start(bf16[128,1024]{1,0:T(8,128)(2,1)S(1)} %get-tuple-element.113), channel_id=1, source_target_pairs={{0,2},{1,3},{2,4},{3,5},{4,6},{5,7},{6,0},{7,1},{8,10},{9,11},{10,... | collective-permute-start | bytes 786440 | tf_op jit(solution)/shard_map/ppermute | solution.py:515
  75.7 10.4 %collective-permute-start.15 = (bf16[128,1024]{1,0:T(8,128)(2,1)S(1)}, bf16[128,1024]{1,0:T(8,128)(2,1)S(1)}, u32[]{:S(2)}, u32[]{:S(2)}) collective-permute-start(bf16[128,1024]{1,0:T(8,128)(2,1)S(1)} %get-tuple-element.110), channel_id=1, source_target_pairs={{0,2},{1,3},{2,4},{3,5},{4,6},{5,7},{6,0},{7,1},{8,10},{9,11},{10,... | collective-permute-start | bytes 786440 | tf_op jit(solution)/shard_map/ppermute | solution.py:515
  83.3 1.4 %collective-permute-start.17 = (bf16[64,1024]{1,0:T(8,128)(2,1)S(1)}, bf16[64,1024]{1,0:T(8,128)(2,1)S(1)}, u32[]{:S(2)}, u32[]{:S(2)}) collective-permute-start(bf16[64,1024]{1,0:T(8,128)(2,1)S(1)} %get-tuple-element.118), channel_id=1, source_target_pairs={{0,8},{8,0},{16,24},{24,16},{1,9},{9,1},{17,25},{25,17},{2,10},{10... | collective-permute-start | bytes 393224 | tf_op jit(solution)/shard_map/ppermute | solution.py:529
  83.4 1.9 %collective-permute-start.18 = (bf16[64,1024]{1,0:T(8,128)(2,1)S(1)}, bf16[64,1024]{1,0:T(8,128)(2,1)S(1)}, u32[]{:S(2)}, u32[]{:S(2)}) collective-permute-start(bf16[64,1024]{1,0:T(8,128)(2,1)S(1)} %get-tuple-element.119), channel_id=1, source_target_pairs={{0,8},{8,0},{16,24},{24,16},{1,9},{9,1},{17,25},{25,17},{2,10},{10... | collective-permute-start | bytes 393224 | tf_op jit(solution)/shard_map/ppermute | solution.py:529
  83.9 1.4 %collective-permute-start.19 = (bf16[64,1024]{1,0:T(8,128)(2,1)S(1)}, bf16[64,1024]{1,0:T(8,128)(2,1)S(1)}, u32[]{:S(2)}, u32[]{:S(2)}) collective-permute-start(bf16[64,1024]{1,0:T(8,128)(2,1)S(1)} %get-tuple-element.120), channel_id=1, source_target_pairs={{0,8},{8,0},{16,24},{24,16},{1,9},{9,1},{17,25},{25,17},{2,10},{10... | collective-permute-start | bytes 393224 | tf_op jit(solution)/shard_map/ppermute | solution.py:529
  84.0 1.5 %collective-permute-start.20 = (bf16[64,1024]{1,0:T(8,128)(2,1)S(1)}, bf16[64,1024]{1,0:T(8,128)(2,1)S(1)}, u32[]{:S(2)}, u32[]{:S(2)}) collective-permute-start(bf16[64,1024]{1,0:T(8,128)(2,1)S(1)} %get-tuple-element.121), channel_id=1, source_target_pairs={{0,8},{8,0},{16,24},{24,16},{1,9},{9,1},{17,25},{25,17},{2,10},{10... | collective-permute-start | bytes 393224 | tf_op jit(solution)/shard_map/ppermute | solution.py:529
  84.7 8.5 %collective-permute-start.13 = (bf16[128,1024]{1,0:T(8,128)(2,1)S(1)}, bf16[128,1024]{1,0:T(8,128)(2,1)S(1)}, u32[]{:S(2)}, u32[]{:S(2)}) collective-permute-start(bf16[128,1024]{1,0:T(8,128)(2,1)S(1)} %get-tuple-element.105), channel_id=1, source_target_pairs={{0,1},{1,0},{2,3},{3,2},{4,5},{5,4},{6,7},{7,6},{8,9},{9,8},{10,11... | collective-permute-start | bytes 786440 | tf_op jit(solution)/shard_map/ppermute | solution.py:529
  88.7 1.4 %collective-permute-start.21 = (bf16[64,1024]{1,0:T(8,128)(2,1)S(1)}, bf16[64,1024]{1,0:T(8,128)(2,1)S(1)}, u32[]{:S(2)}, u32[]{:S(2)}) collective-permute-start(bf16[64,1024]{1,0:T(8,128)(2,1)S(1)} %get-tuple-element.125), channel_id=1, source_target_pairs={{0,8},{8,0},{16,24},{24,16},{1,9},{9,1},{17,25},{25,17},{2,10},{10... | collective-permute-start | bytes 393224 | tf_op jit(solution)/shard_map/ppermute | solution.py:529
  89.1 2.5 %collective-permute-start.22 = (bf16[64,1024]{1,0:T(8,128)(2,1)S(1)}, bf16[64,1024]{1,0:T(8,128)(2,1)S(1)}, u32[]{:S(2)}, u32[]{:S(2)}) collective-permute-start(bf16[64,1024]{1,0:T(8,128)(2,1)S(1)} %get-tuple-element.126), channel_id=1, source_target_pairs={{0,8},{8,0},{16,24},{24,16},{1,9},{9,1},{17,25},{25,17},{2,10},{10... | collective-permute-start | bytes 393224 | tf_op jit(solution)/shard_map/ppermute | solution.py:529
  89.3 2.4 %collective-permute-start.23 = (bf16[64,1024]{1,0:T(8,128)(2,1)S(1)}, bf16[64,1024]{1,0:T(8,128)(2,1)S(1)}, u32[]{:S(2)}, u32[]{:S(2)}) collective-permute-start(bf16[64,1024]{1,0:T(8,128)(2,1)S(1)} %get-tuple-element.127), channel_id=1, source_target_pairs={{0,8},{8,0},{16,24},{24,16},{1,9},{9,1},{17,25},{25,17},{2,10},{10... | collective-permute-start | bytes 393224 | tf_op jit(solution)/shard_map/ppermute | solution.py:529
  89.6 2.0 %collective-permute-start.24 = (bf16[64,1024]{1,0:T(8,128)(2,1)S(1)}, bf16[64,1024]{1,0:T(8,128)(2,1)S(1)}, u32[]{:S(2)}, u32[]{:S(2)}) collective-permute-start(bf16[64,1024]{1,0:T(8,128)(2,1)S(1)} %get-tuple-element.128), channel_id=1, source_target_pairs={{0,8},{8,0},{16,24},{24,16},{1,9},{9,1},{17,25},{25,17},{2,10},{10... | collective-permute-start | bytes 393224 | tf_op jit(solution)/shard_map/ppermute | solution.py:529
  90.1 14.7 %collective-permute-start.26 = (bf16[64,4096]{1,0:T(8,128)(2,1)S(1)}, bf16[64,4096]{1,0:T(8,128)(2,1)S(1)}, u32[]{:S(2)}, u32[]{:S(2)}) collective-permute-start(bf16[64,4096]{1,0:T(8,128)(2,1)S(1)} %get-tuple-element.133), channel_id=1, source_target_pairs={{0,16},{8,24},{16,0},{24,8},{1,17},{9,25},{17,1},{25,9},{2,18},{10... | collective-permute-start | bytes 1572872 | tf_op jit(solution)/shard_map/ppermute | solution.py:534
  92.3 23.2 %collective-permute-start.27 = (bf16[64,4096]{1,0:T(8,128)(2,1)S(1)}, bf16[64,4096]{1,0:T(8,128)(2,1)S(1)}, u32[]{:S(2)}, u32[]{:S(2)}) collective-permute-start(bf16[64,4096]{1,0:T(8,128)(2,1)S(1)} %get-tuple-element.134), channel_id=1, source_target_pairs={{0,16},{8,24},{16,0},{24,8},{1,17},{9,25},{17,1},{25,9},{2,18},{10... | collective-permute-start | bytes 1572872 | tf_op jit(solution)/shard_map/ppermute | solution.py:534
  97.8 20.4 %collective-permute-start.25 = (bf16[128,4096]{1,0:T(8,128)(2,1)S(1)}, bf16[128,4096]{1,0:T(8,128)(2,1)S(1)}, u32[]{:S(2)}, u32[]{:S(2)}) collective-permute-start(bf16[128,4096]{1,0:T(8,128)(2,1)S(1)} %get-tuple-element.132), channel_id=1, source_target_pairs={{0,8},{8,0},{16,24},{24,16},{1,9},{9,1},{17,25},{25,17},{2,10},{10... | collective-permute-start | bytes 3145736 | tf_op jit(solution)/shard_map/ppermute | solution.py:529
  116.2 2.0 %collective-permute-start.28 = (bf16[64,4096]{1,0:T(8,128)(2,1)S(1)}, bf16[64,4096]{1,0:T(8,128)(2,1)S(1)}, u32[]{:S(2)}, u32[]{:S(2)}) collective-permute-start(bf16[64,4096]{1,0:T(8,128)(2,1)S(1)} %get-tuple-element.136), channel_id=1, source_target_pairs={{0,8},{8,0},{16,24},{24,16},{1,9},{9,1},{17,25},{25,17},{2,10},{10... | collective-permute-start | bytes 1572872 | tf_op jit(solution)/shard_map/ppermute | solution.py:529
  (12 other events, 139.2 us)

commit v3 on v2

--- a/solution.py
+++ b/solution.py
@@ -15,7 +15,7 @@
 TAILS = 16
 WIDE = 256
 PIECES = 4
-STATE_ROWS = N + 16
+FACTOR_ROWS = 16
 
 epsilon = 1e-05
 highest = lax.Precision.HIGHEST
@@ -66,15 +66,21 @@
     return jnp.sum(jnp.where(line == flags_ref[at], ids, 0.0), axis=0, keepdims=True)
 
 
-def tail_kernel(flags_ref, own_ref, segments_ref, after_ref, tail_ref):
-    del after_ref
-    tail_ref[...] = own_ref[CH - TAILS : CH]
-    line = lax.broadcasted_iota(jnp.int32, (TAILS, CH), 0)
-    tail_ref[:, 0:CH] = jnp.where(
+def tail_kernel(flags_ref, own_ref, opposite_ref, segments_ref, tail_ref):
+    half = tail_ref.shape[1]
+    own, opposite = (
+        ref[CH - TAILS : CH].astype(f32)[TAILS - TAIL :] for ref in (own_ref, opposite_ref)
+    )
+    line = lax.broadcasted_iota(jnp.int32, own.shape, 0)
+    both = jnp.where(line < TAIL // 2, pltpu.roll(own, TAIL // 2, 0), opposite)
+    line = line[:, 0:CH]
+    labelled = jnp.where(
         line == 0,
         ids_row(flags_ref, segments_ref, 3),
-        own_ref[CH - TAILS : CH, 0:CH].astype(f32),
-    ).astype(bf16)
+        jnp.where(line == TAIL // 2, ids_row(flags_ref, segments_ref, 4), both[:, 0:CH]),
+    )
+    both = jnp.concatenate([labelled, both[:, CH:]], axis=1)
+    tail_ref[...] = jnp.concatenate([both[:, :half], both[:, half:]]).astype(bf16)
 
 
 def facts(rows_ref, s, ids, prior, reach):
@@ -92,13 +98,14 @@
     rows_ref[s] = found
 
 
-def mix_kernel(slots, streams, flip, flags_ref, *refs):
+def mix_kernel(slots, streams, flip, carried, flags_ref, *refs):
     sources, refs = refs[:2], refs[2:]
-    tail_refs, refs = refs[:2], refs[-(12 + slots) :]
-    segments_ref, value_ref, coupling_ref, step_ref, taps_ref, head_ref = refs[:6]
-    refs = refs[6:]
+    tail_ref, refs = refs[0], refs[-15 - carried :]
+    segments_ref, value_ref, coupling_ref, step_ref, *taps_refs, head_ref = refs[:9]
+    refs = refs[9:]
     values_ref, coupled_ref, sums_ref, rows_ref = refs[:4]
-    state_refs, (rows_scr, pad_scr) = refs[4 : 4 + slots], refs[4 + slots :]
+    state_refs, (rows_scr, pad_scr) = refs[4 : 4 + carried], refs[4 + carried :]
+    lines = state_refs[0].shape[0] - FACTOR_ROWS
     odd = flags_ref[0] == 1
     heads = step_ref.shape[0]
     reach = 3
@@ -111,33 +118,34 @@
 
     work = []
     for g in range(groups):
-        work.append((coupling_ref, coupled_ref, width, g))
+        work.append((coupling_ref, coupled_ref, taps_refs[1::2], g))
         for piece in range(share // WIDE):
-            work.append((value_ref, values_ref, 0, g * (share // WIDE) + piece))
+            work.append((value_ref, values_ref, taps_refs[0::2], g * (share // WIDE) + piece))
     fill_rows(rows_scr, sources, flags_ref[1], flip)
     later = flags_ref[2] > 0
-    tails = [ref[...].astype(f32) for ref in tail_refs]
+    tail = jnp.where(later, tail_ref[...].astype(f32), 0.0)
+    tail = jnp.concatenate([tail[0:TAIL], tail[TAIL:TAILS]], axis=1)
+    tails = [pltpu.roll(tail, TAIL // 2, 0), tail]
     if slots == 1:
-        tails = [jnp.where(flags_ref[1] == flip, tails[0], tails[1])]
-    for s, tail in enumerate(tails):
-        tail = jnp.where(later, tail, 0.0)
-        rows_scr[held + TAILS * s : held + TAILS * (s + 1)] = tail.astype(bf16)
-        facts(rows_ref, s, ids_row(flags_ref, segments_ref, streams[s]), tail[0:1, 0:CH], reach)
+        tails = [jnp.where(flags_ref[1] == flip, *tails)] * 2
+    rows_scr[held : held + TAILS] = jnp.concatenate(tails).astype(bf16)
+    for s, tail in enumerate(tails[:slots]):
+        facts(rows_ref, s, ids_row(flags_ref, segments_ref, streams[s]), tail[4:5, 0:CH], reach)
     masks = [turned(rows_ref[s]) for s in range(slots)]
     rows = rows_scr[...]
     step_rows = lax.dot_general(
         step_ref[...], rows_scr[0:held], (((1,), (1,)), ((), ())), preferred_element_type=f32
     )
 
-    def convolved(projected, out_ref, base, at, slot):
+    def convolved(projected, out_ref, taps_and_shift, at, slot):
         projected = projected.astype(bf16).astype(f32)
-        taps = taps_ref[:, base + at * WIDE : base + (at + 1) * WIDE]
+        taps, shift = (ref[:, at * WIDE : (at + 1) * WIDE].astype(f32) for ref in taps_and_shift)
         for s in range(slots):
             body = projected[CH * s : CH * (s + 1)]
-            start = held + TAILS * (s + 1) - TAIL
+            start = held + TAIL * s
             pad_scr[slot, s, 0:TAIL] = projected[start : start + TAIL]
             pad_scr[slot, s, TAIL : TAIL + CH] = body
-            running = taps[reach + 1 : reach + 2] + taps[reach : reach + 1] * body
+            running = shift + taps[reach : reach + 1] * body
             for k in range(reach):
                 window = pad_scr[slot, s, TAIL - reach + k : TAIL - reach + k + CH]
                 running = running + taps[k : k + 1] * window * masks[s][:, k : k + 1]
@@ -147,11 +155,14 @@
     position = lax.broadcasted_iota(jnp.int32, (CH, CH), 1)
     upto = (source <= position).astype(f32)
 
-    def put_states(parts, lines, columns):
-        if slots == 2:
-            parts = [jnp.where(odd, parts[1], parts[0]), jnp.where(odd, parts[0], parts[1])]
-        for ref, part in zip(state_refs, parts):
-            ref[lines, columns] = part.astype(bf16)
+    def put_states(parts, first, columns):
+        if carried == 1:
+            state_refs[0][first : first + parts[0].shape[0], columns] = parts[0].astype(bf16)
+            return
+        given = jnp.where(odd, parts[1], parts[0]).astype(bf16)
+        kept = jnp.where(odd, parts[0], parts[1]).astype(bf16)
+        for ref, part in zip(state_refs, (given, kept)):
+            ref[first : first + part.shape[0], columns] = part
 
     def weighed(s):
         sizes = jax.nn.softplus(
@@ -175,7 +186,7 @@
             turned(jnp.concatenate(spaced_growth, axis=0))[CH - 8 : CH], per_step, count
         )[7:8]
         coarse = leading.astype(bf16).astype(f32)
-        line = lax.broadcasted_iota(jnp.int32, (STATE_ROWS - N, width), 0)
+        line = lax.broadcasted_iota(jnp.int32, (FACTOR_ROWS, width), 0)
         factor = jnp.where(line == 0, coarse, jnp.where(line == 1, leading - coarse, 0.0))
         return turned(jnp.concatenate(spaced_tail, axis=0)), factor
 
@@ -195,20 +206,22 @@
                     keys, weighted, (((0,), (0,)), ((), ())), preferred_element_type=f32
                 )
             )
-        put_states(parts, slice(0, N), own)
+        if slots < carried:
+            parts = [parts[0][:lines], parts[0][lines:]]
+        put_states(parts, 0, own)
 
     weights = [weighed(s) for s in range(slots)]
-    put_states([w[1] for w in weights], slice(N, STATE_ROWS), slice(0, width))
+    put_states([weights[0][1], weights[-1][1]], lines, slice(0, width))
     per_group = len(work) // groups
     waiting = None
     for i in range(len(work) + 1):
         following = None
         if i < len(work):
-            weight_ref, out_ref, base, at = work[i]
+            weight_ref, out_ref, taps_and_shift, at = work[i]
             following = (
                 dot(rows, weight_ref[:, at * WIDE : (at + 1) * WIDE]),
                 out_ref,
-                base,
+                taps_and_shift,
                 at,
                 i % 2,
             )
@@ -281,25 +294,23 @@
             gates_ref[s, :, own] = projected[s * CH : (s + 1) * CH]
 
 
-def unpacked(state, tail):
-    tail = tail.astype(f32)
-    return state.astype(f32), tail[0:1] + tail[1:2]
+def unpacked(block):
+    tail = block[block.shape[0] - FACTOR_ROWS :]
+    return block[: block.shape[0] - FACTOR_ROWS], tail[0:1] + tail[1:2]
 
 
 def paired(odd, mine_ref, got_ref):
-    lines = (slice(0, N), slice(N, STATE_ROWS))
-    mine, got = [[ref[line] for line in lines] for ref in (mine_ref, got_ref)]
-    even = [jnp.where(odd, g.astype(f32), m.astype(f32)) for m, g in zip(mine, got)]
-    later = [jnp.where(odd, m.astype(f32), g.astype(f32)) for m, g in zip(mine, got)]
-    return unpacked(*even), unpacked(*later)
+    mine, got = mine_ref[...].astype(f32), got_ref[...].astype(f32)
+    return unpacked(jnp.where(odd, got, mine)), unpacked(jnp.where(odd, mine, got))
 
 
 def put_packed(out_ref, state, factor):
-    out_ref[0:N] = state.astype(bf16)
-    if out_ref.shape[0] > N:
+    lines = state.shape[0]
+    out_ref[0:lines] = state.astype(bf16)
+    if out_ref.shape[0] > lines:
         coarse = factor.astype(bf16).astype(f32)
-        line = lax.broadcasted_iota(jnp.int32, (STATE_ROWS - N, state.shape[1]), 0)
-        out_ref[N:STATE_ROWS] = jnp.where(
+        line = lax.broadcasted_iota(jnp.int32, (FACTOR_ROWS, state.shape[1]), 0)
+        out_ref[lines : lines + FACTOR_ROWS] = jnp.where(
             line == 0, coarse, jnp.where(line == 1, factor - coarse, 0.0)
         ).astype(bf16)
 
@@ -310,27 +321,24 @@
 
 
 def chain_kernel(distance, flags_ref, mine_ref, got_ref, out_ref):
-    state, factor = unpacked(mine_ref[0:N], mine_ref[N:STATE_ROWS])
-    earlier, leading = unpacked(got_ref[0:N], got_ref[N:STATE_ROWS])
+    state, factor = unpacked(mine_ref[...].astype(f32))
+    earlier, leading = unpacked(got_ref[...].astype(f32))
     reached = jnp.where(flags_ref[2] >= distance, factor, 0.0)
     put_packed(out_ref, state + reached * earlier, reached * leading)
 
 
-def entered(flags_ref, mine_ref, got_ref, before_ref):
-    even, _ = paired(flags_ref[0] == 1, mine_ref, got_ref)
+def finish_kernel(flags_ref, mine_ref, got_ref, before_ref, own_ref, *other_refs):
+    odd = flags_ref[0] == 1
+    even, _ = paired(odd, mine_ref, got_ref)
     before = jnp.where(flags_ref[2] >= 2, before_ref[...].astype(f32), 0.0)
-    return before, even[0] + even[1] * before
-
-
-def finish_kernel(flags_ref, mine_ref, got_ref, before_ref, own_ref, other_ref):
-    odd = flags_ref[0] == 1
-    before, between = entered(flags_ref, mine_ref, got_ref, before_ref)
+    between = even[0] + even[1] * before
     own_ref[...] = jnp.where(odd, between, before).astype(bf16)
-    other_ref[...] = jnp.where(odd, before, between).astype(bf16)
-
-
-def out_kernel(slots, blocks, flags_ref, *refs):
-    entry_refs, refs = refs[: 4 - slots], refs[4 - slots :]
+    for other_ref in other_refs:
+        other_ref[...] = jnp.where(odd, before, between).astype(bf16)
+
+
+def out_kernel(slots, blocks, carried, flags_ref, *refs):
+    entry_refs, refs = refs[:carried], refs[carried:]
     (
         local_ref,
         gates_ref,
@@ -339,22 +347,26 @@
         rows_ref,
         gain_ref,
         out_ref,
+        *refs,
+    ) = refs
+    pieces = 1 if slots == 2 else PIECES
+    (
         first_ref,
         *second_refs,
         normed_scr,
-    ) = refs
+    ) = refs[-(2 + pieces) :]
     wide = out_ref.shape[1] // blocks
     odd = flags_ref[0] == 1
     groups = coupled_ref.shape[2] // (2 * N)
     share = local_ref.shape[2] // groups
     count = sums_ref.shape[1]
     per_step = WIDE // P_SIZE
-    if slots == 1:
-        before, between = entered(flags_ref, *entry_refs)
-        entries = [jnp.where(odd, between, before).astype(bf16)]
-    else:
+    entries = [entry_refs[0][...]]
+    if carried == 2:
         own, other = [ref[...].astype(f32) for ref in entry_refs]
-        entries = [jnp.where(odd, own, other).astype(bf16), jnp.where(odd, other, own).astype(bf16)]
+        entries = [jnp.where(odd, a, b).astype(bf16) for a, b in ((own, other), (other, own))]
+        if slots == 1:
+            entries = [jnp.concatenate(entries)]
     for s in range(slots):
         sums = jnp.concatenate([sums_ref[s, jj] for jj in range(count)], axis=0)
         line = lax.broadcasted_iota(jnp.int32, sums.shape, 0) % 8
@@ -393,9 +405,9 @@
     return sum(ref[...].astype(f32) for ref in refs)
 
 
-def add_kernel(flags_ref, mine_ref, *refs):
+def add_kernel(pieces, flags_ref, mine_ref, *refs):
     del flags_ref
-    *other_refs, out_ref = refs
+    other_refs, out_ref = refs[:pieces], refs[-1]
     wide = out_ref.shape[1] // len(other_refs)
     for j, ref in enumerate(other_refs):
         own = slice(j * wide, (j + 1) * wide)
@@ -473,20 +485,20 @@
     return jax.ShapeDtypeStruct(sizes, dtype)
 
 
-def mix(run, slots, streams, flip, sources, tails, segments, weights, small):
+def mix(run, slots, streams, flip, carried, sources, tails, segments, weights, small):
     value_weight, coupling_weight = weights
-    width, narrow, depth = value_weight.shape[1], coupling_weight.shape[1], tails[0].shape[1]
+    width, narrow, depth = value_weight.shape[1], coupling_weight.shape[1], value_weight.shape[0]
     shapes = [
         shape(bf16, slots, CH, width),
         shape(bf16, slots, CH, narrow),
         shape(f32, slots, narrow // N, 8, CH),
         shape(f32, slots, 8, CH),
-    ] + [shape(bf16, STATE_ROWS, width)] * slots
+    ] + [shape(bf16, N * slots // carried + FACTOR_ROWS, width)] * carried
     scratch = [
-        pltpu.VMEM((slots * (CH + TAILS), depth), bf16),
+        pltpu.VMEM((slots * CH + TAILS, depth), bf16),
         pltpu.VMEM((2, slots, CH + TAIL, WIDE), f32),
     ]
-    kernel = functools.partial(mix_kernel, slots, streams, flip)
+    kernel = functools.partial(mix_kernel, slots, streams, flip, carried)
     operands = (*sources, *tails, segments, *weights, *small)
     return run(kernel, f"mix{slots}", shapes, scratch, *operands, mib=8, us=4 * slots)
 
@@ -496,15 +508,15 @@
     scratch = [pltpu.VMEM((slots * CH, gate_weight.shape[0]), bf16)]
     kernel = functools.partial(scan_kernel, slots, flip)
     operands = (*sources, rows, gate_weight, values, coupled, sums, skip)
-    return run(kernel, f"scan{slots}", shapes, scratch, *operands, mib=6, us=2 * slots)
-
-
-def project_out(run, slots, entries, local, gates, coupled, sums, rows, gain, out_weight):
+    return run(kernel, f"scan{slots}", shapes, scratch, *operands, mib=6, us=0.1)
+
+
+def project_out(run, slots, entries, local, gates, coupled, sums, rows, gain, out_weight, *waits):
     width, depth = out_weight.shape
     lines = CH if slots == 2 else HALF
     scratch = [pltpu.VMEM((slots * CH, width), bf16)]
-    kernel = functools.partial(out_kernel, slots, 8)
-    operands = (*entries, local, gates, coupled, sums, rows, gain, out_weight)
+    kernel = functools.partial(out_kernel, slots, 8, len(entries))
+    operands = (*entries, local, gates, coupled, sums, rows, gain, out_weight, *waits)
     pieces = 1 if slots == 2 else PIECES
     shapes = [shape(bf16, lines, depth)] + [shape(bf16, lines, depth // pieces)] * pieces
     return run(kernel, f"out{slots}", shapes, scratch, *operands, mib=6, us=0.1)
@@ -515,10 +527,10 @@
     return lax.ppermute(block, "ctx", [(i, (i + distance) % spans) for i in range(spans)])
 
 
-def tail_from(block, chips_on, flip):
+def tail_from(block, chips_on):
     places, spans = lax.axis_size("fsdp"), lax.axis_size("ctx")
     route = [
-        (((f + 2 * chips_on) % places ^ flip) * spans + c, f * spans + (c + 1) % spans)
+        ((f + 2 * chips_on) % places * spans + c, f * spans + (c + 1) % spans)
         for f in range(places)
         for c in range(spans)
     ]
@@ -539,15 +551,22 @@
 
 
 def chained(run, block):
-    spans, width = lax.axis_size("ctx"), block.shape[1]
+    spans = lax.axis_size("ctx")
+    lines, width = block.shape
     distance = 2
     while distance < spans // 2:
         last = 2 * distance >= spans // 2
-        out = [shape(bf16, N if last else STATE_ROWS, width)]
+        out = [shape(bf16, lines - FACTOR_ROWS if last else lines, width)]
         kernel = functools.partial(chain_kernel, distance)
         block = run(kernel, "chain", out, [], block, along(block, distance), us=0.1)[0]
         distance *= 2
     return block
+
+
+def finished(run, kept, got, before, carried):
+    out = [shape(bf16, *before.shape)] * carried
+    own, *others = run(finish_kernel, "finish", out, [], kept, got, before, us=0.1)
+    return own, *[partner(other, "ctx") for other in others]
 
 
 def on_device(
@@ -572,7 +591,6 @@
     span = lax.axis_index("ctx")
     chips = lax.axis_size("fsdp") // 2
     chip, core = place // 2, place % 2
-    reach = value_conv.shape[0] - 1
     own = tokens[0]
     phases = [(d, j) for d in range(1, chips) for j in range(2)]
     far_streams = [(chip + d) % chips * 2 + j for d, j in phases]
@@ -584,24 +602,22 @@
     arrived = {d: over(own, -d) for d in range(1, chips)}
     opposite = partner(own, "fsdp")
     half_shape = shape(bf16, HALF, own.shape[1])
-    tail_shape = shape(bf16, TAILS, own.shape[1])
-    tail = run(tail_kernel, "tail", [tail_shape], [], own, segments, opposite, us=8)[0]
+    tail_shape = shape(bf16, TAILS, own.shape[1] // 2)
+    tail = run(tail_kernel, "tail", [tail_shape], [], own, opposite, segments, us=8)[0]
 
     heads = step_weight.shape[1]
     head = jnp.broadcast_to(jnp.stack([step_bias, decay_log])[:, :, None], (2, heads, CH))
     skip = skip_gain[None]
-    taps = jnp.concatenate([value_conv, coupling_conv], axis=1).astype(f32)
-    shifts = jnp.concatenate([value_shift, coupling_shift])[None]
-    taps = jnp.concatenate([taps, shifts, jnp.zeros((4 - reach, taps.shape[1]), f32)], axis=0)
-    small = (step_weight.T, taps, head)
+    shifts = (value_shift[None], coupling_shift[None])
+    small = (step_weight.T, value_conv, coupling_conv, *shifts, head)
     gain = norm_gain[None]
 
     weights = (value_weight, coupling_weight)
-    near = [tail_from(tail, 0, flip) for flip in range(2)]
-    far = {d: [tail_from(tail, d, flip) for flip in range(2)] for d in range(1, chips)}
+    near = tail_from(tail, 0)
+    far = [tail_from(tail, d) for d in range(1, chips)]
     near_sources = (own, opposite)
-    values, coupled, near_sums, near_rows, given, kept = mix(
-        run, 2, (3, 4), None, near_sources, near + sum(far.values(), []), segments, weights, small
+    values, coupled, near_sums, near_rows, given, near_kept = mix(
+        run, 2, (3, 4), None, 2, near_sources, [near, *far], segments, weights, small
     )
     near_mixed = (values, coupled, near_sums)
     near_got = partner(given, "ctx")
@@ -611,44 +627,58 @@
         if j == 0:
             arrival = sequence.held(arrived[d])
             sources = (arrival, partner(arrival, "fsdp"))
-        *mixed, state = mix(run, 1, (5 + i,), j, sources, far[d], segments, weights, small)
-        far_mixed.append((sources, *mixed, state, partner(state, "ctx")))
+        carried = 1
+        mixed = mix(
+            run, 1, (5 + i,), j, carried, sources, far[d - 1 : d], segments, weights, small
+        )
+        given, kept = mixed[4], mixed[-1]
+        far_mixed.append((sources, *mixed[:4], kept, partner(given, "ctx"), carried))
         if i == 0:
-            near_block = joined(run, kept, near_got)
-
-    far_scans, blocks = [], []
-    for (d, j), (sources, values, coupled, sums, rows, state, got) in zip(phases, far_mixed):
-        blocks.append(joined(run, state, got))
+            near_block = joined(run, near_kept, near_got)
+
+    far_scans, blocks, befores = [], [], []
+    for i, ((d, j), far_one) in enumerate(zip(phases, far_mixed)):
+        sources, values, coupled, sums, rows, kept, got, _ = far_one
+        blocks.append(joined(run, kept, got))
+        if i == 0:
+            near_before = along(chained(run, near_block), 2)
+        if i == 1:
+            befores.append(along(chained(run, blocks[0]), 2))
         far_scans.append(
             scan(run, 1, j, sources, rows, gate_weight, values, coupled, sums, skip)
         )
-        if len(blocks) == 1:
-            near_before = along(chained(run, near_block), 2)
-    near_gates, near_local = scan(
-        run, 2, None, near_sources, near_rows, gate_weight, *near_mixed, skip
-    )
-    entry_shape = shape(bf16, N, kept.shape[1])
-    befores = []
-    for block in blocks:
-        befores.append(along(chained(run, block), 2))
-        if len(befores) == 1:
-            entry, other_entry = run(
-                finish_kernel, "finish", [entry_shape] * 2, [], kept, near_got, near_before, us=0.1
+
+    back, latest = {}, ()
+    for i, ((d, j), (gates, local), far_one) in enumerate(zip(phases, far_scans, far_mixed)):
+        _, _, coupled, sums, rows, kept, got, carried = far_one
+        entries = finished(run, kept, got, befores[i], carried)
+        mine, *pieces = project_out(
+            run,
+            1,
+            entries,
+            local,
+            gates,
+            coupled,
+            sums,
+            rows,
+            gain,
+            out_weight,
+            *(near_entries[1:] if i == 1 else ()),
+        )
+        pieces = [partner(piece, "fsdp") for piece in pieces]
+        if i == 0:
+            near_entries = finished(run, near_kept, near_got, near_before, 2)
+        kernel = functools.partial(add_kernel, len(pieces))
+        total = run(kernel, "add", [half_shape], [], mine, *pieces, *latest, us=0.1)[0]
+        back[d, j] = over(total, d)
+        latest = (back[d, j],)
+        if i == 0:
+            befores += [along(chained(run, block), 2) for block in blocks[1:]]
+            near_gates, near_local = scan(
+                run, 2, None, near_sources, near_rows, gate_weight, *near_mixed, skip
             )
-    near_entries = (entry, partner(other_entry, "ctx"))
-
-    back = {}
-    for (d, j), before, (gates, local), (_, _, coupled, sums, rows, state, got) in zip(
-        phases, befores, far_scans, far_mixed
-    ):
-        mine, *others = project_out(
-            run, 1, (state, got, before), local, gates, coupled, sums, rows, gain, out_weight
-        )
-        others = [partner(piece, "fsdp") for piece in others]
-        total = run(add_kernel, "add", [half_shape], [], mine, *others, us=0.1)[0]
-        back[d, j] = over(total, d)
-
-    mine, others = project_out(
+
+    near_mine, near_others = project_out(
         run,
         2,
         near_entries,
@@ -660,7 +690,7 @@
         gain,
         out_weight,
     )
-    others = partner(others, "fsdp")
+    near_others = partner(near_others, "fsdp")
     returned = [back[d, j] for j in range(2) for d in range(1, chips)]
     given = run(give_kernel, "give", [half_shape], [], *returned, us=0.1)[0]
     return run(
@@ -669,8 +699,8 @@
         [shape(bf16, *own.shape)],
         [],
         own,
-        mine,
-        others,
+        near_mine,
+        near_others,
         partner(given, "fsdp"),
         *returned,
         mib=4,

time: 121 us -> 114 us (0.942)
  starting transfers between devices: 28 us -> 23.5 us
  other arithmetic: 1.51 us -> 0.01 us
    ppermute x6, waiting for transfers between devices: 9.86 us -> 16.9 us  [along(): lax.ppermute(block, 'ctx', [(i, (i + distance) % spans) for i in range(sp...]
    ppermute x3, waiting for transfers between devices: 18.6 us -> 13.5 us  [over(): lax.ppermute(block, 'fsdp', [(i, (i + 2 * distance) % size) for i in rang...]
    ppermute x4 -> x2, waiting for transfers between devices: 10.3 us -> 5.42 us  [tail_from(): return lax.ppermute(block, ('fsdp', 'ctx'), route)]
    ppermute x6, starting transfers between devices: 8.26 us -> 5.48 us  [along(): lax.ppermute(block, 'ctx', [(i, (i + distance) % spans) for i in range(sp...]
    ppermute x16, waiting for transfers between devices: 3.43 us -> 5.14 us  [partner(): lax.ppermute(block, axis, [(i, i ^ 1) for i in range(lax.axis_size(axis))])]
    ppermute x4 -> x2, starting transfers between devices: 6.47 us -> 5.31 us  [tail_from(): return lax.ppermute(block, ('fsdp', 'ctx'), route)]
    pallas_call x21 -> x23, Pallas kernels: 45.5 us -> 46.5 us  [run(): pl.pallas_call(ordered, in_specs=[IN_SMEM] * (1 + len(scalars)) + [IN_VME...]
  transfers between devices with their start and end apart: 29 -> 27, of which waited for: 15 -> 18; matrix products, arithmetic and copies ran while one was open for 1% -> 0% of each run, Pallas kernels for 36% -> 38%
where the time goes in v3:
time: 114 us
  Pallas kernels  46.5 us (41%)
  waiting for transfers between devices  41 us (36%)
  starting transfers between devices  23.5 us (21%)
  local copies, waits for them, and re-layouts  2.15 us (2%)
    pallas_call x23, Pallas kernels, run(): pl.pallas_call(ordered, in_specs=[IN_SMEM] * (1 + len(scalars)) + [IN_VME...  46.5 us
    ppermute x6, waiting for transfers between devices, along(): lax.ppermute(block, 'ctx', [(i, (i + distance) % spans) for i in range(sp...  16.9 us
    ppermute x3, waiting for transfers between devices, over(): lax.ppermute(block, 'fsdp', [(i, (i + 2 * distance) % size) for i in rang...  13.5 us
    ppermute x16, starting transfers between devices, partner(): lax.ppermute(block, axis, [(i, i ^ 1) for i in range(lax.axis_size(axis))])  8.02 us
    ppermute x6, starting transfers between devices, along(): lax.ppermute(block, 'ctx', [(i, (i + distance) % spans) for i in range(sp...  5.48 us
    ppermute x2, waiting for transfers between devices, tail_from(): return lax.ppermute(block, ('fsdp', 'ctx'), route)  5.42 us
    ppermute x2, starting transfers between devices, tail_from(): return lax.ppermute(block, ('fsdp', 'ctx'), route)  5.31 us
    ppermute x16, waiting for transfers between devices, partner(): lax.ppermute(block, axis, [(i, i ^ 1) for i in range(lax.axis_size(axis))])  5.14 us
  transfers between devices with their start and end apart: 27, of which 18 were waited for; matrix products, arithmetic and copies ran while one was open for 0% of the time, Pallas kernels for 38%

profile of v3, /device:TPU:0, one launch (start us, length us, event | category | flops | bytes accessed | tf_op | source)
XLA Modules:
  0.0 114.2 jit_solution(16346184586263120640)
XLA Ops:
  0.5 2.5 %collective-permute-start.4 = (bf16[128,4096]{1,0:T(8,128)(2,1)}, bf16[128,4096]{1,0:T(8,128)(2,1)S(1)}, u32[]{:S(2)}, u32[]{:S(2)}) collective-permute-start(bf16[128,4096]{1,0:T(8,128)(2,1)} %bitcast.21), channel_id=1, source_target_pairs={{0,16},{8,24},{16,0},{24,8},{1,17},{9,25},{17,1},{25,9},{2,18},{10... | collective-permute-start | bytes 3145736 | tf_op jit(solution)/shard_map/ppermute | solution.py:546
  3.1 1.2 %copy-done = bf16[1,128,4096]{2,1,0:T(8,128)(2,1)S(1)} copy-done((bf16[1,128,4096]{2,1,0:T(8,128)(2,1)S(1)}, bf16[1,128,4096]{2,1,0:T(8,128)(2,1)}, u32[]{:S(2)}) %copy-start) | copy-done | bytes 1048600
  5.6 2.8 %collective-permute-start.1 = (bf16[16,2048]{1,0:T(8,128)(2,1)S(1)}, bf16[16,2048]{1,0:T(8,128)(2,1)S(1)}, u32[]{:S(2)}, u32[]{:S(2)}) collective-permute-start(bf16[16,2048]{1,0:T(8,128)(2,1)S(1)} %get-tuple-element.76), channel_id=1, source_target_pairs={{0,1},{1,2},{2,3},{3,4},{4,5},{5,6},{6,7},{7,0},{8,9},{9,10},{10,1... | collective-permute-start | bytes 196616 | tf_op jit(solution)/shard_map/ppermute | solution.py:537
  8.4 2.5 %collective-permute-start.2 = (bf16[16,2048]{1,0:T(8,128)(2,1)S(1)}, bf16[16,2048]{1,0:T(8,128)(2,1)S(1)}, u32[]{:S(2)}, u32[]{:S(2)}) collective-permute-start(bf16[16,2048]{1,0:T(8,128)(2,1)S(1)} %get-tuple-element.76), channel_id=1, source_target_pairs={{16,1},{17,2},{18,3},{19,4},{20,5},{21,6},{22,7},{23,0},{24,9},{25... | collective-permute-start | bytes 196616 | tf_op jit(solution)/shard_map/ppermute | solution.py:537
  11.0 2.9 %collective-permute-done.1.refs_3_ = bf16[16,2048]{1,0:T(8,128)(2,1)S(1)} collective-permute-done((bf16[16,2048]{1,0:T(8,128)(2,1)S(1)}, bf16[16,2048]{1,0:T(8,128)(2,1)S(1)}, u32[]{:S(2)}, u32[]{:S(2)}) %collective-permute-start.1) | collective-permute-done | bytes 65568 | tf_op jit(solution)/shard_map/ppermute | solution.py:537
  13.9 2.5 %collective-permute-done.2.refs_4_.refs_3_ = bf16[16,2048]{1,0:T(8,128)(2,1)S(1)} collective-permute-done((bf16[16,2048]{1,0:T(8,128)(2,1)S(1)}, bf16[16,2048]{1,0:T(8,128)(2,1)S(1)}, u32[]{:S(2)}, u32[]{:S(2)}) %collective-permute-start.2) | collective-permute-done | bytes 65568 | tf_op jit(solution)/shard_map/ppermute | solution.py:537
  16.5 7.4 %mix2.1 = (bf16[2,128,1024]{2,1,0:T(8,128)(2,1)S(1)}, bf16[2,128,512]{2,1,0:T(8,128)(2,1)S(1)}, f32[2,4,8,128]{3,2,1,0:T(8,128)S(1)}, f32[2,8,128]{2,1,0:T(8,128...) custom-call(s32[7]{0:T(128)S(1)} %stack.40.refs_0_, ...), custom_call_target="tpu_custom_call" | custom-call | flops 9200000000 | tf_op jit(solution)/shard_map/mix2/pallas_call | solution.py:455
  23.9 4.5 %collective-permute-done.4.block_ref = bf16[128,4096]{1,0:T(8,128)(2,1)S(1)} collective-permute-done((bf16[128,4096]{1,0:T(8,128)(2,1)}, bf16[128,4096]{1,0:T(8,128)(2,1)S(1)}, u32[]{:S(2)}, u32[]{:S(2)}) %collective-permute-start.4) | collective-permute-done | bytes 1048608 | tf_op jit(solution)/shard_map/ppermute | solution.py:546
  28.4 1.7 %collective-permute-start.3 = (bf16[144,1024]{1,0:T(8,128)(2,1)S(1)}, bf16[144,1024]{1,0:T(8,128)(2,1)S(1)}, u32[]{:S(2)}, u32[]{:S(2)}) collective-permute-start(bf16[144,1024]{1,0:T(8,128)(2,1)S(1)} %get-tuple-element.79), channel_id=1, source_target_pairs={{0,1},{1,0},{2,3},{3,2},{4,5},{5,4},{6,7},{7,6},{8,9},{9,8},{10,11... | collective-permute-start | bytes 884744 | tf_op jit(solution)/shard_map/ppermute | solution.py:541
  30.1 0.9 collective-permute-done.5.refs_2_
  31.1 4.5 %mix1.2 = (bf16[1,128,1024]{2,1,0:T(8,128)(2,1)S(1)}, bf16[1,128,512]{2,1,0:T(8,128)(2,1)S(1)}, f32[1,4,8,128]{3,2,1,0:T(8,128)S(1)}, f32[1,8,128]{2,1,0:T(8,128...) custom-call(s32[7]{0:T(128)S(1)} %stack.40.refs_0_, bf16[128,4096]{1,0:T(8,128)(2,1)S(1)} %hold.1.refs_1_, ...), custom_call_target="tpu_custom_call" | custom-call | flops 4600000000 | tf_op jit(solution)/shard_map/mix1/pallas_call | solution.py:455
  35.6 1.8 %collective-permute-start.7 = (bf16[144,1024]{1,0:T(8,128)(2,1)S(1)}, bf16[144,1024]{1,0:T(8,128)(2,1)S(1)}, u32[]{:S(2)}, u32[]{:S(2)}) collective-permute-start(bf16[144,1024]{1,0:T(8,128)(2,1)S(1)} %get-tuple-element.83.refs_1_), channel_id=1, source_target_pairs={{0,1},{1,0},{2,3},{3,2},{4,5},{5,4},{6,7},{7,6},{8,9},{9,8},{10,11... | collective-permute-start | bytes 884744 | tf_op jit(solution)/shard_map/ppermute | solution.py:541
  38.5 1.9 %collective-permute-start.6 = (bf16[144,1024]{1,0:T(8,128)(2,1)S(1)}, bf16[144,1024]{1,0:T(8,128)(2,1)S(1)}, u32[]{:S(2)}, u32[]{:S(2)}) collective-permute-start(bf16[144,1024]{1,0:T(8,128)(2,1)S(1)} %get-tuple-element.82.refs_1_), channel_id=1, source_target_pairs={{0,2},{1,3},{2,4},{3,5},{4,6},{5,7},{6,0},{7,1},{8,10},{9,11},{10,... | collective-permute-start | bytes 884744 | tf_op jit(solution)/shard_map/ppermute | solution.py:527
  40.4 4.7 %mix1.3 = (bf16[1,128,1024]{2,1,0:T(8,128)(2,1)S(1)}, bf16[1,128,512]{2,1,0:T(8,128)(2,1)S(1)}, f32[1,4,8,128]{3,2,1,0:T(8,128)S(1)}, f32[1,8,128]{2,1,0:T(8,128...) custom-call(s32[7]{0:T(128)S(1)} %stack.40.refs_0_, bf16[128,4096]{1,0:T(8,128)(2,1)S(1)} %hold.1.refs_1_, ...), custom_call_target="tpu_custom_call" | custom-call | flops 4600000000 | tf_op jit(solution)/shard_map/mix1/pallas_call | solution.py:455
  45.1 1.6 %collective-permute-start.10 = (bf16[144,1024]{1,0:T(8,128)(2,1)S(1)}, bf16[144,1024]{1,0:T(8,128)(2,1)S(1)}, u32[]{:S(2)}, u32[]{:S(2)}) collective-permute-start(bf16[144,1024]{1,0:T(8,128)(2,1)S(1)} %get-tuple-element.89.refs_1_), channel_id=1, source_target_pairs={{0,1},{1,0},{2,3},{3,2},{4,5},{5,4},{6,7},{7,6},{8,9},{9,8},{10,11... | collective-permute-start | bytes 884744 | tf_op jit(solution)/shard_map/ppermute | solution.py:541
  47.3 1.6 %collective-permute-start.9 = (bf16[144,1024]{1,0:T(8,128)(2,1)S(1)}, bf16[144,1024]{1,0:T(8,128)(2,1)S(1)}, u32[]{:S(2)}, u32[]{:S(2)}) collective-permute-start(bf16[144,1024]{1,0:T(8,128)(2,1)S(1)} %get-tuple-element.88.refs_1_), channel_id=1, source_target_pairs={{0,2},{1,3},{2,4},{3,5},{4,6},{5,7},{6,0},{7,1},{8,10},{9,11},{10,... | collective-permute-start | bytes 884744 | tf_op jit(solution)/shard_map/ppermute | solution.py:527
  50.0 2.6 %scan1.2 = (bf16[1,128,1024]{2,1,0:T(8,128)(2,1)S(1)}, f32[1,128,1024]{2,1,0:T(8,128)S(1)}, f32[8,128]{1,0:T(8,128)S(1)}) custom-call(s32[7]{0:T(128)S(1)} %stack.40.refs_0_, bf16[128,4096]{1,0:T(8,128)(2,1)S(1)} %hold.1.refs_1_, bf16[128,4096]{1,0:T(8,128)(2,1)S(1)} %collective-permute-done.5.refs_2_, f32[1,8,128]{2,1,0:T(8,128)S(1)} %get-tuple-element.90.refs_3_.refs_6_, ...), custom_call_target="tpu_custom_call" | custom-call | flops 115000000 | tf_op jit(solution)/shard_map/scan1/pallas_call | solution.py:455
  52.6 0.9 collective-permute-done.10.refs_2_
  54.2 3.1 %collective-permute-done.9.refs_2_ = bf16[144,1024]{1,0:T(8,128)(2,1)S(1)} collective-permute-done((bf16[144,1024]{1,0:T(8,128)(2,1)S(1)}, bf16[144,1024]{1,0:T(8,128)(2,1)S(1)}, u32[]{:S(2)}, u32[]{:S(2)}) %collective-permute-start.9) | collective-permute-done | bytes 294944 | tf_op jit(solution)/shard_map/ppermute | solution.py:527
  58.0 1.3 %collective-permute-start.8 = (bf16[128,1024]{1,0:T(8,128)(2,1)S(1)}, bf16[128,1024]{1,0:T(8,128)(2,1)S(1)}, u32[]{:S(2)}, u32[]{:S(2)}) collective-permute-start(bf16[128,1024]{1,0:T(8,128)(2,1)S(1)} %get-tuple-element.87), channel_id=1, source_target_pairs={{0,2},{1,3},{2,4},{3,5},{4,6},{5,7},{6,0},{7,1},{8,10},{9,11},{10,... | collective-permute-start | bytes 786440 | tf_op jit(solution)/shard_map/ppermute | solution.py:527
  59.6 2.6 %scan1.3 = (bf16[1,128,1024]{2,1,0:T(8,128)(2,1)S(1)}, f32[1,128,1024]{2,1,0:T(8,128)S(1)}, f32[8,128]{1,0:T(8,128)S(1)}) custom-call(s32[7]{0:T(128)S(1)} %stack.40.refs_0_, bf16[128,4096]{1,0:T(8,128)(2,1)S(1)} %hold.1.refs_1_, bf16[128,4096]{1,0:T(8,128)(2,1)S(1)} %collective-permute-done.5.refs_2_, f32[1,8,128]{2,1,0:T(8,128)S(1)} %get-tuple-element.98.refs_3_.refs_6_, ...), custom_call_target="tpu_custom_call" | custom-call | flops 115000000 | tf_op jit(solution)/shard_map/scan1/pallas_call | solution.py:455
  62.3 6.7 %collective-permute-done.11.refs_3_ = bf16[128,1024]{1,0:T(8,128)(2,1)S(1)} collective-permute-done((bf16[128,1024]{1,0:T(8,128)(2,1)S(1)}, bf16[128,1024]{1,0:T(8,128)(2,1)S(1)}, u32[]{:S(2)}, u32[]{:S(2)}) %collective-permute-start.11) | collective-permute-done | bytes 262176 | tf_op jit(solution)/shard_map/ppermute | solution.py:527
  69.7 2.6 %out1.2 = (bf16[64,4096]{1,0:T(8,128)(2,1)S(1)}, bf16[64,1024]{1,0:T(8,128)(2,1)S(1)}, bf16[64,1024]{1,0:T(8,128)(2,1)S(1)}, bf16[64,1024]{1,0:T(8,128)(2,1)S(1)...) custom-call(s32[7]{0:T(128)S(1)} %stack.40.refs_0_, bf16[128,1024]{1,0:T(8,128)(2,1)S(1)} %get-tuple-element.104.refs_1_, ...), custom_call_target="tpu_custom_call" | custom-call | flops 115000000 | tf_op jit(solution)/shard_map/out1/pallas_call | solution.py:455
  73.0 1.6 %collective-permute-done.8.refs_3_ = bf16[128,1024]{1,0:T(8,128)(2,1)S(1)} collective-permute-done((bf16[128,1024]{1,0:T(8,128)(2,1)S(1)}, bf16[128,1024]{1,0:T(8,128)(2,1)S(1)}, u32[]{:S(2)}, u32[]{:S(2)}) %collective-permute-start.8) | collective-permute-done | bytes 262176 | tf_op jit(solution)/shard_map/ppermute | solution.py:527
  76.6 1.6 %collective-permute-start.23 = (bf16[64,4096]{1,0:T(8,128)(2,1)S(1)}, bf16[64,4096]{1,0:T(8,128)(2,1)S(1)}, u32[]{:S(2)}, u32[]{:S(2)}) collective-permute-start(bf16[64,4096]{1,0:T(8,128)(2,1)S(1)} %get-tuple-element.137), channel_id=1, source_target_pairs={{0,16},{8,24},{16,0},{24,8},{1,17},{9,25},{17,1},{25,9},{2,18},{10... | collective-permute-start | bytes 1572872 | tf_op jit(solution)/shard_map/ppermute | solution.py:546
  79.7 4.0 %scan2.1 = (bf16[2,128,1024]{2,1,0:T(8,128)(2,1)S(1)}, f32[2,128,1024]{2,1,0:T(8,128)S(1)}, f32[8,128]{1,0:T(8,128)S(1)}) custom-call(s32[7]{0:T(128)S(1)} %stack.40.refs_0_, bf16[128,4096]{1,0:T(8,128)(2,1)S(1)} %bitcast.24, bf16[128,4096]{1,0:T(8,128)(2,1)S(1)} %collective-permute-done.refs_2_, f32[2,8,128]{2,1,0:T(8,128)S(1)} %get-tuple-element.111.refs_3_.refs_7_, ...), custom_call_target="tpu_custom_call" | custom-call | flops 115000000 | tf_op jit(solution)/shard_map/scan2/pallas_call | solution.py:455
  83.8 5.2 %collective-permute-done.18.refs_3_ = bf16[128,1024]{1,0:T(8,128)(2,1)S(1)} collective-permute-done((bf16[128,1024]{1,0:T(8,128)(2,1)S(1)}, bf16[128,1024]{1,0:T(8,128)(2,1)S(1)}, u32[]{:S(2)}, u32[]{:S(2)}) %collective-permute-start.18) | collective-permute-done | bytes 262176 | tf_op jit(solution)/shard_map/ppermute | solution.py:527
  89.7 2.6 %out1.3 = (bf16[64,4096]{1,0:T(8,128)(2,1)S(1)}, bf16[64,1024]{1,0:T(8,128)(2,1)S(1)}, bf16[64,1024]{1,0:T(8,128)(2,1)S(1)}, bf16[64,1024]{1,0:T(8,128)(2,1)S(1)...) custom-call(s32[7]{0:T(128)S(1)} %stack.40.refs_0_, bf16[128,1024]{1,0:T(8,128)(2,1)S(1)} %get-tuple-element.128.refs_1_, ...), custom_call_target="tpu_custom_call" | custom-call | flops 115000000 | tf_op jit(solution)/shard_map/out1/pallas_call | solution.py:455
  95.7 4.5 %out2.1 = (bf16[128,4096]{1,0:T(8,128)(2,1)S(1)}, bf16[128,4096]{1,0:T(8,128)(2,1)S(1)}, f32[8,128]{1,0:T(8,128)S(1)}) custom-call(s32[7]{0:T(128)S(1)} %stack.40.refs_0_, bf16[128,1024]{1,0:T(8,128)(2,1)S(1)} %get-tuple-element.109.refs_1_, bf16[128,1024]{1,0:T(8,128)(2,1)S(1)} %collective-permute-done.12.refs_9_.refs_2_, ...), custom_call_target="tpu_custom_call" | custom-call | flops 115000000 | tf_op jit(solution)/shard_map/out2/pallas_call | solution.py:455
  100.3 9.0 %collective-permute-done.25.refs_2_.refs_7_ = bf16[64,4096]{1,0:T(8,128)(2,1)S(1)} collective-permute-done((bf16[64,4096]{1,0:T(8,128)(2,1)S(1)}, bf16[64,4096]{1,0:T(8,128)(2,1)S(1)}, u32[]{:S(2)}, u32[]{:S(2)}) %collective-permute-start.25) | collective-permute-done | bytes 524320 | tf_op jit(solution)/shard_map/ppermute | solution.py:546
  110.7 1.2 %collective-permute-done.26.refs_5_ = bf16[64,4096]{1,0:T(8,128)(2,1)S(1)} collective-permute-done((bf16[64,4096]{1,0:T(8,128)(2,1)S(1)}, bf16[64,4096]{1,0:T(8,128)(2,1)S(1)}, u32[]{:S(2)}, u32[]{:S(2)}) %collective-permute-start.26) | collective-permute-done | bytes 524320 | tf_op jit(solution)/shard_map/ppermute | solution.py:541
  112.0 2.2 %close.1 = (bf16[128,4096]{1,0:T(8,128)(2,1)}, f32[8,128]{1,0:T(8,128)}) custom-call(s32[7]{0:T(128)S(1)} %stack.40.refs_0_, f32[1]{0:T(128)S(6)} %copy.19.refs_1_, bf16[128,4096]{1,0:T(8,128)(2,1)S(1)} %bitcast.25, bf16[128,4096]{1,0:T(8,128)(2,1)S(1)} %get-tuple-element.140.refs_3_, bf16[128,4096]{1,0:T(8,128)(2,1)S(1)} %collective-permute-done.24.refs_4_, ...), custom_call_target="tpu_custom_call" | custom-call | flops 1150000000 | tf_op jit(solution)/shard_map/close/pallas_call | solution.py:455
  (89 shorter events, 16.2 us)
Async XLA Ops:
  0.0 3.1 %collective-permute-start = (bf16[128,4096]{1,0:T(8,128)(2,1)}, bf16[128,4096]{1,0:T(8,128)(2,1)S(1)}, u32[]{:S(2)}, u32[]{:S(2)}) collective-permute-start(bf16[128,4096]{1,0:T(8,128)(2,1)} %bitcast.20), channel_id=1, source_target_pairs={{0,8},{8,0},{16,24},{24,16},{1,9},{9,1},{17,25},{25,17},{2,10},{10... | collective-permute-start | bytes 3145736 | tf_op jit(solution)/shard_map/ppermute | solution.py:541
  0.5 28.0 %collective-permute-start.4 = (bf16[128,4096]{1,0:T(8,128)(2,1)}, bf16[128,4096]{1,0:T(8,128)(2,1)S(1)}, u32[]{:S(2)}, u32[]{:S(2)}) collective-permute-start(bf16[128,4096]{1,0:T(8,128)(2,1)} %bitcast.21), channel_id=1, source_target_pairs={{0,16},{8,24},{16,0},{24,8},{1,17},{9,25},{17,1},{25,9},{2,18},{10... | collective-permute-start | bytes 3145736 | tf_op jit(solution)/shard_map/ppermute | solution.py:546
  5.0 11.5 %copy-start.4 = (bf16[4096,1024]{1,0:T(8,128)(2,1)S(1)}, bf16[4096,1024]{1,0:T(8,128)(2,1)}, u32[]{:S(2)}) copy-start(bf16[4096,1024]{1,0:T(8,128)(2,1)} %refs_5_.5) | copy-start | bytes 25165828
  5.6 8.2 %collective-permute-start.1 = (bf16[16,2048]{1,0:T(8,128)(2,1)S(1)}, bf16[16,2048]{1,0:T(8,128)(2,1)S(1)}, u32[]{:S(2)}, u32[]{:S(2)}) collective-permute-start(bf16[16,2048]{1,0:T(8,128)(2,1)S(1)} %get-tuple-element.76), channel_id=1, source_target_pairs={{0,1},{1,2},{2,3},{3,4},{4,5},{5,6},{6,7},{7,0},{8,9},{9,10},{10,1... | collective-permute-start | bytes 196616 | tf_op jit(solution)/shard_map/ppermute | solution.py:537
  8.4 7.9 %collective-permute-start.2 = (bf16[16,2048]{1,0:T(8,128)(2,1)S(1)}, bf16[16,2048]{1,0:T(8,128)(2,1)S(1)}, u32[]{:S(2)}, u32[]{:S(2)}) collective-permute-start(bf16[16,2048]{1,0:T(8,128)(2,1)S(1)} %get-tuple-element.76), channel_id=1, source_target_pairs={{16,1},{17,2},{18,3},{19,4},{20,5},{21,6},{22,7},{23,0},{24,9},{25... | collective-permute-start | bytes 196616 | tf_op jit(solution)/shard_map/ppermute | solution.py:537
  28.4 2.7 %collective-permute-start.5 = (bf16[128,4096]{1,0:T(8,128)(2,1)S(1)}, bf16[128,4096]{1,0:T(8,128)(2,1)S(1)}, u32[]{:S(2)}, u32[]{:S(2)}) collective-permute-start(bf16[128,4096]{1,0:T(8,128)(2,1)S(1)} %hold.1.refs_1_), channel_id=1, source_target_pairs={{0,8},{8,0},{16,24},{24,16},{1,9},{9,1},{17,25},{25,17},{2,10},{10... | collective-permute-start | bytes 3145736 | tf_op jit(solution)/shard_map/ppermute | solution.py:541
  28.4 9.4 %collective-permute-start.3 = (bf16[144,1024]{1,0:T(8,128)(2,1)S(1)}, bf16[144,1024]{1,0:T(8,128)(2,1)S(1)}, u32[]{:S(2)}, u32[]{:S(2)}) collective-permute-start(bf16[144,1024]{1,0:T(8,128)(2,1)S(1)} %get-tuple-element.79), channel_id=1, source_target_pairs={{0,1},{1,0},{2,3},{3,2},{4,5},{5,4},{6,7},{7,6},{8,9},{9,8},{10,11... | collective-permute-start | bytes 884744 | tf_op jit(solution)/shard_map/ppermute | solution.py:541
  31.1 18.9 %slice-start = ((s8[8388608]{0:T(1024)(128)(4,1)}), s8[4194304]{0:T(1024)(128)(4,1)S(1)}, s32[]{:S(2)}) async-start(s8[8388608]{0:T(1024)(128)(4,1)} %bitcast.16), calls=%async_computation | async-start | bytes 8388608
  35.6 11.0 %collective-permute-start.7 = (bf16[144,1024]{1,0:T(8,128)(2,1)S(1)}, bf16[144,1024]{1,0:T(8,128)(2,1)S(1)}, u32[]{:S(2)}, u32[]{:S(2)}) collective-permute-start(bf16[144,1024]{1,0:T(8,128)(2,1)S(1)} %get-tuple-element.83.refs_1_), channel_id=1, source_target_pairs={{0,1},{1,0},{2,3},{3,2},{4,5},{5,4},{6,7},{7,6},{8,9},{9,8},{10,11... | collective-permute-start | bytes 884744 | tf_op jit(solution)/shard_map/ppermute | solution.py:541
  38.5 10.8 %collective-permute-start.6 = (bf16[144,1024]{1,0:T(8,128)(2,1)S(1)}, bf16[144,1024]{1,0:T(8,128)(2,1)S(1)}, u32[]{:S(2)}, u32[]{:S(2)}) collective-permute-start(bf16[144,1024]{1,0:T(8,128)(2,1)S(1)} %get-tuple-element.82.refs_1_), channel_id=1, source_target_pairs={{0,2},{1,3},{2,4},{3,5},{4,6},{5,7},{6,0},{7,1},{8,10},{9,11},{10,... | collective-permute-start | bytes 884744 | tf_op jit(solution)/shard_map/ppermute | solution.py:527
  45.1 8.4 %collective-permute-start.10 = (bf16[144,1024]{1,0:T(8,128)(2,1)S(1)}, bf16[144,1024]{1,0:T(8,128)(2,1)S(1)}, u32[]{:S(2)}, u32[]{:S(2)}) collective-permute-start(bf16[144,1024]{1,0:T(8,128)(2,1)S(1)} %get-tuple-element.89.refs_1_), channel_id=1, source_target_pairs={{0,1},{1,0},{2,3},{3,2},{4,5},{5,4},{6,7},{7,6},{8,9},{9,8},{10,11... | collective-permute-start | bytes 884744 | tf_op jit(solution)/shard_map/ppermute | solution.py:541
  47.3 9.9 %collective-permute-start.9 = (bf16[144,1024]{1,0:T(8,128)(2,1)S(1)}, bf16[144,1024]{1,0:T(8,128)(2,1)S(1)}, u32[]{:S(2)}, u32[]{:S(2)}) collective-permute-start(bf16[144,1024]{1,0:T(8,128)(2,1)S(1)} %get-tuple-element.88.refs_1_), channel_id=1, source_target_pairs={{0,2},{1,3},{2,4},{3,5},{4,6},{5,7},{6,0},{7,1},{8,10},{9,11},{10,... | collective-permute-start | bytes 884744 | tf_op jit(solution)/shard_map/ppermute | solution.py:527
  50.0 19.7 %slice-start.2 = ((s8[8388608]{0:T(1024)(128)(4,1)}), s8[4194304]{0:T(1024)(128)(4,1)S(1)}, s32[]{:S(2)}) async-start(s8[8388608]{0:T(1024)(128)(4,1)} %bitcast.18), calls=%async_computation.2 | async-start | bytes 8388608
  52.6 17.1 %copy-start.2 = (f32[1024]{0:T(1024)S(1)}, f32[1024]{0:T(1024)}, u32[]{:S(2)}) copy-start(f32[1024]{0:T(1024)} %param.29) | copy-start | bytes 12292
  57.3 12.5 %slice-start.3 = ((s8[8388608]{0:T(1024)(128)(4,1)}), s8[4194304]{0:T(1024)(128)(4,1)S(1)}, s32[]{:S(2)}) async-start(s8[8388608]{0:T(1024)(128)(4,1)} %bitcast.18), calls=%async_computation.3 | async-start | bytes 8388608
  57.9 11.1 %collective-permute-start.11 = (bf16[128,1024]{1,0:T(8,128)(2,1)S(1)}, bf16[128,1024]{1,0:T(8,128)(2,1)S(1)}, u32[]{:S(2)}, u32[]{:S(2)}) collective-permute-start(bf16[128,1024]{1,0:T(8,128)(2,1)S(1)} %get-tuple-element.97), channel_id=1, source_target_pairs={{0,2},{1,3},{2,4},{3,5},{4,6},{5,7},{6,0},{7,1},{8,10},{9,11},{10,... | collective-permute-start | bytes 786440 | tf_op jit(solution)/shard_map/ppermute | solution.py:527
  58.0 16.6 %collective-permute-start.8 = (bf16[128,1024]{1,0:T(8,128)(2,1)S(1)}, bf16[128,1024]{1,0:T(8,128)(2,1)S(1)}, u32[]{:S(2)}, u32[]{:S(2)}) collective-permute-start(bf16[128,1024]{1,0:T(8,128)(2,1)S(1)} %get-tuple-element.87), channel_id=1, source_target_pairs={{0,2},{1,3},{2,4},{3,5},{4,6},{5,7},{6,0},{7,1},{8,10},{9,11},{10,... | collective-permute-start | bytes 786440 | tf_op jit(solution)/shard_map/ppermute | solution.py:527
  59.3 18.9 %collective-permute-start.13 = (bf16[144,1024]{1,0:T(8,128)(2,1)S(1)}, bf16[144,1024]{1,0:T(8,128)(2,1)S(1)}, u32[]{:S(2)}, u32[]{:S(2)}) collective-permute-start(bf16[144,1024]{1,0:T(8,128)(2,1)S(1)} %get-tuple-element.115.refs_1_), channel_id=1, source_target_pairs={{0,2},{1,3},{2,4},{3,5},{4,6},{5,7},{6,0},{7,1},{8,10},{9,11},{10,... | collective-permute-start | bytes 884744 | tf_op jit(solution)/shard_map/ppermute | solution.py:527
  72.4 3.0 %collective-permute-start.14 = (bf16[64,1024]{1,0:T(8,128)(2,1)S(1)}, bf16[64,1024]{1,0:T(8,128)(2,1)S(1)}, u32[]{:S(2)}, u32[]{:S(2)}) collective-permute-start(bf16[64,1024]{1,0:T(8,128)(2,1)S(1)} %get-tuple-element.117), channel_id=1, source_target_pairs={{0,8},{8,0},{16,24},{24,16},{1,9},{9,1},{17,25},{25,17},{2,10},{10... | collective-permute-start | bytes 393224 | tf_op jit(solution)/shard_map/ppermute | solution.py:541
  72.4 2.9 %collective-permute-start.15 = (bf16[64,1024]{1,0:T(8,128)(2,1)S(1)}, bf16[64,1024]{1,0:T(8,128)(2,1)S(1)}, u32[]{:S(2)}, u32[]{:S(2)}) collective-permute-start(bf16[64,1024]{1,0:T(8,128)(2,1)S(1)} %get-tuple-element.118), channel_id=1, source_target_pairs={{0,8},{8,0},{16,24},{24,16},{1,9},{9,1},{17,25},{25,17},{2,10},{10... | collective-permute-start | bytes 393224 | tf_op jit(solution)/shard_map/ppermute | solution.py:541
  72.9 2.4 %collective-permute-start.16 = (bf16[64,1024]{1,0:T(8,128)(2,1)S(1)}, bf16[64,1024]{1,0:T(8,128)(2,1)S(1)}, u32[]{:S(2)}, u32[]{:S(2)}) collective-permute-start(bf16[64,1024]{1,0:T(8,128)(2,1)S(1)} %get-tuple-element.119), channel_id=1, source_target_pairs={{0,8},{8,0},{16,24},{24,16},{1,9},{9,1},{17,25},{25,17},{2,10},{10... | collective-permute-start | bytes 393224 | tf_op jit(solution)/shard_map/ppermute | solution.py:541
  74.6 1.3 %collective-permute-start.17 = (bf16[64,1024]{1,0:T(8,128)(2,1)S(1)}, bf16[64,1024]{1,0:T(8,128)(2,1)S(1)}, u32[]{:S(2)}, u32[]{:S(2)}) collective-permute-start(bf16[64,1024]{1,0:T(8,128)(2,1)S(1)} %get-tuple-element.120), channel_id=1, source_target_pairs={{0,8},{8,0},{16,24},{24,16},{1,9},{9,1},{17,25},{25,17},{2,10},{10... | collective-permute-start | bytes 393224 | tf_op jit(solution)/shard_map/ppermute | solution.py:541
  76.6 17.8 %collective-permute-start.23 = (bf16[64,4096]{1,0:T(8,128)(2,1)S(1)}, bf16[64,4096]{1,0:T(8,128)(2,1)S(1)}, u32[]{:S(2)}, u32[]{:S(2)}) collective-permute-start(bf16[64,4096]{1,0:T(8,128)(2,1)S(1)} %get-tuple-element.137), channel_id=1, source_target_pairs={{0,16},{8,24},{16,0},{24,8},{1,17},{9,25},{17,1},{25,9},{2,18},{10... | collective-permute-start | bytes 1572872 | tf_op jit(solution)/shard_map/ppermute | solution.py:546
  78.8 10.2 %collective-permute-start.18 = (bf16[128,1024]{1,0:T(8,128)(2,1)S(1)}, bf16[128,1024]{1,0:T(8,128)(2,1)S(1)}, u32[]{:S(2)}, u32[]{:S(2)}) collective-permute-start(bf16[128,1024]{1,0:T(8,128)(2,1)S(1)} %get-tuple-element.126), channel_id=1, source_target_pairs={{0,2},{1,3},{2,4},{3,5},{4,6},{5,7},{6,0},{7,1},{8,10},{9,11},{10,... | collective-permute-start | bytes 786440 | tf_op jit(solution)/shard_map/ppermute | solution.py:527
  79.1 10.6 %collective-permute-start.12 = (bf16[128,1024]{1,0:T(8,128)(2,1)S(1)}, bf16[128,1024]{1,0:T(8,128)(2,1)S(1)}, u32[]{:S(2)}, u32[]{:S(2)}) collective-permute-start(bf16[128,1024]{1,0:T(8,128)(2,1)S(1)} %get-tuple-element.110), channel_id=1, source_target_pairs={{0,1},{1,0},{2,3},{3,2},{4,5},{5,4},{6,7},{7,6},{8,9},{9,8},{10,11... | collective-permute-start | bytes 786440 | tf_op jit(solution)/shard_map/ppermute | solution.py:541
  92.3 1.4 %collective-permute-start.19 = (bf16[64,1024]{1,0:T(8,128)(2,1)S(1)}, bf16[64,1024]{1,0:T(8,128)(2,1)S(1)}, u32[]{:S(2)}, u32[]{:S(2)}) collective-permute-start(bf16[64,1024]{1,0:T(8,128)(2,1)S(1)} %get-tuple-element.133), channel_id=1, source_target_pairs={{0,8},{8,0},{16,24},{24,16},{1,9},{9,1},{17,25},{25,17},{2,10},{10... | collective-permute-start | bytes 393224 | tf_op jit(solution)/shard_map/ppermute | solution.py:541
  92.4 1.5 %collective-permute-start.20 = (bf16[64,1024]{1,0:T(8,128)(2,1)S(1)}, bf16[64,1024]{1,0:T(8,128)(2,1)S(1)}, u32[]{:S(2)}, u32[]{:S(2)}) collective-permute-start(bf16[64,1024]{1,0:T(8,128)(2,1)S(1)} %get-tuple-element.134), channel_id=1, source_target_pairs={{0,8},{8,0},{16,24},{24,16},{1,9},{9,1},{17,25},{25,17},{2,10},{10... | collective-permute-start | bytes 393224 | tf_op jit(solution)/shard_map/ppermute | solution.py:541
  92.9 1.3 %collective-permute-start.21 = (bf16[64,1024]{1,0:T(8,128)(2,1)S(1)}, bf16[64,1024]{1,0:T(8,128)(2,1)S(1)}, u32[]{:S(2)}, u32[]{:S(2)}) collective-permute-start(bf16[64,1024]{1,0:T(8,128)(2,1)S(1)} %get-tuple-element.135), channel_id=1, source_target_pairs={{0,8},{8,0},{16,24},{24,16},{1,9},{9,1},{17,25},{25,17},{2,10},{10... | collective-permute-start | bytes 393224 | tf_op jit(solution)/shard_map/ppermute | solution.py:541
  93.0 1.5 %collective-permute-start.22 = (bf16[64,1024]{1,0:T(8,128)(2,1)S(1)}, bf16[64,1024]{1,0:T(8,128)(2,1)S(1)}, u32[]{:S(2)}, u32[]{:S(2)}) collective-permute-start(bf16[64,1024]{1,0:T(8,128)(2,1)S(1)} %get-tuple-element.136), channel_id=1, source_target_pairs={{0,8},{8,0},{16,24},{24,16},{1,9},{9,1},{17,25},{25,17},{2,10},{10... | collective-permute-start | bytes 393224 | tf_op jit(solution)/shard_map/ppermute | solution.py:541
  95.1 14.2 %collective-permute-start.25 = (bf16[64,4096]{1,0:T(8,128)(2,1)S(1)}, bf16[64,4096]{1,0:T(8,128)(2,1)S(1)}, u32[]{:S(2)}, u32[]{:S(2)}) collective-permute-start(bf16[64,4096]{1,0:T(8,128)(2,1)S(1)} %get-tuple-element.142), channel_id=1, source_target_pairs={{0,16},{8,24},{16,0},{24,8},{1,17},{9,25},{17,1},{25,9},{2,18},{10... | collective-permute-start | bytes 1572872 | tf_op jit(solution)/shard_map/ppermute | solution.py:546
  100.2 11.8 %collective-permute-start.24 = (bf16[128,4096]{1,0:T(8,128)(2,1)S(1)}, bf16[128,4096]{1,0:T(8,128)(2,1)S(1)}, u32[]{:S(2)}, u32[]{:S(2)}) collective-permute-start(bf16[128,4096]{1,0:T(8,128)(2,1)S(1)} %get-tuple-element.141), channel_id=1, source_target_pairs={{0,8},{8,0},{16,24},{24,16},{1,9},{9,1},{17,25},{25,17},{2,10},{10... | collective-permute-start | bytes 3145736 | tf_op jit(solution)/shard_map/ppermute | solution.py:541
  110.0 2.0 %collective-permute-start.26 = (bf16[64,4096]{1,0:T(8,128)(2,1)S(1)}, bf16[64,4096]{1,0:T(8,128)(2,1)S(1)}, u32[]{:S(2)}, u32[]{:S(2)}) collective-permute-start(bf16[64,4096]{1,0:T(8,128)(2,1)S(1)} %get-tuple-element.144), channel_id=1, source_target_pairs={{0,8},{8,0},{16,24},{24,16},{1,9},{9,1},{17,25},{25,17},{2,10},{10... | collective-permute-start | bytes 1572872 | tf_op jit(solution)/shard_map/ppermute | solution.py:541
  (14 other events, 124.8 us)

commit v4 on v3

--- a/solution.py
+++ b/solution.py
@@ -98,14 +98,13 @@
     rows_ref[s] = found
 
 
-def mix_kernel(slots, streams, flip, carried, flags_ref, *refs):
+def mix_kernel(slots, streams, flip, flags_ref, *refs):
     sources, refs = refs[:2], refs[2:]
-    tail_ref, refs = refs[0], refs[-15 - carried :]
+    tail_ref, refs = refs[0], refs[-15 - slots :]
     segments_ref, value_ref, coupling_ref, step_ref, *taps_refs, head_ref = refs[:9]
     refs = refs[9:]
     values_ref, coupled_ref, sums_ref, rows_ref = refs[:4]
-    state_refs, (rows_scr, pad_scr) = refs[4 : 4 + carried], refs[4 + carried :]
-    lines = state_refs[0].shape[0] - FACTOR_ROWS
+    state_refs, (rows_scr, pad_scr) = refs[4 : 4 + slots], refs[4 + slots :]
     odd = flags_ref[0] == 1
     heads = step_ref.shape[0]
     reach = 3
@@ -156,7 +155,7 @@
     upto = (source <= position).astype(f32)
 
     def put_states(parts, first, columns):
-        if carried == 1:
+        if slots == 1:
             state_refs[0][first : first + parts[0].shape[0], columns] = parts[0].astype(bf16)
             return
         given = jnp.where(odd, parts[1], parts[0]).astype(bf16)
@@ -206,12 +205,10 @@
                     keys, weighted, (((0,), (0,)), ((), ())), preferred_element_type=f32
                 )
             )
-        if slots < carried:
-            parts = [parts[0][:lines], parts[0][lines:]]
         put_states(parts, 0, own)
 
     weights = [weighed(s) for s in range(slots)]
-    put_states([weights[0][1], weights[-1][1]], lines, slice(0, width))
+    put_states([w[1] for w in weights], N, slice(0, width))
     per_group = len(work) // groups
     waiting = None
     for i in range(len(work) + 1):
@@ -327,18 +324,22 @@
     put_packed(out_ref, state + reached * earlier, reached * leading)
 
 
-def finish_kernel(flags_ref, mine_ref, got_ref, before_ref, own_ref, *other_refs):
+def entered(flags_ref, mine_ref, got_ref, before_ref):
     odd = flags_ref[0] == 1
     even, _ = paired(odd, mine_ref, got_ref)
     before = jnp.where(flags_ref[2] >= 2, before_ref[...].astype(f32), 0.0)
     between = even[0] + even[1] * before
-    own_ref[...] = jnp.where(odd, between, before).astype(bf16)
-    for other_ref in other_refs:
-        other_ref[...] = jnp.where(odd, before, between).astype(bf16)
-
-
-def out_kernel(slots, blocks, carried, flags_ref, *refs):
-    entry_refs, refs = refs[:carried], refs[carried:]
+    return jnp.where(odd, between, before), jnp.where(odd, before, between)
+
+
+def finish_kernel(flags_ref, mine_ref, got_ref, before_ref, own_ref, other_ref):
+    own, other = entered(flags_ref, mine_ref, got_ref, before_ref)
+    own_ref[...] = own.astype(bf16)
+    other_ref[...] = other.astype(bf16)
+
+
+def out_kernel(slots, blocks, flags_ref, *refs):
+    entry_refs, refs = refs[: 4 - slots], refs[4 - slots :]
     (
         local_ref,
         gates_ref,
@@ -361,12 +362,11 @@
     share = local_ref.shape[2] // groups
     count = sums_ref.shape[1]
     per_step = WIDE // P_SIZE
-    entries = [entry_refs[0][...]]
-    if carried == 2:
+    if slots == 1:
+        entries = [entered(flags_ref, *entry_refs)[0].astype(bf16)]
+    else:
         own, other = [ref[...].astype(f32) for ref in entry_refs]
         entries = [jnp.where(odd, a, b).astype(bf16) for a, b in ((own, other), (other, own))]
-        if slots == 1:
-            entries = [jnp.concatenate(entries)]
     for s in range(slots):
         sums = jnp.concatenate([sums_ref[s, jj] for jj in range(count)], axis=0)
         line = lax.broadcasted_iota(jnp.int32, sums.shape, 0) % 8
@@ -414,20 +414,13 @@
         out_ref[:, own] = (mine_ref[:, own].astype(f32) + ref[...].astype(f32)).astype(bf16)
 
 
-def give_kernel(flags_ref, *refs):
+def close_kernel(flags_ref, rezero_ref, own_ref, mine_ref, others_ref, *refs):
     *back, out_ref = refs
-    chips = len(back) // 2
-    out_ref[...] = jnp.where(
-        flags_ref[1] == 0, summed(back[chips:]), summed(back[:chips])
-    ).astype(bf16)
-
-
-def close_kernel(flags_ref, rezero_ref, own_ref, mine_ref, others_ref, theirs_ref, *refs):
-    *back, out_ref = refs
-    chips = len(back) // 2
-    core = flags_ref[1]
-    ours = jnp.where(core == 0, summed(back[:chips]), summed(back[chips:]))
-    for at, far in ((core, ours), (1 - core, theirs_ref[...].astype(f32))):
+    chips, core = len(back) // 4, flags_ref[1]
+    sums = [back[i * chips : (i + 1) * chips] for i in range(4)]
+    ours = jnp.where(core == 0, summed(sums[0]), summed(sums[1]))
+    theirs = jnp.where(core == 0, summed(sums[2]), summed(sums[3]))
+    for at, far in ((core, ours), (1 - core, theirs)):
         lines = pl.ds(pl.multiple_of(at * HALF, HALF), HALF)
         branch = mine_ref[lines].astype(f32) + others_ref[lines].astype(f32) + far
         out_ref[lines] = (own_ref[lines].astype(f32) + rezero_ref[0] * branch).astype(bf16)
@@ -485,7 +478,7 @@
     return jax.ShapeDtypeStruct(sizes, dtype)
 
 
-def mix(run, slots, streams, flip, carried, sources, tails, segments, weights, small):
+def mix(run, slots, streams, flip, sources, tails, segments, weights, small):
     value_weight, coupling_weight = weights
     width, narrow, depth = value_weight.shape[1], coupling_weight.shape[1], value_weight.shape[0]
     shapes = [
@@ -493,12 +486,12 @@
         shape(bf16, slots, CH, narrow),
         shape(f32, slots, narrow // N, 8, CH),
         shape(f32, slots, 8, CH),
-    ] + [shape(bf16, N * slots // carried + FACTOR_ROWS, width)] * carried
+    ] + [shape(bf16, N + FACTOR_ROWS, width)] * slots
     scratch = [
         pltpu.VMEM((slots * CH + TAILS, depth), bf16),
         pltpu.VMEM((2, slots, CH + TAIL, WIDE), f32),
     ]
-    kernel = functools.partial(mix_kernel, slots, streams, flip, carried)
+    kernel = functools.partial(mix_kernel, slots, streams, flip)
     operands = (*sources, *tails, segments, *weights, *small)
     return run(kernel, f"mix{slots}", shapes, scratch, *operands, mib=8, us=4 * slots)
 
@@ -515,7 +508,7 @@
     width, depth = out_weight.shape
     lines = CH if slots == 2 else HALF
     scratch = [pltpu.VMEM((slots * CH, width), bf16)]
-    kernel = functools.partial(out_kernel, slots, 8, len(entries))
+    kernel = functools.partial(out_kernel, slots, 8)
     operands = (*entries, local, gates, coupled, sums, rows, gain, out_weight, *waits)
     pieces = 1 if slots == 2 else PIECES
     shapes = [shape(bf16, lines, depth)] + [shape(bf16, lines, depth // pieces)] * pieces
@@ -563,10 +556,10 @@
     return block
 
 
-def finished(run, kept, got, before, carried):
-    out = [shape(bf16, *before.shape)] * carried
-    own, *others = run(finish_kernel, "finish", out, [], kept, got, before, us=0.1)
-    return own, *[partner(other, "ctx") for other in others]
+def finished(run, kept, got, before):
+    out = [shape(bf16, *before.shape)] * 2
+    own, other = run(finish_kernel, "finish", out, [], kept, got, before, us=0.1)
+    return own, partner(other, "ctx")
 
 
 def on_device(
@@ -617,7 +610,7 @@
     far = [tail_from(tail, d) for d in range(1, chips)]
     near_sources = (own, opposite)
     values, coupled, near_sums, near_rows, given, near_kept = mix(
-        run, 2, (3, 4), None, 2, near_sources, [near, *far], segments, weights, small
+        run, 2, (3, 4), None, near_sources, [near, *far], segments, weights, small
     )
     near_mixed = (values, coupled, near_sums)
     near_got = partner(given, "ctx")
@@ -627,18 +620,16 @@
         if j == 0:
             arrival = sequence.held(arrived[d])
             sources = (arrival, partner(arrival, "fsdp"))
-        carried = 1
         mixed = mix(
-            run, 1, (5 + i,), j, carried, sources, far[d - 1 : d], segments, weights, small
+            run, 1, (5 + i,), j, sources, far[d - 1 : d], segments, weights, small
         )
-        given, kept = mixed[4], mixed[-1]
-        far_mixed.append((sources, *mixed[:4], kept, partner(given, "ctx"), carried))
+        far_mixed.append((sources, *mixed, partner(mixed[-1], "ctx")))
         if i == 0:
             near_block = joined(run, near_kept, near_got)
 
     far_scans, blocks, befores = [], [], []
     for i, ((d, j), far_one) in enumerate(zip(phases, far_mixed)):
-        sources, values, coupled, sums, rows, kept, got, _ = far_one
+        sources, values, coupled, sums, rows, kept, got = far_one
         blocks.append(joined(run, kept, got))
         if i == 0:
             near_before = along(chained(run, near_block), 2)
@@ -650,12 +641,11 @@
 
     back, latest = {}, ()
     for i, ((d, j), (gates, local), far_one) in enumerate(zip(phases, far_scans, far_mixed)):
-        _, _, coupled, sums, rows, kept, got, carried = far_one
-        entries = finished(run, kept, got, befores[i], carried)
+        _, _, coupled, sums, rows, kept, got = far_one
         mine, *pieces = project_out(
             run,
             1,
-            entries,
+            (kept, got, befores[i]),
             local,
             gates,
             coupled,
@@ -667,7 +657,7 @@
         )
         pieces = [partner(piece, "fsdp") for piece in pieces]
         if i == 0:
-            near_entries = finished(run, near_kept, near_got, near_before, 2)
+            near_entries = finished(run, near_kept, near_got, near_before)
         kernel = functools.partial(add_kernel, len(pieces))
         total = run(kernel, "add", [half_shape], [], mine, *pieces, *latest, us=0.1)[0]
         back[d, j] = over(total, d)
@@ -692,7 +682,6 @@
     )
     near_others = partner(near_others, "fsdp")
     returned = [back[d, j] for j in range(2) for d in range(1, chips)]
-    given = run(give_kernel, "give", [half_shape], [], *returned, us=0.1)[0]
     return run(
         close_kernel,
         "close",
@@ -701,8 +690,8 @@
         own,
         near_mine,
         near_others,
-        partner(given, "fsdp"),
         *returned,
+        *[partner(block, "fsdp") for block in returned],
         mib=4,
         scalars=(rezero,),
     )[0][None]

time: 114 us -> 113 us (level)
  Pallas kernels: 46.5 us -> 44.4 us
    ppermute x16 -> x17, waiting for transfers between devices: 5.14 us -> 7.7 us  [partner(): lax.ppermute(block, axis, [(i, i ^ 1) for i in range(lax.axis_size(axis))])]
    pallas_call x23 -> x20, Pallas kernels: 46.5 us -> 44.4 us  [run(): pl.pallas_call(ordered, in_specs=[IN_SMEM] * (1 + len(scalars)) + [IN_VME...]
    ppermute x6, waiting for transfers between devices: 16.9 us -> 15.4 us  [along(): lax.ppermute(block, 'ctx', [(i, (i + distance) % spans) for i in range(sp...]
    ppermute x16 -> x17, starting transfers between devices: 8.02 us -> 8.35 us  [partner(): lax.ppermute(block, axis, [(i, i ^ 1) for i in range(lax.axis_size(axis))])]
  transfers between devices with their start and end apart: 27 -> 28, of which waited for: 18 -> 19; matrix products, arithmetic and copies ran while one was open for 0% -> 0% of each run, Pallas kernels for 38% -> 36%
where the time goes in v4:
time: 113 us
  Pallas kernels  44.4 us (39%)
  waiting for transfers between devices  41.6 us (37%)
  starting transfers between devices  23.8 us (21%)
  local copies, waits for them, and re-layouts  2.15 us (2%)
    pallas_call x20, Pallas kernels, run(): pl.pallas_call(ordered, in_specs=[IN_SMEM] * (1 + len(scalars)) + [IN_VME...  44.4 us
    ppermute x6, waiting for transfers between devices, along(): lax.ppermute(block, 'ctx', [(i, (i + distance) % spans) for i in range(sp...  15.4 us
    ppermute x3, waiting for transfers between devices, over(): lax.ppermute(block, 'fsdp', [(i, (i + 2 * distance) % size) for i in rang...  13.1 us
    ppermute x17, starting transfers between devices, partner(): lax.ppermute(block, axis, [(i, i ^ 1) for i in range(lax.axis_size(axis))])  8.35 us
    ppermute x17, waiting for transfers between devices, partner(): lax.ppermute(block, axis, [(i, i ^ 1) for i in range(lax.axis_size(axis))])  7.7 us
    ppermute x6, starting transfers between devices, along(): lax.ppermute(block, 'ctx', [(i, (i + distance) % spans) for i in range(sp...  5.49 us
    ppermute x2, waiting for transfers between devices, tail_from(): return lax.ppermute(block, ('fsdp', 'ctx'), route)  5.42 us
    ppermute x2, starting transfers between devices, tail_from(): return lax.ppermute(block, ('fsdp', 'ctx'), route)  5.31 us
  transfers between devices with their start and end apart: 28, of which 19 were waited for; matrix products, arithmetic and copies ran while one was open for 0% of the time, Pallas kernels for 36%

profile of v4, /device:TPU:0, one launch (start us, length us, event | category | flops | bytes accessed | tf_op | source)
XLA Modules:
  0.0 113.1 jit_solution(7130574619988247833)
XLA Ops:
  0.5 2.5 %collective-permute-start.4 = (bf16[128,4096]{1,0:T(8,128)(2,1)}, bf16[128,4096]{1,0:T(8,128)(2,1)S(1)}, u32[]{:S(2)}, u32[]{:S(2)}) collective-permute-start(bf16[128,4096]{1,0:T(8,128)(2,1)} %bitcast.21), channel_id=1, source_target_pairs={{0,16},{8,24},{16,0},{24,8},{1,17},{9,25},{17,1},{25,9},{2,18},{10... | collective-permute-start | bytes 3145736 | tf_op jit(solution)/shard_map/ppermute | solution.py:539
  3.1 1.2 %copy-done = bf16[1,128,4096]{2,1,0:T(8,128)(2,1)S(1)} copy-done((bf16[1,128,4096]{2,1,0:T(8,128)(2,1)S(1)}, bf16[1,128,4096]{2,1,0:T(8,128)(2,1)}, u32[]{:S(2)}) %copy-start) | copy-done | bytes 1048600
  5.6 2.8 %collective-permute-start.1 = (bf16[16,2048]{1,0:T(8,128)(2,1)S(1)}, bf16[16,2048]{1,0:T(8,128)(2,1)S(1)}, u32[]{:S(2)}, u32[]{:S(2)}) collective-permute-start(bf16[16,2048]{1,0:T(8,128)(2,1)S(1)} %get-tuple-element.70), channel_id=1, source_target_pairs={{0,1},{1,2},{2,3},{3,4},{4,5},{5,6},{6,7},{7,0},{8,9},{9,10},{10,1... | collective-permute-start | bytes 196616 | tf_op jit(solution)/shard_map/ppermute | solution.py:530
  8.4 2.5 %collective-permute-start.2 = (bf16[16,2048]{1,0:T(8,128)(2,1)S(1)}, bf16[16,2048]{1,0:T(8,128)(2,1)S(1)}, u32[]{:S(2)}, u32[]{:S(2)}) collective-permute-start(bf16[16,2048]{1,0:T(8,128)(2,1)S(1)} %get-tuple-element.70), channel_id=1, source_target_pairs={{16,1},{17,2},{18,3},{19,4},{20,5},{21,6},{22,7},{23,0},{24,9},{25... | collective-permute-start | bytes 196616 | tf_op jit(solution)/shard_map/ppermute | solution.py:530
  11.0 2.9 %collective-permute-done.1.refs_3_ = bf16[16,2048]{1,0:T(8,128)(2,1)S(1)} collective-permute-done((bf16[16,2048]{1,0:T(8,128)(2,1)S(1)}, bf16[16,2048]{1,0:T(8,128)(2,1)S(1)}, u32[]{:S(2)}, u32[]{:S(2)}) %collective-permute-start.1) | collective-permute-done | bytes 65568 | tf_op jit(solution)/shard_map/ppermute | solution.py:530
  13.9 2.5 %collective-permute-done.2.refs_4_.refs_3_ = bf16[16,2048]{1,0:T(8,128)(2,1)S(1)} collective-permute-done((bf16[16,2048]{1,0:T(8,128)(2,1)S(1)}, bf16[16,2048]{1,0:T(8,128)(2,1)S(1)}, u32[]{:S(2)}, u32[]{:S(2)}) %collective-permute-start.2) | collective-permute-done | bytes 65568 | tf_op jit(solution)/shard_map/ppermute | solution.py:530
  16.5 7.4 %mix2.1 = (bf16[2,128,1024]{2,1,0:T(8,128)(2,1)S(1)}, bf16[2,128,512]{2,1,0:T(8,128)(2,1)S(1)}, f32[2,4,8,128]{3,2,1,0:T(8,128)S(1)}, f32[2,8,128]{2,1,0:T(8,128...) custom-call(s32[7]{0:T(128)S(1)} %stack.40.refs_0_, ...), custom_call_target="tpu_custom_call" | custom-call | flops 9200000000 | tf_op jit(solution)/shard_map/mix2/pallas_call | solution.py:448
  23.9 4.5 %collective-permute-done.4.block_ref = bf16[128,4096]{1,0:T(8,128)(2,1)S(1)} collective-permute-done((bf16[128,4096]{1,0:T(8,128)(2,1)}, bf16[128,4096]{1,0:T(8,128)(2,1)S(1)}, u32[]{:S(2)}, u32[]{:S(2)}) %collective-permute-start.4) | collective-permute-done | bytes 1048608 | tf_op jit(solution)/shard_map/ppermute | solution.py:539
  28.4 1.7 %collective-permute-start.3 = (bf16[144,1024]{1,0:T(8,128)(2,1)S(1)}, bf16[144,1024]{1,0:T(8,128)(2,1)S(1)}, u32[]{:S(2)}, u32[]{:S(2)}) collective-permute-start(bf16[144,1024]{1,0:T(8,128)(2,1)S(1)} %get-tuple-element.73), channel_id=1, source_target_pairs={{0,1},{1,0},{2,3},{3,2},{4,5},{5,4},{6,7},{7,6},{8,9},{9,8},{10,11... | collective-permute-start | bytes 884744 | tf_op jit(solution)/shard_map/ppermute | solution.py:534
  30.1 0.9 collective-permute-done.5.refs_2_
  31.1 4.5 %mix1.2 = (bf16[1,128,1024]{2,1,0:T(8,128)(2,1)S(1)}, bf16[1,128,512]{2,1,0:T(8,128)(2,1)S(1)}, f32[1,4,8,128]{3,2,1,0:T(8,128)S(1)}, f32[1,8,128]{2,1,0:T(8,128...) custom-call(s32[7]{0:T(128)S(1)} %stack.40.refs_0_, bf16[128,4096]{1,0:T(8,128)(2,1)S(1)} %hold.1.refs_1_, ...), custom_call_target="tpu_custom_call" | custom-call | flops 4600000000 | tf_op jit(solution)/shard_map/mix1/pallas_call | solution.py:448
  35.6 1.8 %collective-permute-start.7 = (bf16[144,1024]{1,0:T(8,128)(2,1)S(1)}, bf16[144,1024]{1,0:T(8,128)(2,1)S(1)}, u32[]{:S(2)}, u32[]{:S(2)}) collective-permute-start(bf16[144,1024]{1,0:T(8,128)(2,1)S(1)} %get-tuple-element.77.refs_1_), channel_id=1, source_target_pairs={{0,1},{1,0},{2,3},{3,2},{4,5},{5,4},{6,7},{7,6},{8,9},{9,8},{10,11... | collective-permute-start | bytes 884744 | tf_op jit(solution)/shard_map/ppermute | solution.py:534
  38.5 1.9 %collective-permute-start.6 = (bf16[144,1024]{1,0:T(8,128)(2,1)S(1)}, bf16[144,1024]{1,0:T(8,128)(2,1)S(1)}, u32[]{:S(2)}, u32[]{:S(2)}) collective-permute-start(bf16[144,1024]{1,0:T(8,128)(2,1)S(1)} %get-tuple-element.76.refs_1_), channel_id=1, source_target_pairs={{0,2},{1,3},{2,4},{3,5},{4,6},{5,7},{6,0},{7,1},{8,10},{9,11},{10,... | collective-permute-start | bytes 884744 | tf_op jit(solution)/shard_map/ppermute | solution.py:520
  40.4 4.7 %mix1.3 = (bf16[1,128,1024]{2,1,0:T(8,128)(2,1)S(1)}, bf16[1,128,512]{2,1,0:T(8,128)(2,1)S(1)}, f32[1,4,8,128]{3,2,1,0:T(8,128)S(1)}, f32[1,8,128]{2,1,0:T(8,128...) custom-call(s32[7]{0:T(128)S(1)} %stack.40.refs_0_, bf16[128,4096]{1,0:T(8,128)(2,1)S(1)} %hold.1.refs_1_, ...), custom_call_target="tpu_custom_call" | custom-call | flops 4600000000 | tf_op jit(solution)/shard_map/mix1/pallas_call | solution.py:448
  45.1 1.6 %collective-permute-start.10 = (bf16[144,1024]{1,0:T(8,128)(2,1)S(1)}, bf16[144,1024]{1,0:T(8,128)(2,1)S(1)}, u32[]{:S(2)}, u32[]{:S(2)}) collective-permute-start(bf16[144,1024]{1,0:T(8,128)(2,1)S(1)} %get-tuple-element.83.refs_1_), channel_id=1, source_target_pairs={{0,1},{1,0},{2,3},{3,2},{4,5},{5,4},{6,7},{7,6},{8,9},{9,8},{10,11... | collective-permute-start | bytes 884744 | tf_op jit(solution)/shard_map/ppermute | solution.py:534
  47.3 1.6 %collective-permute-start.9 = (bf16[144,1024]{1,0:T(8,128)(2,1)S(1)}, bf16[144,1024]{1,0:T(8,128)(2,1)S(1)}, u32[]{:S(2)}, u32[]{:S(2)}) collective-permute-start(bf16[144,1024]{1,0:T(8,128)(2,1)S(1)} %get-tuple-element.82.refs_1_), channel_id=1, source_target_pairs={{0,2},{1,3},{2,4},{3,5},{4,6},{5,7},{6,0},{7,1},{8,10},{9,11},{10,... | collective-permute-start | bytes 884744 | tf_op jit(solution)/shard_map/ppermute | solution.py:520
  50.0 2.6 %scan1.2 = (bf16[1,128,1024]{2,1,0:T(8,128)(2,1)S(1)}, f32[1,128,1024]{2,1,0:T(8,128)S(1)}, f32[8,128]{1,0:T(8,128)S(1)}) custom-call(s32[7]{0:T(128)S(1)} %stack.40.refs_0_, bf16[128,4096]{1,0:T(8,128)(2,1)S(1)} %hold.1.refs_1_, bf16[128,4096]{1,0:T(8,128)(2,1)S(1)} %collective-permute-done.5.refs_2_, f32[1,8,128]{2,1,0:T(8,128)S(1)} %get-tuple-element.84.refs_3_.refs_8_, ...), custom_call_target="tpu_custom_call" | custom-call | flops 115000000 | tf_op jit(solution)/shard_map/scan1/pallas_call | solution.py:448
  54.2 3.1 %collective-permute-done.9.refs_2_ = bf16[144,1024]{1,0:T(8,128)(2,1)S(1)} collective-permute-done((bf16[144,1024]{1,0:T(8,128)(2,1)S(1)}, bf16[144,1024]{1,0:T(8,128)(2,1)S(1)}, u32[]{:S(2)}, u32[]{:S(2)}) %collective-permute-start.9) | collective-permute-done | bytes 294944 | tf_op jit(solution)/shard_map/ppermute | solution.py:520
  58.0 1.3 %collective-permute-start.8 = (bf16[128,1024]{1,0:T(8,128)(2,1)S(1)}, bf16[128,1024]{1,0:T(8,128)(2,1)S(1)}, u32[]{:S(2)}, u32[]{:S(2)}) collective-permute-start(bf16[128,1024]{1,0:T(8,128)(2,1)S(1)} %get-tuple-element.81), channel_id=1, source_target_pairs={{0,2},{1,3},{2,4},{3,5},{4,6},{5,7},{6,0},{7,1},{8,10},{9,11},{10,... | collective-permute-start | bytes 786440 | tf_op jit(solution)/shard_map/ppermute | solution.py:520
  59.6 2.6 %scan1.3 = (bf16[1,128,1024]{2,1,0:T(8,128)(2,1)S(1)}, f32[1,128,1024]{2,1,0:T(8,128)S(1)}, f32[8,128]{1,0:T(8,128)S(1)}) custom-call(s32[7]{0:T(128)S(1)} %stack.40.refs_0_, bf16[128,4096]{1,0:T(8,128)(2,1)S(1)} %hold.1.refs_1_, bf16[128,4096]{1,0:T(8,128)(2,1)S(1)} %collective-permute-done.5.refs_2_, f32[1,8,128]{2,1,0:T(8,128)S(1)} %get-tuple-element.94.refs_3_.refs_8_, ...), custom_call_target="tpu_custom_call" | custom-call | flops 115000000 | tf_op jit(solution)/shard_map/scan1/pallas_call | solution.py:448
  62.3 6.7 %collective-permute-done.11.refs_3_ = bf16[128,1024]{1,0:T(8,128)(2,1)S(1)} collective-permute-done((bf16[128,1024]{1,0:T(8,128)(2,1)S(1)}, bf16[128,1024]{1,0:T(8,128)(2,1)S(1)}, u32[]{:S(2)}, u32[]{:S(2)}) %collective-permute-start.11) | collective-permute-done | bytes 262176 | tf_op jit(solution)/shard_map/ppermute | solution.py:520
  69.0 2.6 %out1.2 = (bf16[64,4096]{1,0:T(8,128)(2,1)S(1)}, bf16[64,1024]{1,0:T(8,128)(2,1)S(1)}, bf16[64,1024]{1,0:T(8,128)(2,1)S(1)}, bf16[64,1024]{1,0:T(8,128)(2,1)S(1)...) custom-call(s32[7]{0:T(128)S(1)} %stack.40.refs_0_, bf16[144,1024]{1,0:T(8,128)(2,1)S(1)} %get-tuple-element.77.refs_1_, ...), custom_call_target="tpu_custom_call" | custom-call | flops 115000000 | tf_op jit(solution)/shard_map/out1/pallas_call | solution.py:448
  72.3 2.3 %collective-permute-done.8.refs_3_ = bf16[128,1024]{1,0:T(8,128)(2,1)S(1)} collective-permute-done((bf16[128,1024]{1,0:T(8,128)(2,1)S(1)}, bf16[128,1024]{1,0:T(8,128)(2,1)S(1)}, u32[]{:S(2)}, u32[]{:S(2)}) %collective-permute-start.8) | collective-permute-done | bytes 262176 | tf_op jit(solution)/shard_map/ppermute | solution.py:520
  76.6 1.6 %collective-permute-start.23 = (bf16[64,4096]{1,0:T(8,128)(2,1)S(1)}, bf16[64,4096]{1,0:T(8,128)(2,1)S(1)}, u32[]{:S(2)}, u32[]{:S(2)}) collective-permute-start(bf16[64,4096]{1,0:T(8,128)(2,1)S(1)} %get-tuple-element.127), channel_id=1, source_target_pairs={{0,16},{8,24},{16,0},{24,8},{1,17},{9,25},{17,1},{25,9},{2,18},{10... | collective-permute-start | bytes 1572872 | tf_op jit(solution)/shard_map/ppermute | solution.py:539
  79.7 4.0 %scan2.1 = (bf16[2,128,1024]{2,1,0:T(8,128)(2,1)S(1)}, f32[2,128,1024]{2,1,0:T(8,128)S(1)}, f32[8,128]{1,0:T(8,128)S(1)}) custom-call(s32[7]{0:T(128)S(1)} %stack.40.refs_0_, bf16[128,4096]{1,0:T(8,128)(2,1)S(1)} %bitcast.24, bf16[128,4096]{1,0:T(8,128)(2,1)S(1)} %collective-permute-done.refs_2_, f32[2,8,128]{2,1,0:T(8,128)S(1)} %get-tuple-element.103.refs_3_.refs_7_, ...), custom_call_target="tpu_custom_call" | custom-call | flops 115000000 | tf_op jit(solution)/shard_map/scan2/pallas_call | solution.py:448
  83.7 2.6 %collective-permute-done.12.refs_11_.refs_2_ = bf16[128,1024]{1,0:T(8,128)(2,1)S(1)} collective-permute-done((bf16[128,1024]{1,0:T(8,128)(2,1)S(1)}, bf16[128,1024]{1,0:T(8,128)(2,1)S(1)}, u32[]{:S(2)}, u32[]{:S(2)}) %collective-permute-start.12) | collective-permute-done | bytes 262176 | tf_op jit(solution)/shard_map/ppermute | solution.py:534
  86.3 3.0 %collective-permute-done.18.refs_3_ = bf16[128,1024]{1,0:T(8,128)(2,1)S(1)} collective-permute-done((bf16[128,1024]{1,0:T(8,128)(2,1)S(1)}, bf16[128,1024]{1,0:T(8,128)(2,1)S(1)}, u32[]{:S(2)}, u32[]{:S(2)}) %collective-permute-start.18) | collective-permute-done | bytes 262176 | tf_op jit(solution)/shard_map/ppermute | solution.py:520
  89.2 2.6 %out1.3 = (bf16[64,4096]{1,0:T(8,128)(2,1)S(1)}, bf16[64,1024]{1,0:T(8,128)(2,1)S(1)}, bf16[64,1024]{1,0:T(8,128)(2,1)S(1)}, bf16[64,1024]{1,0:T(8,128)(2,1)S(1)...) custom-call(s32[7]{0:T(128)S(1)} %stack.40.refs_0_, bf16[144,1024]{1,0:T(8,128)(2,1)S(1)} %get-tuple-element.83.refs_1_, ...), custom_call_target="tpu_custom_call" | custom-call | flops 115000000 | tf_op jit(solution)/shard_map/out1/pallas_call | solution.py:448
  95.2 4.5 %out2.1 = (bf16[128,4096]{1,0:T(8,128)(2,1)S(1)}, bf16[128,4096]{1,0:T(8,128)(2,1)S(1)}, f32[8,128]{1,0:T(8,128)S(1)}) custom-call(s32[7]{0:T(128)S(1)} %stack.40.refs_0_, bf16[128,1024]{1,0:T(8,128)(2,1)S(1)} %get-tuple-element.101.refs_1_, bf16[128,1024]{1,0:T(8,128)(2,1)S(1)} %collective-permute-done.12.refs_11_.refs_2_, ...), custom_call_target="tpu_custom_call" | custom-call | flops 115000000 | tf_op jit(solution)/shard_map/out2/pallas_call | solution.py:448
  100.3 8.5 %collective-permute-done.25.refs_6_ = bf16[64,4096]{1,0:T(8,128)(2,1)S(1)} collective-permute-done((bf16[64,4096]{1,0:T(8,128)(2,1)S(1)}, bf16[64,4096]{1,0:T(8,128)(2,1)S(1)}, u32[]{:S(2)}, u32[]{:S(2)}) %collective-permute-start.25) | collective-permute-done | bytes 524320 | tf_op jit(solution)/shard_map/ppermute | solution.py:539
  109.5 1.2 %collective-permute-done.27.refs_8_ = bf16[64,4096]{1,0:T(8,128)(2,1)S(1)} collective-permute-done((bf16[64,4096]{1,0:T(8,128)(2,1)S(1)}, bf16[64,4096]{1,0:T(8,128)(2,1)S(1)}, u32[]{:S(2)}, u32[]{:S(2)}) %collective-permute-start.27) | collective-permute-done | bytes 524320 | tf_op jit(solution)/shard_map/ppermute | solution.py:534
  110.8 2.3 %close.1 = (bf16[128,4096]{1,0:T(8,128)(2,1)}, f32[8,128]{1,0:T(8,128)}) custom-call(s32[7]{0:T(128)S(1)} %stack.40.refs_0_, f32[1]{0:T(128)S(6)} %copy.19.refs_1_, bf16[128,4096]{1,0:T(8,128)(2,1)S(1)} %bitcast.25, bf16[128,4096]{1,0:T(8,128)(2,1)S(1)} %get-tuple-element.130.refs_3_, bf16[128,4096]{1,0:T(8,128)(2,1)S(1)} %collective-permute-done.24.refs_4_, ...), custom_call_target="tpu_custom_call" | custom-call | flops 1150000000 | tf_op jit(solution)/shard_map/close/pallas_call | solution.py:448
  (88 shorter events, 15.3 us)
Async XLA Ops:
  0.0 3.1 %collective-permute-start = (bf16[128,4096]{1,0:T(8,128)(2,1)}, bf16[128,4096]{1,0:T(8,128)(2,1)S(1)}, u32[]{:S(2)}, u32[]{:S(2)}) collective-permute-start(bf16[128,4096]{1,0:T(8,128)(2,1)} %bitcast.20), channel_id=1, source_target_pairs={{0,8},{8,0},{16,24},{24,16},{1,9},{9,1},{17,25},{25,17},{2,10},{10... | collective-permute-start | bytes 3145736 | tf_op jit(solution)/shard_map/ppermute | solution.py:534
  0.5 28.0 %collective-permute-start.4 = (bf16[128,4096]{1,0:T(8,128)(2,1)}, bf16[128,4096]{1,0:T(8,128)(2,1)S(1)}, u32[]{:S(2)}, u32[]{:S(2)}) collective-permute-start(bf16[128,4096]{1,0:T(8,128)(2,1)} %bitcast.21), channel_id=1, source_target_pairs={{0,16},{8,24},{16,0},{24,8},{1,17},{9,25},{17,1},{25,9},{2,18},{10... | collective-permute-start | bytes 3145736 | tf_op jit(solution)/shard_map/ppermute | solution.py:539
  5.6 8.2 %collective-permute-start.1 = (bf16[16,2048]{1,0:T(8,128)(2,1)S(1)}, bf16[16,2048]{1,0:T(8,128)(2,1)S(1)}, u32[]{:S(2)}, u32[]{:S(2)}) collective-permute-start(bf16[16,2048]{1,0:T(8,128)(2,1)S(1)} %get-tuple-element.70), channel_id=1, source_target_pairs={{0,1},{1,2},{2,3},{3,4},{4,5},{5,6},{6,7},{7,0},{8,9},{9,10},{10,1... | collective-permute-start | bytes 196616 | tf_op jit(solution)/shard_map/ppermute | solution.py:530
  8.4 7.9 %collective-permute-start.2 = (bf16[16,2048]{1,0:T(8,128)(2,1)S(1)}, bf16[16,2048]{1,0:T(8,128)(2,1)S(1)}, u32[]{:S(2)}, u32[]{:S(2)}) collective-permute-start(bf16[16,2048]{1,0:T(8,128)(2,1)S(1)} %get-tuple-element.70), channel_id=1, source_target_pairs={{16,1},{17,2},{18,3},{19,4},{20,5},{21,6},{22,7},{23,0},{24,9},{25... | collective-permute-start | bytes 196616 | tf_op jit(solution)/shard_map/ppermute | solution.py:530
  28.4 2.7 %collective-permute-start.5 = (bf16[128,4096]{1,0:T(8,128)(2,1)S(1)}, bf16[128,4096]{1,0:T(8,128)(2,1)S(1)}, u32[]{:S(2)}, u32[]{:S(2)}) collective-permute-start(bf16[128,4096]{1,0:T(8,128)(2,1)S(1)} %hold.1.refs_1_), channel_id=1, source_target_pairs={{0,8},{8,0},{16,24},{24,16},{1,9},{9,1},{17,25},{25,17},{2,10},{10... | collective-permute-start | bytes 3145736 | tf_op jit(solution)/shard_map/ppermute | solution.py:534
  28.4 9.4 %collective-permute-start.3 = (bf16[144,1024]{1,0:T(8,128)(2,1)S(1)}, bf16[144,1024]{1,0:T(8,128)(2,1)S(1)}, u32[]{:S(2)}, u32[]{:S(2)}) collective-permute-start(bf16[144,1024]{1,0:T(8,128)(2,1)S(1)} %get-tuple-element.73), channel_id=1, source_target_pairs={{0,1},{1,0},{2,3},{3,2},{4,5},{5,4},{6,7},{7,6},{8,9},{9,8},{10,11... | collective-permute-start | bytes 884744 | tf_op jit(solution)/shard_map/ppermute | solution.py:534
  31.1 18.9 %slice-start = ((s8[8388608]{0:T(1024)(128)(4,1)}), s8[4194304]{0:T(1024)(128)(4,1)S(1)}, s32[]{:S(2)}) async-start(s8[8388608]{0:T(1024)(128)(4,1)} %bitcast.16), calls=%async_computation | async-start | bytes 8388608
  35.6 11.0 %collective-permute-start.7 = (bf16[144,1024]{1,0:T(8,128)(2,1)S(1)}, bf16[144,1024]{1,0:T(8,128)(2,1)S(1)}, u32[]{:S(2)}, u32[]{:S(2)}) collective-permute-start(bf16[144,1024]{1,0:T(8,128)(2,1)S(1)} %get-tuple-element.77.refs_1_), channel_id=1, source_target_pairs={{0,1},{1,0},{2,3},{3,2},{4,5},{5,4},{6,7},{7,6},{8,9},{9,8},{10,11... | collective-permute-start | bytes 884744 | tf_op jit(solution)/shard_map/ppermute | solution.py:534
  38.5 10.8 %collective-permute-start.6 = (bf16[144,1024]{1,0:T(8,128)(2,1)S(1)}, bf16[144,1024]{1,0:T(8,128)(2,1)S(1)}, u32[]{:S(2)}, u32[]{:S(2)}) collective-permute-start(bf16[144,1024]{1,0:T(8,128)(2,1)S(1)} %get-tuple-element.76.refs_1_), channel_id=1, source_target_pairs={{0,2},{1,3},{2,4},{3,5},{4,6},{5,7},{6,0},{7,1},{8,10},{9,11},{10,... | collective-permute-start | bytes 884744 | tf_op jit(solution)/shard_map/ppermute | solution.py:520
  45.1 8.4 %collective-permute-start.10 = (bf16[144,1024]{1,0:T(8,128)(2,1)S(1)}, bf16[144,1024]{1,0:T(8,128)(2,1)S(1)}, u32[]{:S(2)}, u32[]{:S(2)}) collective-permute-start(bf16[144,1024]{1,0:T(8,128)(2,1)S(1)} %get-tuple-element.83.refs_1_), channel_id=1, source_target_pairs={{0,1},{1,0},{2,3},{3,2},{4,5},{5,4},{6,7},{7,6},{8,9},{9,8},{10,11... | collective-permute-start | bytes 884744 | tf_op jit(solution)/shard_map/ppermute | solution.py:534
  47.3 9.9 %collective-permute-start.9 = (bf16[144,1024]{1,0:T(8,128)(2,1)S(1)}, bf16[144,1024]{1,0:T(8,128)(2,1)S(1)}, u32[]{:S(2)}, u32[]{:S(2)}) collective-permute-start(bf16[144,1024]{1,0:T(8,128)(2,1)S(1)} %get-tuple-element.82.refs_1_), channel_id=1, source_target_pairs={{0,2},{1,3},{2,4},{3,5},{4,6},{5,7},{6,0},{7,1},{8,10},{9,11},{10,... | collective-permute-start | bytes 884744 | tf_op jit(solution)/shard_map/ppermute | solution.py:520
  50.0 19.0 %slice-start.2 = ((s8[8388608]{0:T(1024)(128)(4,1)}), s8[4194304]{0:T(1024)(128)(4,1)S(1)}, s32[]{:S(2)}) async-start(s8[8388608]{0:T(1024)(128)(4,1)} %bitcast.18), calls=%async_computation.2 | async-start | bytes 8388608
  52.6 16.4 %copy-start.2 = (f32[1024]{0:T(1024)S(1)}, f32[1024]{0:T(1024)}, u32[]{:S(2)}) copy-start(f32[1024]{0:T(1024)} %param.29) | copy-start | bytes 12292
  57.3 11.7 %slice-start.3 = ((s8[8388608]{0:T(1024)(128)(4,1)}), s8[4194304]{0:T(1024)(128)(4,1)S(1)}, s32[]{:S(2)}) async-start(s8[8388608]{0:T(1024)(128)(4,1)} %bitcast.18), calls=%async_computation.3 | async-start | bytes 8388608
  57.9 11.1 %collective-permute-start.11 = (bf16[128,1024]{1,0:T(8,128)(2,1)S(1)}, bf16[128,1024]{1,0:T(8,128)(2,1)S(1)}, u32[]{:S(2)}, u32[]{:S(2)}) collective-permute-start(bf16[128,1024]{1,0:T(8,128)(2,1)S(1)} %get-tuple-element.91), channel_id=1, source_target_pairs={{0,2},{1,3},{2,4},{3,5},{4,6},{5,7},{6,0},{7,1},{8,10},{9,11},{10,... | collective-permute-start | bytes 786440 | tf_op jit(solution)/shard_map/ppermute | solution.py:520
  58.0 16.6 %collective-permute-start.8 = (bf16[128,1024]{1,0:T(8,128)(2,1)S(1)}, bf16[128,1024]{1,0:T(8,128)(2,1)S(1)}, u32[]{:S(2)}, u32[]{:S(2)}) collective-permute-start(bf16[128,1024]{1,0:T(8,128)(2,1)S(1)} %get-tuple-element.81), channel_id=1, source_target_pairs={{0,2},{1,3},{2,4},{3,5},{4,6},{5,7},{6,0},{7,1},{8,10},{9,11},{10,... | collective-permute-start | bytes 786440 | tf_op jit(solution)/shard_map/ppermute | solution.py:520
  59.3 19.4 %collective-permute-start.13 = (bf16[144,1024]{1,0:T(8,128)(2,1)S(1)}, bf16[144,1024]{1,0:T(8,128)(2,1)S(1)}, u32[]{:S(2)}, u32[]{:S(2)}) collective-permute-start(bf16[144,1024]{1,0:T(8,128)(2,1)S(1)} %get-tuple-element.107.refs_1_), channel_id=1, source_target_pairs={{0,2},{1,3},{2,4},{3,5},{4,6},{5,7},{6,0},{7,1},{8,10},{9,11},{10,... | collective-permute-start | bytes 884744 | tf_op jit(solution)/shard_map/ppermute | solution.py:520
  71.6 3.7 %collective-permute-start.14 = (bf16[64,1024]{1,0:T(8,128)(2,1)S(1)}, bf16[64,1024]{1,0:T(8,128)(2,1)S(1)}, u32[]{:S(2)}, u32[]{:S(2)}) collective-permute-start(bf16[64,1024]{1,0:T(8,128)(2,1)S(1)} %get-tuple-element.109), channel_id=1, source_target_pairs={{0,8},{8,0},{16,24},{24,16},{1,9},{9,1},{17,25},{25,17},{2,10},{10... | collective-permute-start | bytes 393224 | tf_op jit(solution)/shard_map/ppermute | solution.py:534
  71.7 3.7 %collective-permute-start.15 = (bf16[64,1024]{1,0:T(8,128)(2,1)S(1)}, bf16[64,1024]{1,0:T(8,128)(2,1)S(1)}, u32[]{:S(2)}, u32[]{:S(2)}) collective-permute-start(bf16[64,1024]{1,0:T(8,128)(2,1)S(1)} %get-tuple-element.110), channel_id=1, source_target_pairs={{0,8},{8,0},{16,24},{24,16},{1,9},{9,1},{17,25},{25,17},{2,10},{10... | collective-permute-start | bytes 393224 | tf_op jit(solution)/shard_map/ppermute | solution.py:534
  72.2 3.2 %collective-permute-start.16 = (bf16[64,1024]{1,0:T(8,128)(2,1)S(1)}, bf16[64,1024]{1,0:T(8,128)(2,1)S(1)}, u32[]{:S(2)}, u32[]{:S(2)}) collective-permute-start(bf16[64,1024]{1,0:T(8,128)(2,1)S(1)} %get-tuple-element.111), channel_id=1, source_target_pairs={{0,8},{8,0},{16,24},{24,16},{1,9},{9,1},{17,25},{25,17},{2,10},{10... | collective-permute-start | bytes 393224 | tf_op jit(solution)/shard_map/ppermute | solution.py:534
  74.6 1.3 %collective-permute-start.17 = (bf16[64,1024]{1,0:T(8,128)(2,1)S(1)}, bf16[64,1024]{1,0:T(8,128)(2,1)S(1)}, u32[]{:S(2)}, u32[]{:S(2)}) collective-permute-start(bf16[64,1024]{1,0:T(8,128)(2,1)S(1)} %get-tuple-element.112), channel_id=1, source_target_pairs={{0,8},{8,0},{16,24},{24,16},{1,9},{9,1},{17,25},{25,17},{2,10},{10... | collective-permute-start | bytes 393224 | tf_op jit(solution)/shard_map/ppermute | solution.py:534
  76.6 17.4 %collective-permute-start.23 = (bf16[64,4096]{1,0:T(8,128)(2,1)S(1)}, bf16[64,4096]{1,0:T(8,128)(2,1)S(1)}, u32[]{:S(2)}, u32[]{:S(2)}) collective-permute-start(bf16[64,4096]{1,0:T(8,128)(2,1)S(1)} %get-tuple-element.127), channel_id=1, source_target_pairs={{0,16},{8,24},{16,0},{24,8},{1,17},{9,25},{17,1},{25,9},{2,18},{10... | collective-permute-start | bytes 1572872 | tf_op jit(solution)/shard_map/ppermute | solution.py:539
  78.2 8.1 %collective-permute-start.12 = (bf16[128,1024]{1,0:T(8,128)(2,1)S(1)}, bf16[128,1024]{1,0:T(8,128)(2,1)S(1)}, u32[]{:S(2)}, u32[]{:S(2)}) collective-permute-start(bf16[128,1024]{1,0:T(8,128)(2,1)S(1)} %get-tuple-element.102), channel_id=1, source_target_pairs={{0,1},{1,0},{2,3},{3,2},{4,5},{5,4},{6,7},{7,6},{8,9},{9,8},{10,11... | collective-permute-start | bytes 786440 | tf_op jit(solution)/shard_map/ppermute | solution.py:534
  79.4 9.9 %collective-permute-start.18 = (bf16[128,1024]{1,0:T(8,128)(2,1)S(1)}, bf16[128,1024]{1,0:T(8,128)(2,1)S(1)}, u32[]{:S(2)}, u32[]{:S(2)}) collective-permute-start(bf16[128,1024]{1,0:T(8,128)(2,1)S(1)} %get-tuple-element.118), channel_id=1, source_target_pairs={{0,2},{1,3},{2,4},{3,5},{4,6},{5,7},{6,0},{7,1},{8,10},{9,11},{10,... | collective-permute-start | bytes 786440 | tf_op jit(solution)/shard_map/ppermute | solution.py:520
  91.9 1.4 %collective-permute-start.19 = (bf16[64,1024]{1,0:T(8,128)(2,1)S(1)}, bf16[64,1024]{1,0:T(8,128)(2,1)S(1)}, u32[]{:S(2)}, u32[]{:S(2)}) collective-permute-start(bf16[64,1024]{1,0:T(8,128)(2,1)S(1)} %get-tuple-element.123), channel_id=1, source_target_pairs={{0,8},{8,0},{16,24},{24,16},{1,9},{9,1},{17,25},{25,17},{2,10},{10... | collective-permute-start | bytes 393224 | tf_op jit(solution)/shard_map/ppermute | solution.py:534
  92.0 1.5 %collective-permute-start.20 = (bf16[64,1024]{1,0:T(8,128)(2,1)S(1)}, bf16[64,1024]{1,0:T(8,128)(2,1)S(1)}, u32[]{:S(2)}, u32[]{:S(2)}) collective-permute-start(bf16[64,1024]{1,0:T(8,128)(2,1)S(1)} %get-tuple-element.124), channel_id=1, source_target_pairs={{0,8},{8,0},{16,24},{24,16},{1,9},{9,1},{17,25},{25,17},{2,10},{10... | collective-permute-start | bytes 393224 | tf_op jit(solution)/shard_map/ppermute | solution.py:534
  92.4 1.3 %collective-permute-start.21 = (bf16[64,1024]{1,0:T(8,128)(2,1)S(1)}, bf16[64,1024]{1,0:T(8,128)(2,1)S(1)}, u32[]{:S(2)}, u32[]{:S(2)}) collective-permute-start(bf16[64,1024]{1,0:T(8,128)(2,1)S(1)} %get-tuple-element.125), channel_id=1, source_target_pairs={{0,8},{8,0},{16,24},{24,16},{1,9},{9,1},{17,25},{25,17},{2,10},{10... | collective-permute-start | bytes 393224 | tf_op jit(solution)/shard_map/ppermute | solution.py:534
  92.5 1.5 %collective-permute-start.22 = (bf16[64,1024]{1,0:T(8,128)(2,1)S(1)}, bf16[64,1024]{1,0:T(8,128)(2,1)S(1)}, u32[]{:S(2)}, u32[]{:S(2)}) collective-permute-start(bf16[64,1024]{1,0:T(8,128)(2,1)S(1)} %get-tuple-element.126), channel_id=1, source_target_pairs={{0,8},{8,0},{16,24},{24,16},{1,9},{9,1},{17,25},{25,17},{2,10},{10... | collective-permute-start | bytes 393224 | tf_op jit(solution)/shard_map/ppermute | solution.py:534
  94.7 14.2 %collective-permute-start.25 = (bf16[64,4096]{1,0:T(8,128)(2,1)S(1)}, bf16[64,4096]{1,0:T(8,128)(2,1)S(1)}, u32[]{:S(2)}, u32[]{:S(2)}) collective-permute-start(bf16[64,4096]{1,0:T(8,128)(2,1)S(1)} %get-tuple-element.132), channel_id=1, source_target_pairs={{0,16},{8,24},{16,0},{24,8},{1,17},{9,25},{17,1},{25,9},{2,18},{10... | collective-permute-start | bytes 1572872 | tf_op jit(solution)/shard_map/ppermute | solution.py:539
  99.8 11.0 %collective-permute-start.24 = (bf16[128,4096]{1,0:T(8,128)(2,1)S(1)}, bf16[128,4096]{1,0:T(8,128)(2,1)S(1)}, u32[]{:S(2)}, u32[]{:S(2)}) collective-permute-start(bf16[128,4096]{1,0:T(8,128)(2,1)S(1)} %get-tuple-element.131), channel_id=1, source_target_pairs={{0,8},{8,0},{16,24},{24,16},{1,9},{9,1},{17,25},{25,17},{2,10},{10... | collective-permute-start | bytes 3145736 | tf_op jit(solution)/shard_map/ppermute | solution.py:534
  99.9 9.7 %collective-permute-start.26 = (bf16[64,4096]{1,0:T(8,128)(2,1)S(1)}, bf16[64,4096]{1,0:T(8,128)(2,1)S(1)}, u32[]{:S(2)}, u32[]{:S(2)}) collective-permute-start(bf16[64,4096]{1,0:T(8,128)(2,1)S(1)} %collective-permute-done.23.refs_6_.refs_5_), channel_id=1, source_target_pairs={{0,8},{8,0},{16,24},{24,16},{1,9},{9,1},{17,25},{25,17},{2,10},{10... | collective-permute-start | bytes 1572872 | tf_op jit(solution)/shard_map/ppermute | solution.py:534
  108.9 1.9 %collective-permute-start.27 = (bf16[64,4096]{1,0:T(8,128)(2,1)S(1)}, bf16[64,4096]{1,0:T(8,128)(2,1)S(1)}, u32[]{:S(2)}, u32[]{:S(2)}) collective-permute-start(bf16[64,4096]{1,0:T(8,128)(2,1)S(1)} %collective-permute-done.25.refs_6_), channel_id=1, source_target_pairs={{0,8},{8,0},{16,24},{24,16},{1,9},{9,1},{17,25},{25,17},{2,10},{10... | collective-permute-start | bytes 1572872 | tf_op jit(solution)/shard_map/ppermute | solution.py:534
  (15 other events, 136.2 us)

commit v5 on v4

--- a/solution.py
+++ b/solution.py
@@ -14,7 +14,7 @@
 TAIL = 8
 TAILS = 16
 WIDE = 256
-PIECES = 4
+PIECES = 2
 FACTOR_ROWS = 16
 
 epsilon = 1e-05

time: 113 us -> 111 us (0.982)
  waiting for transfers between devices: 41.6 us -> 38.8 us
    ppermute x17 -> x13, waiting for transfers between devices: 7.7 us -> 4.93 us  [partner(): lax.ppermute(block, axis, [(i, i ^ 1) for i in range(lax.axis_size(axis))])]
    ppermute x3, waiting for transfers between devices: 13.1 us -> 11.8 us  [over(): lax.ppermute(block, 'fsdp', [(i, (i + 2 * distance) % size) for i in rang...]
    ppermute x6, waiting for transfers between devices: 15.4 us -> 16.6 us  [along(): lax.ppermute(block, 'ctx', [(i, (i + distance) % spans) for i in range(sp...]
    ppermute x17 -> x13, starting transfers between devices: 8.35 us -> 7.81 us  [partner(): lax.ppermute(block, axis, [(i, i ^ 1) for i in range(lax.axis_size(axis))])]
  transfers between devices with their start and end apart: 28 -> 24, of which waited for: 19 -> 16; matrix products, arithmetic and copies ran while one was open for 0% -> 0% of each run, Pallas kernels for 36% -> 37%
where the time goes in v5:
time: 111 us
  Pallas kernels  44.4 us (40%)
  waiting for transfers between devices  38.8 us (35%)
  starting transfers between devices  24.3 us (22%)
  local copies, waits for them, and re-layouts  2.15 us (2%)
    pallas_call x20, Pallas kernels, run(): pl.pallas_call(ordered, in_specs=[IN_SMEM] * (1 + len(scalars)) + [IN_VME...  44.4 us
    ppermute x6, waiting for transfers between devices, along(): lax.ppermute(block, 'ctx', [(i, (i + distance) % spans) for i in range(sp...  16.6 us
    ppermute x3, waiting for transfers between devices, over(): lax.ppermute(block, 'fsdp', [(i, (i + 2 * distance) % size) for i in rang...  11.8 us
    ppermute x13, starting transfers between devices, partner(): lax.ppermute(block, axis, [(i, i ^ 1) for i in range(lax.axis_size(axis))])  7.81 us
    ppermute x3, starting transfers between devices, over(): lax.ppermute(block, 'fsdp', [(i, (i + 2 * distance) % size) for i in rang...  5.69 us
    ppermute x6, starting transfers between devices, along(): lax.ppermute(block, 'ctx', [(i, (i + distance) % spans) for i in range(sp...  5.47 us
    ppermute x2, waiting for transfers between devices, tail_from(): return lax.ppermute(block, ('fsdp', 'ctx'), route)  5.42 us
    ppermute x2, starting transfers between devices, tail_from(): return lax.ppermute(block, ('fsdp', 'ctx'), route)  5.31 us
  transfers between devices with their start and end apart: 24, of which 16 were waited for; matrix products, arithmetic and copies ran while one was open for 0% of the time, Pallas kernels for 37%

profile of v5, /device:TPU:0, one launch (start us, length us, event | category | flops | bytes accessed | tf_op | source)
XLA Modules:
  0.0 110.7 jit_solution(16712476663164121739)
XLA Ops:
  0.5 2.5 %collective-permute-start.4 = (bf16[128,4096]{1,0:T(8,128)(2,1)}, bf16[128,4096]{1,0:T(8,128)(2,1)S(1)}, u32[]{:S(2)}, u32[]{:S(2)}) collective-permute-start(bf16[128,4096]{1,0:T(8,128)(2,1)} %bitcast.21), channel_id=1, source_target_pairs={{0,16},{8,24},{16,0},{24,8},{1,17},{9,25},{17,1},{25,9},{2,18},{10... | collective-permute-start | bytes 3145736 | tf_op jit(solution)/shard_map/ppermute | solution.py:539
  3.1 1.2 %copy-done = bf16[1,128,4096]{2,1,0:T(8,128)(2,1)S(1)} copy-done((bf16[1,128,4096]{2,1,0:T(8,128)(2,1)S(1)}, bf16[1,128,4096]{2,1,0:T(8,128)(2,1)}, u32[]{:S(2)}) %copy-start) | copy-done | bytes 1048600
  5.6 2.8 %collective-permute-start.1 = (bf16[16,2048]{1,0:T(8,128)(2,1)S(1)}, bf16[16,2048]{1,0:T(8,128)(2,1)S(1)}, u32[]{:S(2)}, u32[]{:S(2)}) collective-permute-start(bf16[16,2048]{1,0:T(8,128)(2,1)S(1)} %get-tuple-element.66), channel_id=1, source_target_pairs={{0,1},{1,2},{2,3},{3,4},{4,5},{5,6},{6,7},{7,0},{8,9},{9,10},{10,1... | collective-permute-start | bytes 196616 | tf_op jit(solution)/shard_map/ppermute | solution.py:530
  8.4 2.5 %collective-permute-start.2 = (bf16[16,2048]{1,0:T(8,128)(2,1)S(1)}, bf16[16,2048]{1,0:T(8,128)(2,1)S(1)}, u32[]{:S(2)}, u32[]{:S(2)}) collective-permute-start(bf16[16,2048]{1,0:T(8,128)(2,1)S(1)} %get-tuple-element.66), channel_id=1, source_target_pairs={{16,1},{17,2},{18,3},{19,4},{20,5},{21,6},{22,7},{23,0},{24,9},{25... | collective-permute-start | bytes 196616 | tf_op jit(solution)/shard_map/ppermute | solution.py:530
  11.0 2.9 %collective-permute-done.1.refs_3_ = bf16[16,2048]{1,0:T(8,128)(2,1)S(1)} collective-permute-done((bf16[16,2048]{1,0:T(8,128)(2,1)S(1)}, bf16[16,2048]{1,0:T(8,128)(2,1)S(1)}, u32[]{:S(2)}, u32[]{:S(2)}) %collective-permute-start.1) | collective-permute-done | bytes 65568 | tf_op jit(solution)/shard_map/ppermute | solution.py:530
  13.9 2.5 %collective-permute-done.2.refs_4_.refs_3_ = bf16[16,2048]{1,0:T(8,128)(2,1)S(1)} collective-permute-done((bf16[16,2048]{1,0:T(8,128)(2,1)S(1)}, bf16[16,2048]{1,0:T(8,128)(2,1)S(1)}, u32[]{:S(2)}, u32[]{:S(2)}) %collective-permute-start.2) | collective-permute-done | bytes 65568 | tf_op jit(solution)/shard_map/ppermute | solution.py:530
  16.5 7.4 %mix2.1 = (bf16[2,128,1024]{2,1,0:T(8,128)(2,1)S(1)}, bf16[2,128,512]{2,1,0:T(8,128)(2,1)S(1)}, f32[2,4,8,128]{3,2,1,0:T(8,128)S(1)}, f32[2,8,128]{2,1,0:T(8,128...) custom-call(s32[7]{0:T(128)S(1)} %stack.40.refs_0_, ...), custom_call_target="tpu_custom_call" | custom-call | flops 9200000000 | tf_op jit(solution)/shard_map/mix2/pallas_call | solution.py:448
  23.9 4.5 %collective-permute-done.4.block_ref = bf16[128,4096]{1,0:T(8,128)(2,1)S(1)} collective-permute-done((bf16[128,4096]{1,0:T(8,128)(2,1)}, bf16[128,4096]{1,0:T(8,128)(2,1)S(1)}, u32[]{:S(2)}, u32[]{:S(2)}) %collective-permute-start.4) | collective-permute-done | bytes 1048608 | tf_op jit(solution)/shard_map/ppermute | solution.py:539
  28.4 1.7 %collective-permute-start.3 = (bf16[144,1024]{1,0:T(8,128)(2,1)S(1)}, bf16[144,1024]{1,0:T(8,128)(2,1)S(1)}, u32[]{:S(2)}, u32[]{:S(2)}) collective-permute-start(bf16[144,1024]{1,0:T(8,128)(2,1)S(1)} %get-tuple-element.69), channel_id=1, source_target_pairs={{0,1},{1,0},{2,3},{3,2},{4,5},{5,4},{6,7},{7,6},{8,9},{9,8},{10,11... | collective-permute-start | bytes 884744 | tf_op jit(solution)/shard_map/ppermute | solution.py:534
  31.1 4.5 %mix1.2 = (bf16[1,128,1024]{2,1,0:T(8,128)(2,1)S(1)}, bf16[1,128,512]{2,1,0:T(8,128)(2,1)S(1)}, f32[1,4,8,128]{3,2,1,0:T(8,128)S(1)}, f32[1,8,128]{2,1,0:T(8,128...) custom-call(s32[7]{0:T(128)S(1)} %stack.40.refs_0_, bf16[128,4096]{1,0:T(8,128)(2,1)S(1)} %hold.1.refs_1_, ...), custom_call_target="tpu_custom_call" | custom-call | flops 4600000000 | tf_op jit(solution)/shard_map/mix1/pallas_call | solution.py:448
  35.6 1.8 %collective-permute-start.7 = (bf16[144,1024]{1,0:T(8,128)(2,1)S(1)}, bf16[144,1024]{1,0:T(8,128)(2,1)S(1)}, u32[]{:S(2)}, u32[]{:S(2)}) collective-permute-start(bf16[144,1024]{1,0:T(8,128)(2,1)S(1)} %get-tuple-element.73.refs_1_), channel_id=1, source_target_pairs={{0,1},{1,0},{2,3},{3,2},{4,5},{5,4},{6,7},{7,6},{8,9},{9,8},{10,11... | collective-permute-start | bytes 884744 | tf_op jit(solution)/shard_map/ppermute | solution.py:534
  38.5 1.9 %collective-permute-start.6 = (bf16[144,1024]{1,0:T(8,128)(2,1)S(1)}, bf16[144,1024]{1,0:T(8,128)(2,1)S(1)}, u32[]{:S(2)}, u32[]{:S(2)}) collective-permute-start(bf16[144,1024]{1,0:T(8,128)(2,1)S(1)} %get-tuple-element.72.refs_1_), channel_id=1, source_target_pairs={{0,2},{1,3},{2,4},{3,5},{4,6},{5,7},{6,0},{7,1},{8,10},{9,11},{10,... | collective-permute-start | bytes 884744 | tf_op jit(solution)/shard_map/ppermute | solution.py:520
  40.4 4.7 %mix1.3 = (bf16[1,128,1024]{2,1,0:T(8,128)(2,1)S(1)}, bf16[1,128,512]{2,1,0:T(8,128)(2,1)S(1)}, f32[1,4,8,128]{3,2,1,0:T(8,128)S(1)}, f32[1,8,128]{2,1,0:T(8,128...) custom-call(s32[7]{0:T(128)S(1)} %stack.40.refs_0_, bf16[128,4096]{1,0:T(8,128)(2,1)S(1)} %hold.1.refs_1_, ...), custom_call_target="tpu_custom_call" | custom-call | flops 4600000000 | tf_op jit(solution)/shard_map/mix1/pallas_call | solution.py:448
  45.1 1.6 %collective-permute-start.10 = (bf16[144,1024]{1,0:T(8,128)(2,1)S(1)}, bf16[144,1024]{1,0:T(8,128)(2,1)S(1)}, u32[]{:S(2)}, u32[]{:S(2)}) collective-permute-start(bf16[144,1024]{1,0:T(8,128)(2,1)S(1)} %get-tuple-element.79.refs_1_), channel_id=1, source_target_pairs={{0,1},{1,0},{2,3},{3,2},{4,5},{5,4},{6,7},{7,6},{8,9},{9,8},{10,11... | collective-permute-start | bytes 884744 | tf_op jit(solution)/shard_map/ppermute | solution.py:534
  47.3 1.6 %collective-permute-start.9 = (bf16[144,1024]{1,0:T(8,128)(2,1)S(1)}, bf16[144,1024]{1,0:T(8,128)(2,1)S(1)}, u32[]{:S(2)}, u32[]{:S(2)}) collective-permute-start(bf16[144,1024]{1,0:T(8,128)(2,1)S(1)} %get-tuple-element.78.refs_1_), channel_id=1, source_target_pairs={{0,2},{1,3},{2,4},{3,5},{4,6},{5,7},{6,0},{7,1},{8,10},{9,11},{10,... | collective-permute-start | bytes 884744 | tf_op jit(solution)/shard_map/ppermute | solution.py:520
  50.0 2.6 %scan1.2 = (bf16[1,128,1024]{2,1,0:T(8,128)(2,1)S(1)}, f32[1,128,1024]{2,1,0:T(8,128)S(1)}, f32[8,128]{1,0:T(8,128)S(1)}) custom-call(s32[7]{0:T(128)S(1)} %stack.40.refs_0_, bf16[128,4096]{1,0:T(8,128)(2,1)S(1)} %hold.1.refs_1_, bf16[128,4096]{1,0:T(8,128)(2,1)S(1)} %collective-permute-done.5.refs_2_, f32[1,8,128]{2,1,0:T(8,128)S(1)} %get-tuple-element.80.refs_3_.refs_8_, ...), custom_call_target="tpu_custom_call" | custom-call | flops 115000000 | tf_op jit(solution)/shard_map/scan1/pallas_call | solution.py:448
  54.2 3.1 %collective-permute-done.9.refs_2_ = bf16[144,1024]{1,0:T(8,128)(2,1)S(1)} collective-permute-done((bf16[144,1024]{1,0:T(8,128)(2,1)S(1)}, bf16[144,1024]{1,0:T(8,128)(2,1)S(1)}, u32[]{:S(2)}, u32[]{:S(2)}) %collective-permute-start.9) | collective-permute-done | bytes 294944 | tf_op jit(solution)/shard_map/ppermute | solution.py:520
  58.0 1.3 %collective-permute-start.8 = (bf16[128,1024]{1,0:T(8,128)(2,1)S(1)}, bf16[128,1024]{1,0:T(8,128)(2,1)S(1)}, u32[]{:S(2)}, u32[]{:S(2)}) collective-permute-start(bf16[128,1024]{1,0:T(8,128)(2,1)S(1)} %get-tuple-element.77), channel_id=1, source_target_pairs={{0,2},{1,3},{2,4},{3,5},{4,6},{5,7},{6,0},{7,1},{8,10},{9,11},{10,... | collective-permute-start | bytes 786440 | tf_op jit(solution)/shard_map/ppermute | solution.py:520
  59.6 2.6 %scan1.3 = (bf16[1,128,1024]{2,1,0:T(8,128)(2,1)S(1)}, f32[1,128,1024]{2,1,0:T(8,128)S(1)}, f32[8,128]{1,0:T(8,128)S(1)}) custom-call(s32[7]{0:T(128)S(1)} %stack.40.refs_0_, bf16[128,4096]{1,0:T(8,128)(2,1)S(1)} %hold.1.refs_1_, bf16[128,4096]{1,0:T(8,128)(2,1)S(1)} %collective-permute-done.5.refs_2_, f32[1,8,128]{2,1,0:T(8,128)S(1)} %get-tuple-element.90.refs_3_.refs_8_, ...), custom_call_target="tpu_custom_call" | custom-call | flops 115000000 | tf_op jit(solution)/shard_map/scan1/pallas_call | solution.py:448
  62.3 6.7 %collective-permute-done.11.refs_3_ = bf16[128,1024]{1,0:T(8,128)(2,1)S(1)} collective-permute-done((bf16[128,1024]{1,0:T(8,128)(2,1)S(1)}, bf16[128,1024]{1,0:T(8,128)(2,1)S(1)}, u32[]{:S(2)}, u32[]{:S(2)}) %collective-permute-start.11) | collective-permute-done | bytes 262176 | tf_op jit(solution)/shard_map/ppermute | solution.py:520
  69.0 2.6 %out1.2 = (bf16[64,4096]{1,0:T(8,128)(2,1)S(1)}, bf16[64,2048]{1,0:T(8,128)(2,1)S(1)}, bf16[64,2048]{1,0:T(8,128)(2,1)S(1)}, f32[8,128]{1,0:T(8,128)S(1)}) custom-call(s32[7]{0:T(128)S(1)} %stack.40.refs_0_, bf16[144,1024]{1,0:T(8,128)(2,1)S(1)} %get-tuple-element.73.refs_1_, bf16[144,1024]{1,0:T(8,128)(2,1)S(1)} %collective-permute-done.7.refs_2_, ...), custom_call_target="tpu_custom_call" | custom-call | flops 115000000 | tf_op jit(solution)/shard_map/out1/pallas_call | solution.py:448
  72.2 2.4 %collective-permute-done.8.refs_3_ = bf16[128,1024]{1,0:T(8,128)(2,1)S(1)} collective-permute-done((bf16[128,1024]{1,0:T(8,128)(2,1)S(1)}, bf16[128,1024]{1,0:T(8,128)(2,1)S(1)}, u32[]{:S(2)}, u32[]{:S(2)}) %collective-permute-start.8) | collective-permute-done | bytes 262176 | tf_op jit(solution)/shard_map/ppermute | solution.py:520
  76.6 1.5 %collective-permute-done.13.refs_2_ = bf16[144,1024]{1,0:T(8,128)(2,1)S(1)} collective-permute-done((bf16[144,1024]{1,0:T(8,128)(2,1)S(1)}, bf16[144,1024]{1,0:T(8,128)(2,1)S(1)}, u32[]{:S(2)}, u32[]{:S(2)}) %collective-permute-start.13) | collective-permute-done | bytes 294944 | tf_op jit(solution)/shard_map/ppermute | solution.py:520
  79.1 1.6 %collective-permute-start.19 = (bf16[64,4096]{1,0:T(8,128)(2,1)S(1)}, bf16[64,4096]{1,0:T(8,128)(2,1)S(1)}, u32[]{:S(2)}, u32[]{:S(2)}) collective-permute-start(bf16[64,4096]{1,0:T(8,128)(2,1)S(1)} %get-tuple-element.119), channel_id=1, source_target_pairs={{0,16},{8,24},{16,0},{24,8},{1,17},{9,25},{17,1},{25,9},{2,18},{10... | collective-permute-start | bytes 1572872 | tf_op jit(solution)/shard_map/ppermute | solution.py:539
  80.6 4.0 %scan2.1 = (bf16[2,128,1024]{2,1,0:T(8,128)(2,1)S(1)}, f32[2,128,1024]{2,1,0:T(8,128)S(1)}, f32[8,128]{1,0:T(8,128)S(1)}) custom-call(s32[7]{0:T(128)S(1)} %stack.40.refs_0_, bf16[128,4096]{1,0:T(8,128)(2,1)S(1)} %bitcast.24, bf16[128,4096]{1,0:T(8,128)(2,1)S(1)} %collective-permute-done.refs_2_, f32[2,8,128]{2,1,0:T(8,128)S(1)} %get-tuple-element.99.refs_3_.refs_7_, ...), custom_call_target="tpu_custom_call" | custom-call | flops 115000000 | tf_op jit(solution)/shard_map/scan2/pallas_call | solution.py:448
  84.7 2.5 %collective-permute-done.16.refs_3_ = bf16[128,1024]{1,0:T(8,128)(2,1)S(1)} collective-permute-done((bf16[128,1024]{1,0:T(8,128)(2,1)S(1)}, bf16[128,1024]{1,0:T(8,128)(2,1)S(1)}, u32[]{:S(2)}, u32[]{:S(2)}) %collective-permute-start.16) | collective-permute-done | bytes 262176 | tf_op jit(solution)/shard_map/ppermute | solution.py:520
  87.2 2.6 %out1.3 = (bf16[64,4096]{1,0:T(8,128)(2,1)S(1)}, bf16[64,2048]{1,0:T(8,128)(2,1)S(1)}, bf16[64,2048]{1,0:T(8,128)(2,1)S(1)}, f32[8,128]{1,0:T(8,128)S(1)}) custom-call(s32[7]{0:T(128)S(1)} %stack.40.refs_0_, bf16[144,1024]{1,0:T(8,128)(2,1)S(1)} %get-tuple-element.79.refs_1_, bf16[144,1024]{1,0:T(8,128)(2,1)S(1)} %collective-permute-done.10.refs_2_, ...), custom_call_target="tpu_custom_call" | custom-call | flops 115000000 | tf_op jit(solution)/shard_map/out1/pallas_call | solution.py:448
  92.5 1.6 %collective-permute-start.21 = (bf16[64,4096]{1,0:T(8,128)(2,1)S(1)}, bf16[64,4096]{1,0:T(8,128)(2,1)S(1)}, u32[]{:S(2)}, u32[]{:S(2)}) collective-permute-start(bf16[64,4096]{1,0:T(8,128)(2,1)S(1)} %get-tuple-element.124), channel_id=1, source_target_pairs={{0,16},{8,24},{16,0},{24,8},{1,17},{9,25},{17,1},{25,9},{2,18},{10... | collective-permute-start | bytes 1572872 | tf_op jit(solution)/shard_map/ppermute | solution.py:539
  94.1 4.5 %out2.1 = (bf16[128,4096]{1,0:T(8,128)(2,1)S(1)}, bf16[128,4096]{1,0:T(8,128)(2,1)S(1)}, f32[8,128]{1,0:T(8,128)S(1)}) custom-call(s32[7]{0:T(128)S(1)} %stack.40.refs_0_, bf16[128,1024]{1,0:T(8,128)(2,1)S(1)} %get-tuple-element.97.refs_1_, bf16[128,1024]{1,0:T(8,128)(2,1)S(1)} %collective-permute-done.12.refs_11_.refs_2_, ...), custom_call_target="tpu_custom_call" | custom-call | flops 115000000 | tf_op jit(solution)/shard_map/out2/pallas_call | solution.py:448
  99.2 7.3 %collective-permute-done.21.refs_6_ = bf16[64,4096]{1,0:T(8,128)(2,1)S(1)} collective-permute-done((bf16[64,4096]{1,0:T(8,128)(2,1)S(1)}, bf16[64,4096]{1,0:T(8,128)(2,1)S(1)}, u32[]{:S(2)}, u32[]{:S(2)}) %collective-permute-start.21) | collective-permute-done | bytes 524320 | tf_op jit(solution)/shard_map/ppermute | solution.py:539
  107.2 1.2 %collective-permute-done.23.refs_8_ = bf16[64,4096]{1,0:T(8,128)(2,1)S(1)} collective-permute-done((bf16[64,4096]{1,0:T(8,128)(2,1)S(1)}, bf16[64,4096]{1,0:T(8,128)(2,1)S(1)}, u32[]{:S(2)}, u32[]{:S(2)}) %collective-permute-start.23) | collective-permute-done | bytes 524320 | tf_op jit(solution)/shard_map/ppermute | solution.py:534
  108.4 2.3 %close.1 = (bf16[128,4096]{1,0:T(8,128)(2,1)}, f32[8,128]{1,0:T(8,128)}) custom-call(s32[7]{0:T(128)S(1)} %stack.40.refs_0_, f32[1]{0:T(128)S(6)} %copy.19.refs_1_, bf16[128,4096]{1,0:T(8,128)(2,1)S(1)} %bitcast.25, bf16[128,4096]{1,0:T(8,128)(2,1)S(1)} %get-tuple-element.122.refs_3_, bf16[128,4096]{1,0:T(8,128)(2,1)S(1)} %collective-permute-done.20.refs_4_, ...), custom_call_target="tpu_custom_call" | custom-call | flops 1150000000 | tf_op jit(solution)/shard_map/close/pallas_call | solution.py:448
  (80 shorter events, 14.9 us)
Async XLA Ops:
  0.0 3.1 %collective-permute-start = (bf16[128,4096]{1,0:T(8,128)(2,1)}, bf16[128,4096]{1,0:T(8,128)(2,1)S(1)}, u32[]{:S(2)}, u32[]{:S(2)}) collective-permute-start(bf16[128,4096]{1,0:T(8,128)(2,1)} %bitcast.20), channel_id=1, source_target_pairs={{0,8},{8,0},{16,24},{24,16},{1,9},{9,1},{17,25},{25,17},{2,10},{10... | collective-permute-start | bytes 3145736 | tf_op jit(solution)/shard_map/ppermute | solution.py:534
  0.5 28.0 %collective-permute-start.4 = (bf16[128,4096]{1,0:T(8,128)(2,1)}, bf16[128,4096]{1,0:T(8,128)(2,1)S(1)}, u32[]{:S(2)}, u32[]{:S(2)}) collective-permute-start(bf16[128,4096]{1,0:T(8,128)(2,1)} %bitcast.21), channel_id=1, source_target_pairs={{0,16},{8,24},{16,0},{24,8},{1,17},{9,25},{17,1},{25,9},{2,18},{10... | collective-permute-start | bytes 3145736 | tf_op jit(solution)/shard_map/ppermute | solution.py:539
  5.0 11.5 %copy-start.1 = (bf16[1,128,4096]{2,1,0:T(8,128)(2,1)S(1)}, bf16[1,128,4096]{2,1,0:T(8,128)(2,1)}, u32[]{:S(2)}) copy-start(bf16[1,128,4096]{2,1,0:T(8,128)(2,1)} %param.16) | copy-start | bytes 3145732
  5.0 11.5 %copy-start.4 = (bf16[4096,1024]{1,0:T(8,128)(2,1)S(1)}, bf16[4096,1024]{1,0:T(8,128)(2,1)}, u32[]{:S(2)}) copy-start(bf16[4096,1024]{1,0:T(8,128)(2,1)} %refs_5_.5) | copy-start | bytes 25165828
  5.0 11.5 %copy-start.5 = (bf16[4096,512]{1,0:T(8,128)(2,1)S(1)}, bf16[4096,512]{1,0:T(8,128)(2,1)}, u32[]{:S(2)}) copy-start(bf16[4096,512]{1,0:T(8,128)(2,1)} %refs_6_.5) | copy-start | bytes 12582916
  5.0 11.5 %copy-start.6 = (bf16[4096,16]{0,1:T(8,128)(2,1)S(1)}, bf16[4096,16]{0,1:T(8,128)(2,1)}, u32[]{:S(2)}) copy-start(bf16[4096,16]{0,1:T(8,128)(2,1)} %param.21) | copy-start | bytes 393220
  5.6 8.2 %collective-permute-start.1 = (bf16[16,2048]{1,0:T(8,128)(2,1)S(1)}, bf16[16,2048]{1,0:T(8,128)(2,1)S(1)}, u32[]{:S(2)}, u32[]{:S(2)}) collective-permute-start(bf16[16,2048]{1,0:T(8,128)(2,1)S(1)} %get-tuple-element.66), channel_id=1, source_target_pairs={{0,1},{1,2},{2,3},{3,4},{4,5},{5,6},{6,7},{7,0},{8,9},{9,10},{10,1... | collective-permute-start | bytes 196616 | tf_op jit(solution)/shard_map/ppermute | solution.py:530
  8.4 7.9 %collective-permute-start.2 = (bf16[16,2048]{1,0:T(8,128)(2,1)S(1)}, bf16[16,2048]{1,0:T(8,128)(2,1)S(1)}, u32[]{:S(2)}, u32[]{:S(2)}) collective-permute-start(bf16[16,2048]{1,0:T(8,128)(2,1)S(1)} %get-tuple-element.66), channel_id=1, source_target_pairs={{16,1},{17,2},{18,3},{19,4},{20,5},{21,6},{22,7},{23,0},{24,9},{25... | collective-permute-start | bytes 196616 | tf_op jit(solution)/shard_map/ppermute | solution.py:530
  28.4 2.7 %collective-permute-start.5 = (bf16[128,4096]{1,0:T(8,128)(2,1)S(1)}, bf16[128,4096]{1,0:T(8,128)(2,1)S(1)}, u32[]{:S(2)}, u32[]{:S(2)}) collective-permute-start(bf16[128,4096]{1,0:T(8,128)(2,1)S(1)} %hold.1.refs_1_), channel_id=1, source_target_pairs={{0,8},{8,0},{16,24},{24,16},{1,9},{9,1},{17,25},{25,17},{2,10},{10... | collective-permute-start | bytes 3145736 | tf_op jit(solution)/shard_map/ppermute | solution.py:534
  28.4 9.4 %collective-permute-start.3 = (bf16[144,1024]{1,0:T(8,128)(2,1)S(1)}, bf16[144,1024]{1,0:T(8,128)(2,1)S(1)}, u32[]{:S(2)}, u32[]{:S(2)}) collective-permute-start(bf16[144,1024]{1,0:T(8,128)(2,1)S(1)} %get-tuple-element.69), channel_id=1, source_target_pairs={{0,1},{1,0},{2,3},{3,2},{4,5},{5,4},{6,7},{7,6},{8,9},{9,8},{10,11... | collective-permute-start | bytes 884744 | tf_op jit(solution)/shard_map/ppermute | solution.py:534
  31.1 18.9 %slice-start = ((s8[8388608]{0:T(1024)(128)(4,1)}), s8[4194304]{0:T(1024)(128)(4,1)S(1)}, s32[]{:S(2)}) async-start(s8[8388608]{0:T(1024)(128)(4,1)} %bitcast.16), calls=%async_computation | async-start | bytes 8388608
  35.6 11.0 %collective-permute-start.7 = (bf16[144,1024]{1,0:T(8,128)(2,1)S(1)}, bf16[144,1024]{1,0:T(8,128)(2,1)S(1)}, u32[]{:S(2)}, u32[]{:S(2)}) collective-permute-start(bf16[144,1024]{1,0:T(8,128)(2,1)S(1)} %get-tuple-element.73.refs_1_), channel_id=1, source_target_pairs={{0,1},{1,0},{2,3},{3,2},{4,5},{5,4},{6,7},{7,6},{8,9},{9,8},{10,11... | collective-permute-start | bytes 884744 | tf_op jit(solution)/shard_map/ppermute | solution.py:534
  38.5 10.8 %collective-permute-start.6 = (bf16[144,1024]{1,0:T(8,128)(2,1)S(1)}, bf16[144,1024]{1,0:T(8,128)(2,1)S(1)}, u32[]{:S(2)}, u32[]{:S(2)}) collective-permute-start(bf16[144,1024]{1,0:T(8,128)(2,1)S(1)} %get-tuple-element.72.refs_1_), channel_id=1, source_target_pairs={{0,2},{1,3},{2,4},{3,5},{4,6},{5,7},{6,0},{7,1},{8,10},{9,11},{10,... | collective-permute-start | bytes 884744 | tf_op jit(solution)/shard_map/ppermute | solution.py:520
  45.1 8.4 %collective-permute-start.10 = (bf16[144,1024]{1,0:T(8,128)(2,1)S(1)}, bf16[144,1024]{1,0:T(8,128)(2,1)S(1)}, u32[]{:S(2)}, u32[]{:S(2)}) collective-permute-start(bf16[144,1024]{1,0:T(8,128)(2,1)S(1)} %get-tuple-element.79.refs_1_), channel_id=1, source_target_pairs={{0,1},{1,0},{2,3},{3,2},{4,5},{5,4},{6,7},{7,6},{8,9},{9,8},{10,11... | collective-permute-start | bytes 884744 | tf_op jit(solution)/shard_map/ppermute | solution.py:534
  47.3 9.9 %collective-permute-start.9 = (bf16[144,1024]{1,0:T(8,128)(2,1)S(1)}, bf16[144,1024]{1,0:T(8,128)(2,1)S(1)}, u32[]{:S(2)}, u32[]{:S(2)}) collective-permute-start(bf16[144,1024]{1,0:T(8,128)(2,1)S(1)} %get-tuple-element.78.refs_1_), channel_id=1, source_target_pairs={{0,2},{1,3},{2,4},{3,5},{4,6},{5,7},{6,0},{7,1},{8,10},{9,11},{10,... | collective-permute-start | bytes 884744 | tf_op jit(solution)/shard_map/ppermute | solution.py:520
  50.0 19.0 %slice-start.2 = ((s8[8388608]{0:T(1024)(128)(4,1)}), s8[4194304]{0:T(1024)(128)(4,1)S(1)}, s32[]{:S(2)}) async-start(s8[8388608]{0:T(1024)(128)(4,1)} %bitcast.18), calls=%async_computation.2 | async-start | bytes 8388608
  52.6 16.4 %copy-start.2 = (f32[1024]{0:T(1024)S(1)}, f32[1024]{0:T(1024)}, u32[]{:S(2)}) copy-start(f32[1024]{0:T(1024)} %param.29) | copy-start | bytes 12292
  57.3 11.7 %slice-start.3 = ((s8[8388608]{0:T(1024)(128)(4,1)}), s8[4194304]{0:T(1024)(128)(4,1)S(1)}, s32[]{:S(2)}) async-start(s8[8388608]{0:T(1024)(128)(4,1)} %bitcast.18), calls=%async_computation.3 | async-start | bytes 8388608
  57.9 11.1 %collective-permute-start.11 = (bf16[128,1024]{1,0:T(8,128)(2,1)S(1)}, bf16[128,1024]{1,0:T(8,128)(2,1)S(1)}, u32[]{:S(2)}, u32[]{:S(2)}) collective-permute-start(bf16[128,1024]{1,0:T(8,128)(2,1)S(1)} %get-tuple-element.87), channel_id=1, source_target_pairs={{0,2},{1,3},{2,4},{3,5},{4,6},{5,7},{6,0},{7,1},{8,10},{9,11},{10,... | collective-permute-start | bytes 786440 | tf_op jit(solution)/shard_map/ppermute | solution.py:520
  58.0 16.6 %collective-permute-start.8 = (bf16[128,1024]{1,0:T(8,128)(2,1)S(1)}, bf16[128,1024]{1,0:T(8,128)(2,1)S(1)}, u32[]{:S(2)}, u32[]{:S(2)}) collective-permute-start(bf16[128,1024]{1,0:T(8,128)(2,1)S(1)} %get-tuple-element.77), channel_id=1, source_target_pairs={{0,2},{1,3},{2,4},{3,5},{4,6},{5,7},{6,0},{7,1},{8,10},{9,11},{10,... | collective-permute-start | bytes 786440 | tf_op jit(solution)/shard_map/ppermute | solution.py:520
  59.3 18.8 %collective-permute-start.13 = (bf16[144,1024]{1,0:T(8,128)(2,1)S(1)}, bf16[144,1024]{1,0:T(8,128)(2,1)S(1)}, u32[]{:S(2)}, u32[]{:S(2)}) collective-permute-start(bf16[144,1024]{1,0:T(8,128)(2,1)S(1)} %get-tuple-element.103.refs_1_), channel_id=1, source_target_pairs={{0,2},{1,3},{2,4},{3,5},{4,6},{5,7},{6,0},{7,1},{8,10},{9,11},{10,... | collective-permute-start | bytes 884744 | tf_op jit(solution)/shard_map/ppermute | solution.py:520
  71.6 4.3 %collective-permute-start.14 = (bf16[64,2048]{1,0:T(8,128)(2,1)S(1)}, bf16[64,2048]{1,0:T(8,128)(2,1)S(1)}, u32[]{:S(2)}, u32[]{:S(2)}) collective-permute-start(bf16[64,2048]{1,0:T(8,128)(2,1)S(1)} %get-tuple-element.105), channel_id=1, source_target_pairs={{0,8},{8,0},{16,24},{24,16},{1,9},{9,1},{17,25},{25,17},{2,10},{10... | collective-permute-start | bytes 786440 | tf_op jit(solution)/shard_map/ppermute | solution.py:534
  71.7 4.2 %collective-permute-start.15 = (bf16[64,2048]{1,0:T(8,128)(2,1)S(1)}, bf16[64,2048]{1,0:T(8,128)(2,1)S(1)}, u32[]{:S(2)}, u32[]{:S(2)}) collective-permute-start(bf16[64,2048]{1,0:T(8,128)(2,1)S(1)} %get-tuple-element.106), channel_id=1, source_target_pairs={{0,8},{8,0},{16,24},{24,16},{1,9},{9,1},{17,25},{25,17},{2,10},{10... | collective-permute-start | bytes 786440 | tf_op jit(solution)/shard_map/ppermute | solution.py:534
  75.3 9.4 %collective-permute-start.12 = (bf16[128,1024]{1,0:T(8,128)(2,1)S(1)}, bf16[128,1024]{1,0:T(8,128)(2,1)S(1)}, u32[]{:S(2)}, u32[]{:S(2)}) collective-permute-start(bf16[128,1024]{1,0:T(8,128)(2,1)S(1)} %get-tuple-element.98), channel_id=1, source_target_pairs={{0,1},{1,0},{2,3},{3,2},{4,5},{5,4},{6,7},{7,6},{8,9},{9,8},{10,11... | collective-permute-start | bytes 786440 | tf_op jit(solution)/shard_map/ppermute | solution.py:534
  78.8 8.4 %collective-permute-start.16 = (bf16[128,1024]{1,0:T(8,128)(2,1)S(1)}, bf16[128,1024]{1,0:T(8,128)(2,1)S(1)}, u32[]{:S(2)}, u32[]{:S(2)}) collective-permute-start(bf16[128,1024]{1,0:T(8,128)(2,1)S(1)} %get-tuple-element.112), channel_id=1, source_target_pairs={{0,2},{1,3},{2,4},{3,5},{4,6},{5,7},{6,0},{7,1},{8,10},{9,11},{10,... | collective-permute-start | bytes 786440 | tf_op jit(solution)/shard_map/ppermute | solution.py:520
  79.1 11.3 %collective-permute-start.19 = (bf16[64,4096]{1,0:T(8,128)(2,1)S(1)}, bf16[64,4096]{1,0:T(8,128)(2,1)S(1)}, u32[]{:S(2)}, u32[]{:S(2)}) collective-permute-start(bf16[64,4096]{1,0:T(8,128)(2,1)S(1)} %get-tuple-element.119), channel_id=1, source_target_pairs={{0,16},{8,24},{16,0},{24,8},{1,17},{9,25},{17,1},{25,9},{2,18},{10... | collective-permute-start | bytes 1572872 | tf_op jit(solution)/shard_map/ppermute | solution.py:539
  89.8 1.6 %collective-permute-start.17 = (bf16[64,2048]{1,0:T(8,128)(2,1)S(1)}, bf16[64,2048]{1,0:T(8,128)(2,1)S(1)}, u32[]{:S(2)}, u32[]{:S(2)}) collective-permute-start(bf16[64,2048]{1,0:T(8,128)(2,1)S(1)} %get-tuple-element.117), channel_id=1, source_target_pairs={{0,8},{8,0},{16,24},{24,16},{1,9},{9,1},{17,25},{25,17},{2,10},{10... | collective-permute-start | bytes 786440 | tf_op jit(solution)/shard_map/ppermute | solution.py:534
  89.9 1.9 %collective-permute-start.18 = (bf16[64,2048]{1,0:T(8,128)(2,1)S(1)}, bf16[64,2048]{1,0:T(8,128)(2,1)S(1)}, u32[]{:S(2)}, u32[]{:S(2)}) collective-permute-start(bf16[64,2048]{1,0:T(8,128)(2,1)S(1)} %get-tuple-element.118), channel_id=1, source_target_pairs={{0,8},{8,0},{16,24},{24,16},{1,9},{9,1},{17,25},{25,17},{2,10},{10... | collective-permute-start | bytes 786440 | tf_op jit(solution)/shard_map/ppermute | solution.py:534
  92.5 14.0 %collective-permute-start.21 = (bf16[64,4096]{1,0:T(8,128)(2,1)S(1)}, bf16[64,4096]{1,0:T(8,128)(2,1)S(1)}, u32[]{:S(2)}, u32[]{:S(2)}) collective-permute-start(bf16[64,4096]{1,0:T(8,128)(2,1)S(1)} %get-tuple-element.124), channel_id=1, source_target_pairs={{0,16},{8,24},{16,0},{24,8},{1,17},{9,25},{17,1},{25,9},{2,18},{10... | collective-permute-start | bytes 1572872 | tf_op jit(solution)/shard_map/ppermute | solution.py:539
  98.6 9.8 %collective-permute-start.20 = (bf16[128,4096]{1,0:T(8,128)(2,1)S(1)}, bf16[128,4096]{1,0:T(8,128)(2,1)S(1)}, u32[]{:S(2)}, u32[]{:S(2)}) collective-permute-start(bf16[128,4096]{1,0:T(8,128)(2,1)S(1)} %get-tuple-element.123), channel_id=1, source_target_pairs={{0,8},{8,0},{16,24},{24,16},{1,9},{9,1},{17,25},{25,17},{2,10},{10... | collective-permute-start | bytes 3145736 | tf_op jit(solution)/shard_map/ppermute | solution.py:534
  98.7 8.5 %collective-permute-start.22 = (bf16[64,4096]{1,0:T(8,128)(2,1)S(1)}, bf16[64,4096]{1,0:T(8,128)(2,1)S(1)}, u32[]{:S(2)}, u32[]{:S(2)}) collective-permute-start(bf16[64,4096]{1,0:T(8,128)(2,1)S(1)} %collective-permute-done.19.refs_4_.refs_5_), channel_id=1, source_target_pairs={{0,8},{8,0},{16,24},{24,16},{1,9},{9,1},{17,25},{25,17},{2,10},{10... | collective-permute-start | bytes 1572872 | tf_op jit(solution)/shard_map/ppermute | solution.py:534
  106.5 1.9 %collective-permute-start.23 = (bf16[64,4096]{1,0:T(8,128)(2,1)S(1)}, bf16[64,4096]{1,0:T(8,128)(2,1)S(1)}, u32[]{:S(2)}, u32[]{:S(2)}) collective-permute-start(bf16[64,4096]{1,0:T(8,128)(2,1)S(1)} %collective-permute-done.21.refs_6_), channel_id=1, source_target_pairs={{0,8},{8,0},{16,24},{24,16},{1,9},{9,1},{17,25},{25,17},{2,10},{10... | collective-permute-start | bytes 1572872 | tf_op jit(solution)/shard_map/ppermute | solution.py:534
  (11 other events, 90.3 us)

commit v6 on v5

--- a/solution.py
+++ b/solution.py
@@ -508,7 +508,7 @@
     width, depth = out_weight.shape
     lines = CH if slots == 2 else HALF
     scratch = [pltpu.VMEM((slots * CH, width), bf16)]
-    kernel = functools.partial(out_kernel, slots, 8)
+    kernel = functools.partial(out_kernel, slots, 4)
     operands = (*entries, local, gates, coupled, sums, rows, gain, out_weight, *waits)
     pieces = 1 if slots == 2 else PIECES
     shapes = [shape(bf16, lines, depth)] + [shape(bf16, lines, depth // pieces)] * pieces

time: 111 us -> 111 us (level)
  no operation moved by 1% of the time
where the time goes in v6:
time: 111 us
  Pallas kernels  44.4 us (40%)
  waiting for transfers between devices  38.8 us (35%)
  starting transfers between devices  24.3 us (22%)
  local copies, waits for them, and re-layouts  2.15 us (2%)
    pallas_call x20, Pallas kernels, run(): pl.pallas_call(ordered, in_specs=[IN_SMEM] * (1 + len(scalars)) + [IN_VME...  44.4 us
    ppermute x6, waiting for transfers between devices, along(): lax.ppermute(block, 'ctx', [(i, (i + distance) % spans) for i in range(sp...  16.6 us
    ppermute x3, waiting for transfers between devices, over(): lax.ppermute(block, 'fsdp', [(i, (i + 2 * distance) % size) for i in rang...  11.8 us
    ppermute x13, starting transfers between devices, partner(): lax.ppermute(block, axis, [(i, i ^ 1) for i in range(lax.axis_size(axis))])  7.81 us
    ppermute x3, starting transfers between devices, over(): lax.ppermute(block, 'fsdp', [(i, (i + 2 * distance) % size) for i in rang...  5.69 us
    ppermute x6, starting transfers between devices, along(): lax.ppermute(block, 'ctx', [(i, (i + distance) % spans) for i in range(sp...  5.47 us
    ppermute x2, waiting for transfers between devices, tail_from(): return lax.ppermute(block, ('fsdp', 'ctx'), route)  5.42 us
    ppermute x2, starting transfers between devices, tail_from(): return lax.ppermute(block, ('fsdp', 'ctx'), route)  5.31 us
  transfers between devices with their start and end apart: 24, of which 16 were waited for; matrix products, arithmetic and copies ran while one was open for 0% of the time, Pallas kernels for 37%

profile of v6, /device:TPU:0, one launch (start us, length us, event | category | flops | bytes accessed | tf_op | source)
XLA Modules:
  0.0 110.7 jit_solution(16712476663164121739)
XLA Ops:
  0.5 2.5 %collective-permute-start.4 = (bf16[128,4096]{1,0:T(8,128)(2,1)}, bf16[128,4096]{1,0:T(8,128)(2,1)S(1)}, u32[]{:S(2)}, u32[]{:S(2)}) collective-permute-start(bf16[128,4096]{1,0:T(8,128)(2,1)} %bitcast.21), channel_id=1, source_target_pairs={{0,16},{8,24},{16,0},{24,8},{1,17},{9,25},{17,1},{25,9},{2,18},{10... | collective-permute-start | bytes 3145736 | tf_op jit(solution)/shard_map/ppermute | solution.py:539
  3.1 1.2 %copy-done = bf16[1,128,4096]{2,1,0:T(8,128)(2,1)S(1)} copy-done((bf16[1,128,4096]{2,1,0:T(8,128)(2,1)S(1)}, bf16[1,128,4096]{2,1,0:T(8,128)(2,1)}, u32[]{:S(2)}) %copy-start) | copy-done | bytes 1048600
  5.6 2.8 %collective-permute-start.1 = (bf16[16,2048]{1,0:T(8,128)(2,1)S(1)}, bf16[16,2048]{1,0:T(8,128)(2,1)S(1)}, u32[]{:S(2)}, u32[]{:S(2)}) collective-permute-start(bf16[16,2048]{1,0:T(8,128)(2,1)S(1)} %get-tuple-element.66), channel_id=1, source_target_pairs={{0,1},{1,2},{2,3},{3,4},{4,5},{5,6},{6,7},{7,0},{8,9},{9,10},{10,1... | collective-permute-start | bytes 196616 | tf_op jit(solution)/shard_map/ppermute | solution.py:530
  8.4 2.5 %collective-permute-start.2 = (bf16[16,2048]{1,0:T(8,128)(2,1)S(1)}, bf16[16,2048]{1,0:T(8,128)(2,1)S(1)}, u32[]{:S(2)}, u32[]{:S(2)}) collective-permute-start(bf16[16,2048]{1,0:T(8,128)(2,1)S(1)} %get-tuple-element.66), channel_id=1, source_target_pairs={{16,1},{17,2},{18,3},{19,4},{20,5},{21,6},{22,7},{23,0},{24,9},{25... | collective-permute-start | bytes 196616 | tf_op jit(solution)/shard_map/ppermute | solution.py:530
  11.0 2.9 %collective-permute-done.1.refs_3_ = bf16[16,2048]{1,0:T(8,128)(2,1)S(1)} collective-permute-done((bf16[16,2048]{1,0:T(8,128)(2,1)S(1)}, bf16[16,2048]{1,0:T(8,128)(2,1)S(1)}, u32[]{:S(2)}, u32[]{:S(2)}) %collective-permute-start.1) | collective-permute-done | bytes 65568 | tf_op jit(solution)/shard_map/ppermute | solution.py:530
  13.9 2.5 %collective-permute-done.2.refs_4_.refs_3_ = bf16[16,2048]{1,0:T(8,128)(2,1)S(1)} collective-permute-done((bf16[16,2048]{1,0:T(8,128)(2,1)S(1)}, bf16[16,2048]{1,0:T(8,128)(2,1)S(1)}, u32[]{:S(2)}, u32[]{:S(2)}) %collective-permute-start.2) | collective-permute-done | bytes 65568 | tf_op jit(solution)/shard_map/ppermute | solution.py:530
  16.5 7.4 %mix2.1 = (bf16[2,128,1024]{2,1,0:T(8,128)(2,1)S(1)}, bf16[2,128,512]{2,1,0:T(8,128)(2,1)S(1)}, f32[2,4,8,128]{3,2,1,0:T(8,128)S(1)}, f32[2,8,128]{2,1,0:T(8,128...) custom-call(s32[7]{0:T(128)S(1)} %stack.40.refs_0_, ...), custom_call_target="tpu_custom_call" | custom-call | flops 9200000000 | tf_op jit(solution)/shard_map/mix2/pallas_call | solution.py:448
  23.9 4.5 %collective-permute-done.4.block_ref = bf16[128,4096]{1,0:T(8,128)(2,1)S(1)} collective-permute-done((bf16[128,4096]{1,0:T(8,128)(2,1)}, bf16[128,4096]{1,0:T(8,128)(2,1)S(1)}, u32[]{:S(2)}, u32[]{:S(2)}) %collective-permute-start.4) | collective-permute-done | bytes 1048608 | tf_op jit(solution)/shard_map/ppermute | solution.py:539
  28.4 1.7 %collective-permute-start.3 = (bf16[144,1024]{1,0:T(8,128)(2,1)S(1)}, bf16[144,1024]{1,0:T(8,128)(2,1)S(1)}, u32[]{:S(2)}, u32[]{:S(2)}) collective-permute-start(bf16[144,1024]{1,0:T(8,128)(2,1)S(1)} %get-tuple-element.69), channel_id=1, source_target_pairs={{0,1},{1,0},{2,3},{3,2},{4,5},{5,4},{6,7},{7,6},{8,9},{9,8},{10,11... | collective-permute-start | bytes 884744 | tf_op jit(solution)/shard_map/ppermute | solution.py:534
  31.1 4.5 %mix1.2 = (bf16[1,128,1024]{2,1,0:T(8,128)(2,1)S(1)}, bf16[1,128,512]{2,1,0:T(8,128)(2,1)S(1)}, f32[1,4,8,128]{3,2,1,0:T(8,128)S(1)}, f32[1,8,128]{2,1,0:T(8,128...) custom-call(s32[7]{0:T(128)S(1)} %stack.40.refs_0_, bf16[128,4096]{1,0:T(8,128)(2,1)S(1)} %hold.1.refs_1_, ...), custom_call_target="tpu_custom_call" | custom-call | flops 4600000000 | tf_op jit(solution)/shard_map/mix1/pallas_call | solution.py:448
  35.6 1.8 %collective-permute-start.7 = (bf16[144,1024]{1,0:T(8,128)(2,1)S(1)}, bf16[144,1024]{1,0:T(8,128)(2,1)S(1)}, u32[]{:S(2)}, u32[]{:S(2)}) collective-permute-start(bf16[144,1024]{1,0:T(8,128)(2,1)S(1)} %get-tuple-element.73.refs_1_), channel_id=1, source_target_pairs={{0,1},{1,0},{2,3},{3,2},{4,5},{5,4},{6,7},{7,6},{8,9},{9,8},{10,11... | collective-permute-start | bytes 884744 | tf_op jit(solution)/shard_map/ppermute | solution.py:534
  38.5 1.9 %collective-permute-start.6 = (bf16[144,1024]{1,0:T(8,128)(2,1)S(1)}, bf16[144,1024]{1,0:T(8,128)(2,1)S(1)}, u32[]{:S(2)}, u32[]{:S(2)}) collective-permute-start(bf16[144,1024]{1,0:T(8,128)(2,1)S(1)} %get-tuple-element.72.refs_1_), channel_id=1, source_target_pairs={{0,2},{1,3},{2,4},{3,5},{4,6},{5,7},{6,0},{7,1},{8,10},{9,11},{10,... | collective-permute-start | bytes 884744 | tf_op jit(solution)/shard_map/ppermute | solution.py:520
  40.4 4.7 %mix1.3 = (bf16[1,128,1024]{2,1,0:T(8,128)(2,1)S(1)}, bf16[1,128,512]{2,1,0:T(8,128)(2,1)S(1)}, f32[1,4,8,128]{3,2,1,0:T(8,128)S(1)}, f32[1,8,128]{2,1,0:T(8,128...) custom-call(s32[7]{0:T(128)S(1)} %stack.40.refs_0_, bf16[128,4096]{1,0:T(8,128)(2,1)S(1)} %hold.1.refs_1_, ...), custom_call_target="tpu_custom_call" | custom-call | flops 4600000000 | tf_op jit(solution)/shard_map/mix1/pallas_call | solution.py:448
  45.1 1.6 %collective-permute-start.10 = (bf16[144,1024]{1,0:T(8,128)(2,1)S(1)}, bf16[144,1024]{1,0:T(8,128)(2,1)S(1)}, u32[]{:S(2)}, u32[]{:S(2)}) collective-permute-start(bf16[144,1024]{1,0:T(8,128)(2,1)S(1)} %get-tuple-element.79.refs_1_), channel_id=1, source_target_pairs={{0,1},{1,0},{2,3},{3,2},{4,5},{5,4},{6,7},{7,6},{8,9},{9,8},{10,11... | collective-permute-start | bytes 884744 | tf_op jit(solution)/shard_map/ppermute | solution.py:534
  47.3 1.6 %collective-permute-start.9 = (bf16[144,1024]{1,0:T(8,128)(2,1)S(1)}, bf16[144,1024]{1,0:T(8,128)(2,1)S(1)}, u32[]{:S(2)}, u32[]{:S(2)}) collective-permute-start(bf16[144,1024]{1,0:T(8,128)(2,1)S(1)} %get-tuple-element.78.refs_1_), channel_id=1, source_target_pairs={{0,2},{1,3},{2,4},{3,5},{4,6},{5,7},{6,0},{7,1},{8,10},{9,11},{10,... | collective-permute-start | bytes 884744 | tf_op jit(solution)/shard_map/ppermute | solution.py:520
  50.0 2.6 %scan1.2 = (bf16[1,128,1024]{2,1,0:T(8,128)(2,1)S(1)}, f32[1,128,1024]{2,1,0:T(8,128)S(1)}, f32[8,128]{1,0:T(8,128)S(1)}) custom-call(s32[7]{0:T(128)S(1)} %stack.40.refs_0_, bf16[128,4096]{1,0:T(8,128)(2,1)S(1)} %hold.1.refs_1_, bf16[128,4096]{1,0:T(8,128)(2,1)S(1)} %collective-permute-done.5.refs_2_, f32[1,8,128]{2,1,0:T(8,128)S(1)} %get-tuple-element.80.refs_3_.refs_8_, ...), custom_call_target="tpu_custom_call" | custom-call | flops 115000000 | tf_op jit(solution)/shard_map/scan1/pallas_call | solution.py:448
  54.2 3.1 %collective-permute-done.9.refs_2_ = bf16[144,1024]{1,0:T(8,128)(2,1)S(1)} collective-permute-done((bf16[144,1024]{1,0:T(8,128)(2,1)S(1)}, bf16[144,1024]{1,0:T(8,128)(2,1)S(1)}, u32[]{:S(2)}, u32[]{:S(2)}) %collective-permute-start.9) | collective-permute-done | bytes 294944 | tf_op jit(solution)/shard_map/ppermute | solution.py:520
  58.0 1.3 %collective-permute-start.8 = (bf16[128,1024]{1,0:T(8,128)(2,1)S(1)}, bf16[128,1024]{1,0:T(8,128)(2,1)S(1)}, u32[]{:S(2)}, u32[]{:S(2)}) collective-permute-start(bf16[128,1024]{1,0:T(8,128)(2,1)S(1)} %get-tuple-element.77), channel_id=1, source_target_pairs={{0,2},{1,3},{2,4},{3,5},{4,6},{5,7},{6,0},{7,1},{8,10},{9,11},{10,... | collective-permute-start | bytes 786440 | tf_op jit(solution)/shard_map/ppermute | solution.py:520
  59.6 2.6 %scan1.3 = (bf16[1,128,1024]{2,1,0:T(8,128)(2,1)S(1)}, f32[1,128,1024]{2,1,0:T(8,128)S(1)}, f32[8,128]{1,0:T(8,128)S(1)}) custom-call(s32[7]{0:T(128)S(1)} %stack.40.refs_0_, bf16[128,4096]{1,0:T(8,128)(2,1)S(1)} %hold.1.refs_1_, bf16[128,4096]{1,0:T(8,128)(2,1)S(1)} %collective-permute-done.5.refs_2_, f32[1,8,128]{2,1,0:T(8,128)S(1)} %get-tuple-element.90.refs_3_.refs_8_, ...), custom_call_target="tpu_custom_call" | custom-call | flops 115000000 | tf_op jit(solution)/shard_map/scan1/pallas_call | solution.py:448
  62.3 6.7 %collective-permute-done.11.refs_3_ = bf16[128,1024]{1,0:T(8,128)(2,1)S(1)} collective-permute-done((bf16[128,1024]{1,0:T(8,128)(2,1)S(1)}, bf16[128,1024]{1,0:T(8,128)(2,1)S(1)}, u32[]{:S(2)}, u32[]{:S(2)}) %collective-permute-start.11) | collective-permute-done | bytes 262176 | tf_op jit(solution)/shard_map/ppermute | solution.py:520
  69.0 2.6 %out1.2 = (bf16[64,4096]{1,0:T(8,128)(2,1)S(1)}, bf16[64,2048]{1,0:T(8,128)(2,1)S(1)}, bf16[64,2048]{1,0:T(8,128)(2,1)S(1)}, f32[8,128]{1,0:T(8,128)S(1)}) custom-call(s32[7]{0:T(128)S(1)} %stack.40.refs_0_, bf16[144,1024]{1,0:T(8,128)(2,1)S(1)} %get-tuple-element.73.refs_1_, bf16[144,1024]{1,0:T(8,128)(2,1)S(1)} %collective-permute-done.7.refs_2_, ...), custom_call_target="tpu_custom_call" | custom-call | flops 115000000 | tf_op jit(solution)/shard_map/out1/pallas_call | solution.py:448
  72.2 2.4 %collective-permute-done.8.refs_3_ = bf16[128,1024]{1,0:T(8,128)(2,1)S(1)} collective-permute-done((bf16[128,1024]{1,0:T(8,128)(2,1)S(1)}, bf16[128,1024]{1,0:T(8,128)(2,1)S(1)}, u32[]{:S(2)}, u32[]{:S(2)}) %collective-permute-start.8) | collective-permute-done | bytes 262176 | tf_op jit(solution)/shard_map/ppermute | solution.py:520
  76.6 1.5 %collective-permute-done.13.refs_2_ = bf16[144,1024]{1,0:T(8,128)(2,1)S(1)} collective-permute-done((bf16[144,1024]{1,0:T(8,128)(2,1)S(1)}, bf16[144,1024]{1,0:T(8,128)(2,1)S(1)}, u32[]{:S(2)}, u32[]{:S(2)}) %collective-permute-start.13) | collective-permute-done | bytes 294944 | tf_op jit(solution)/shard_map/ppermute | solution.py:520
  79.1 1.6 %collective-permute-start.19 = (bf16[64,4096]{1,0:T(8,128)(2,1)S(1)}, bf16[64,4096]{1,0:T(8,128)(2,1)S(1)}, u32[]{:S(2)}, u32[]{:S(2)}) collective-permute-start(bf16[64,4096]{1,0:T(8,128)(2,1)S(1)} %get-tuple-element.119), channel_id=1, source_target_pairs={{0,16},{8,24},{16,0},{24,8},{1,17},{9,25},{17,1},{25,9},{2,18},{10... | collective-permute-start | bytes 1572872 | tf_op jit(solution)/shard_map/ppermute | solution.py:539
  80.6 4.0 %scan2.1 = (bf16[2,128,1024]{2,1,0:T(8,128)(2,1)S(1)}, f32[2,128,1024]{2,1,0:T(8,128)S(1)}, f32[8,128]{1,0:T(8,128)S(1)}) custom-call(s32[7]{0:T(128)S(1)} %stack.40.refs_0_, bf16[128,4096]{1,0:T(8,128)(2,1)S(1)} %bitcast.24, bf16[128,4096]{1,0:T(8,128)(2,1)S(1)} %collective-permute-done.refs_2_, f32[2,8,128]{2,1,0:T(8,128)S(1)} %get-tuple-element.99.refs_3_.refs_7_, ...), custom_call_target="tpu_custom_call" | custom-call | flops 115000000 | tf_op jit(solution)/shard_map/scan2/pallas_call | solution.py:448
  84.7 2.5 %collective-permute-done.16.refs_3_ = bf16[128,1024]{1,0:T(8,128)(2,1)S(1)} collective-permute-done((bf16[128,1024]{1,0:T(8,128)(2,1)S(1)}, bf16[128,1024]{1,0:T(8,128)(2,1)S(1)}, u32[]{:S(2)}, u32[]{:S(2)}) %collective-permute-start.16) | collective-permute-done | bytes 262176 | tf_op jit(solution)/shard_map/ppermute | solution.py:520
  87.2 2.6 %out1.3 = (bf16[64,4096]{1,0:T(8,128)(2,1)S(1)}, bf16[64,2048]{1,0:T(8,128)(2,1)S(1)}, bf16[64,2048]{1,0:T(8,128)(2,1)S(1)}, f32[8,128]{1,0:T(8,128)S(1)}) custom-call(s32[7]{0:T(128)S(1)} %stack.40.refs_0_, bf16[144,1024]{1,0:T(8,128)(2,1)S(1)} %get-tuple-element.79.refs_1_, bf16[144,1024]{1,0:T(8,128)(2,1)S(1)} %collective-permute-done.10.refs_2_, ...), custom_call_target="tpu_custom_call" | custom-call | flops 115000000 | tf_op jit(solution)/shard_map/out1/pallas_call | solution.py:448
  92.5 1.6 %collective-permute-start.21 = (bf16[64,4096]{1,0:T(8,128)(2,1)S(1)}, bf16[64,4096]{1,0:T(8,128)(2,1)S(1)}, u32[]{:S(2)}, u32[]{:S(2)}) collective-permute-start(bf16[64,4096]{1,0:T(8,128)(2,1)S(1)} %get-tuple-element.124), channel_id=1, source_target_pairs={{0,16},{8,24},{16,0},{24,8},{1,17},{9,25},{17,1},{25,9},{2,18},{10... | collective-permute-start | bytes 1572872 | tf_op jit(solution)/shard_map/ppermute | solution.py:539
  94.1 4.5 %out2.1 = (bf16[128,4096]{1,0:T(8,128)(2,1)S(1)}, bf16[128,4096]{1,0:T(8,128)(2,1)S(1)}, f32[8,128]{1,0:T(8,128)S(1)}) custom-call(s32[7]{0:T(128)S(1)} %stack.40.refs_0_, bf16[128,1024]{1,0:T(8,128)(2,1)S(1)} %get-tuple-element.97.refs_1_, bf16[128,1024]{1,0:T(8,128)(2,1)S(1)} %collective-permute-done.12.refs_11_.refs_2_, ...), custom_call_target="tpu_custom_call" | custom-call | flops 115000000 | tf_op jit(solution)/shard_map/out2/pallas_call | solution.py:448
  99.2 7.3 %collective-permute-done.21.refs_6_ = bf16[64,4096]{1,0:T(8,128)(2,1)S(1)} collective-permute-done((bf16[64,4096]{1,0:T(8,128)(2,1)S(1)}, bf16[64,4096]{1,0:T(8,128)(2,1)S(1)}, u32[]{:S(2)}, u32[]{:S(2)}) %collective-permute-start.21) | collective-permute-done | bytes 524320 | tf_op jit(solution)/shard_map/ppermute | solution.py:539
  107.2 1.2 %collective-permute-done.23.refs_8_ = bf16[64,4096]{1,0:T(8,128)(2,1)S(1)} collective-permute-done((bf16[64,4096]{1,0:T(8,128)(2,1)S(1)}, bf16[64,4096]{1,0:T(8,128)(2,1)S(1)}, u32[]{:S(2)}, u32[]{:S(2)}) %collective-permute-start.23) | collective-permute-done | bytes 524320 | tf_op jit(solution)/shard_map/ppermute | solution.py:534
  108.4 2.3 %close.1 = (bf16[128,4096]{1,0:T(8,128)(2,1)}, f32[8,128]{1,0:T(8,128)}) custom-call(s32[7]{0:T(128)S(1)} %stack.40.refs_0_, f32[1]{0:T(128)S(6)} %copy.19.refs_1_, bf16[128,4096]{1,0:T(8,128)(2,1)S(1)} %bitcast.25, bf16[128,4096]{1,0:T(8,128)(2,1)S(1)} %get-tuple-element.122.refs_3_, bf16[128,4096]{1,0:T(8,128)(2,1)S(1)} %collective-permute-done.20.refs_4_, ...), custom_call_target="tpu_custom_call" | custom-call | flops 1150000000 | tf_op jit(solution)/shard_map/close/pallas_call | solution.py:448
  (80 shorter events, 14.9 us)
Async XLA Ops:
  0.0 3.1 %collective-permute-start = (bf16[128,4096]{1,0:T(8,128)(2,1)}, bf16[128,4096]{1,0:T(8,128)(2,1)S(1)}, u32[]{:S(2)}, u32[]{:S(2)}) collective-permute-start(bf16[128,4096]{1,0:T(8,128)(2,1)} %bitcast.20), channel_id=1, source_target_pairs={{0,8},{8,0},{16,24},{24,16},{1,9},{9,1},{17,25},{25,17},{2,10},{10... | collective-permute-start | bytes 3145736 | tf_op jit(solution)/shard_map/ppermute | solution.py:534
  0.5 28.0 %collective-permute-start.4 = (bf16[128,4096]{1,0:T(8,128)(2,1)}, bf16[128,4096]{1,0:T(8,128)(2,1)S(1)}, u32[]{:S(2)}, u32[]{:S(2)}) collective-permute-start(bf16[128,4096]{1,0:T(8,128)(2,1)} %bitcast.21), channel_id=1, source_target_pairs={{0,16},{8,24},{16,0},{24,8},{1,17},{9,25},{17,1},{25,9},{2,18},{10... | collective-permute-start | bytes 3145736 | tf_op jit(solution)/shard_map/ppermute | solution.py:539
  5.0 11.5 %copy-start.1 = (bf16[1,128,4096]{2,1,0:T(8,128)(2,1)S(1)}, bf16[1,128,4096]{2,1,0:T(8,128)(2,1)}, u32[]{:S(2)}) copy-start(bf16[1,128,4096]{2,1,0:T(8,128)(2,1)} %param.16) | copy-start | bytes 3145732
  5.0 11.5 %copy-start.4 = (bf16[4096,1024]{1,0:T(8,128)(2,1)S(1)}, bf16[4096,1024]{1,0:T(8,128)(2,1)}, u32[]{:S(2)}) copy-start(bf16[4096,1024]{1,0:T(8,128)(2,1)} %refs_5_.5) | copy-start | bytes 25165828
  5.0 11.5 %copy-start.5 = (bf16[4096,512]{1,0:T(8,128)(2,1)S(1)}, bf16[4096,512]{1,0:T(8,128)(2,1)}, u32[]{:S(2)}) copy-start(bf16[4096,512]{1,0:T(8,128)(2,1)} %refs_6_.5) | copy-start | bytes 12582916
  5.0 11.5 %copy-start.6 = (bf16[4096,16]{0,1:T(8,128)(2,1)S(1)}, bf16[4096,16]{0,1:T(8,128)(2,1)}, u32[]{:S(2)}) copy-start(bf16[4096,16]{0,1:T(8,128)(2,1)} %param.21) | copy-start | bytes 393220
  5.6 8.2 %collective-permute-start.1 = (bf16[16,2048]{1,0:T(8,128)(2,1)S(1)}, bf16[16,2048]{1,0:T(8,128)(2,1)S(1)}, u32[]{:S(2)}, u32[]{:S(2)}) collective-permute-start(bf16[16,2048]{1,0:T(8,128)(2,1)S(1)} %get-tuple-element.66), channel_id=1, source_target_pairs={{0,1},{1,2},{2,3},{3,4},{4,5},{5,6},{6,7},{7,0},{8,9},{9,10},{10,1... | collective-permute-start | bytes 196616 | tf_op jit(solution)/shard_map/ppermute | solution.py:530
  8.4 7.9 %collective-permute-start.2 = (bf16[16,2048]{1,0:T(8,128)(2,1)S(1)}, bf16[16,2048]{1,0:T(8,128)(2,1)S(1)}, u32[]{:S(2)}, u32[]{:S(2)}) collective-permute-start(bf16[16,2048]{1,0:T(8,128)(2,1)S(1)} %get-tuple-element.66), channel_id=1, source_target_pairs={{16,1},{17,2},{18,3},{19,4},{20,5},{21,6},{22,7},{23,0},{24,9},{25... | collective-permute-start | bytes 196616 | tf_op jit(solution)/shard_map/ppermute | solution.py:530
  28.4 2.7 %collective-permute-start.5 = (bf16[128,4096]{1,0:T(8,128)(2,1)S(1)}, bf16[128,4096]{1,0:T(8,128)(2,1)S(1)}, u32[]{:S(2)}, u32[]{:S(2)}) collective-permute-start(bf16[128,4096]{1,0:T(8,128)(2,1)S(1)} %hold.1.refs_1_), channel_id=1, source_target_pairs={{0,8},{8,0},{16,24},{24,16},{1,9},{9,1},{17,25},{25,17},{2,10},{10... | collective-permute-start | bytes 3145736 | tf_op jit(solution)/shard_map/ppermute | solution.py:534
  28.4 9.4 %collective-permute-start.3 = (bf16[144,1024]{1,0:T(8,128)(2,1)S(1)}, bf16[144,1024]{1,0:T(8,128)(2,1)S(1)}, u32[]{:S(2)}, u32[]{:S(2)}) collective-permute-start(bf16[144,1024]{1,0:T(8,128)(2,1)S(1)} %get-tuple-element.69), channel_id=1, source_target_pairs={{0,1},{1,0},{2,3},{3,2},{4,5},{5,4},{6,7},{7,6},{8,9},{9,8},{10,11... | collective-permute-start | bytes 884744 | tf_op jit(solution)/shard_map/ppermute | solution.py:534
  31.1 18.9 %slice-start = ((s8[8388608]{0:T(1024)(128)(4,1)}), s8[4194304]{0:T(1024)(128)(4,1)S(1)}, s32[]{:S(2)}) async-start(s8[8388608]{0:T(1024)(128)(4,1)} %bitcast.16), calls=%async_computation | async-start | bytes 8388608
  35.6 11.0 %collective-permute-start.7 = (bf16[144,1024]{1,0:T(8,128)(2,1)S(1)}, bf16[144,1024]{1,0:T(8,128)(2,1)S(1)}, u32[]{:S(2)}, u32[]{:S(2)}) collective-permute-start(bf16[144,1024]{1,0:T(8,128)(2,1)S(1)} %get-tuple-element.73.refs_1_), channel_id=1, source_target_pairs={{0,1},{1,0},{2,3},{3,2},{4,5},{5,4},{6,7},{7,6},{8,9},{9,8},{10,11... | collective-permute-start | bytes 884744 | tf_op jit(solution)/shard_map/ppermute | solution.py:534
  38.5 10.8 %collective-permute-start.6 = (bf16[144,1024]{1,0:T(8,128)(2,1)S(1)}, bf16[144,1024]{1,0:T(8,128)(2,1)S(1)}, u32[]{:S(2)}, u32[]{:S(2)}) collective-permute-start(bf16[144,1024]{1,0:T(8,128)(2,1)S(1)} %get-tuple-element.72.refs_1_), channel_id=1, source_target_pairs={{0,2},{1,3},{2,4},{3,5},{4,6},{5,7},{6,0},{7,1},{8,10},{9,11},{10,... | collective-permute-start | bytes 884744 | tf_op jit(solution)/shard_map/ppermute | solution.py:520
  45.1 8.4 %collective-permute-start.10 = (bf16[144,1024]{1,0:T(8,128)(2,1)S(1)}, bf16[144,1024]{1,0:T(8,128)(2,1)S(1)}, u32[]{:S(2)}, u32[]{:S(2)}) collective-permute-start(bf16[144,1024]{1,0:T(8,128)(2,1)S(1)} %get-tuple-element.79.refs_1_), channel_id=1, source_target_pairs={{0,1},{1,0},{2,3},{3,2},{4,5},{5,4},{6,7},{7,6},{8,9},{9,8},{10,11... | collective-permute-start | bytes 884744 | tf_op jit(solution)/shard_map/ppermute | solution.py:534
  47.3 9.9 %collective-permute-start.9 = (bf16[144,1024]{1,0:T(8,128)(2,1)S(1)}, bf16[144,1024]{1,0:T(8,128)(2,1)S(1)}, u32[]{:S(2)}, u32[]{:S(2)}) collective-permute-start(bf16[144,1024]{1,0:T(8,128)(2,1)S(1)} %get-tuple-element.78.refs_1_), channel_id=1, source_target_pairs={{0,2},{1,3},{2,4},{3,5},{4,6},{5,7},{6,0},{7,1},{8,10},{9,11},{10,... | collective-permute-start | bytes 884744 | tf_op jit(solution)/shard_map/ppermute | solution.py:520
  50.0 19.0 %slice-start.2 = ((s8[8388608]{0:T(1024)(128)(4,1)}), s8[4194304]{0:T(1024)(128)(4,1)S(1)}, s32[]{:S(2)}) async-start(s8[8388608]{0:T(1024)(128)(4,1)} %bitcast.18), calls=%async_computation.2 | async-start | bytes 8388608
  52.6 16.4 %copy-start.2 = (f32[1024]{0:T(1024)S(1)}, f32[1024]{0:T(1024)}, u32[]{:S(2)}) copy-start(f32[1024]{0:T(1024)} %param.29) | copy-start | bytes 12292
  57.3 11.7 %slice-start.3 = ((s8[8388608]{0:T(1024)(128)(4,1)}), s8[4194304]{0:T(1024)(128)(4,1)S(1)}, s32[]{:S(2)}) async-start(s8[8388608]{0:T(1024)(128)(4,1)} %bitcast.18), calls=%async_computation.3 | async-start | bytes 8388608
  57.9 11.1 %collective-permute-start.11 = (bf16[128,1024]{1,0:T(8,128)(2,1)S(1)}, bf16[128,1024]{1,0:T(8,128)(2,1)S(1)}, u32[]{:S(2)}, u32[]{:S(2)}) collective-permute-start(bf16[128,1024]{1,0:T(8,128)(2,1)S(1)} %get-tuple-element.87), channel_id=1, source_target_pairs={{0,2},{1,3},{2,4},{3,5},{4,6},{5,7},{6,0},{7,1},{8,10},{9,11},{10,... | collective-permute-start | bytes 786440 | tf_op jit(solution)/shard_map/ppermute | solution.py:520
  58.0 16.6 %collective-permute-start.8 = (bf16[128,1024]{1,0:T(8,128)(2,1)S(1)}, bf16[128,1024]{1,0:T(8,128)(2,1)S(1)}, u32[]{:S(2)}, u32[]{:S(2)}) collective-permute-start(bf16[128,1024]{1,0:T(8,128)(2,1)S(1)} %get-tuple-element.77), channel_id=1, source_target_pairs={{0,2},{1,3},{2,4},{3,5},{4,6},{5,7},{6,0},{7,1},{8,10},{9,11},{10,... | collective-permute-start | bytes 786440 | tf_op jit(solution)/shard_map/ppermute | solution.py:520
  59.3 18.8 %collective-permute-start.13 = (bf16[144,1024]{1,0:T(8,128)(2,1)S(1)}, bf16[144,1024]{1,0:T(8,128)(2,1)S(1)}, u32[]{:S(2)}, u32[]{:S(2)}) collective-permute-start(bf16[144,1024]{1,0:T(8,128)(2,1)S(1)} %get-tuple-element.103.refs_1_), channel_id=1, source_target_pairs={{0,2},{1,3},{2,4},{3,5},{4,6},{5,7},{6,0},{7,1},{8,10},{9,11},{10,... | collective-permute-start | bytes 884744 | tf_op jit(solution)/shard_map/ppermute | solution.py:520
  71.6 4.3 %collective-permute-start.14 = (bf16[64,2048]{1,0:T(8,128)(2,1)S(1)}, bf16[64,2048]{1,0:T(8,128)(2,1)S(1)}, u32[]{:S(2)}, u32[]{:S(2)}) collective-permute-start(bf16[64,2048]{1,0:T(8,128)(2,1)S(1)} %get-tuple-element.105), channel_id=1, source_target_pairs={{0,8},{8,0},{16,24},{24,16},{1,9},{9,1},{17,25},{25,17},{2,10},{10... | collective-permute-start | bytes 786440 | tf_op jit(solution)/shard_map/ppermute | solution.py:534
  71.7 4.2 %collective-permute-start.15 = (bf16[64,2048]{1,0:T(8,128)(2,1)S(1)}, bf16[64,2048]{1,0:T(8,128)(2,1)S(1)}, u32[]{:S(2)}, u32[]{:S(2)}) collective-permute-start(bf16[64,2048]{1,0:T(8,128)(2,1)S(1)} %get-tuple-element.106), channel_id=1, source_target_pairs={{0,8},{8,0},{16,24},{24,16},{1,9},{9,1},{17,25},{25,17},{2,10},{10... | collective-permute-start | bytes 786440 | tf_op jit(solution)/shard_map/ppermute | solution.py:534
  75.3 9.4 %collective-permute-start.12 = (bf16[128,1024]{1,0:T(8,128)(2,1)S(1)}, bf16[128,1024]{1,0:T(8,128)(2,1)S(1)}, u32[]{:S(2)}, u32[]{:S(2)}) collective-permute-start(bf16[128,1024]{1,0:T(8,128)(2,1)S(1)} %get-tuple-element.98), channel_id=1, source_target_pairs={{0,1},{1,0},{2,3},{3,2},{4,5},{5,4},{6,7},{7,6},{8,9},{9,8},{10,11... | collective-permute-start | bytes 786440 | tf_op jit(solution)/shard_map/ppermute | solution.py:534
  78.8 8.4 %collective-permute-start.16 = (bf16[128,1024]{1,0:T(8,128)(2,1)S(1)}, bf16[128,1024]{1,0:T(8,128)(2,1)S(1)}, u32[]{:S(2)}, u32[]{:S(2)}) collective-permute-start(bf16[128,1024]{1,0:T(8,128)(2,1)S(1)} %get-tuple-element.112), channel_id=1, source_target_pairs={{0,2},{1,3},{2,4},{3,5},{4,6},{5,7},{6,0},{7,1},{8,10},{9,11},{10,... | collective-permute-start | bytes 786440 | tf_op jit(solution)/shard_map/ppermute | solution.py:520
  79.1 11.3 %collective-permute-start.19 = (bf16[64,4096]{1,0:T(8,128)(2,1)S(1)}, bf16[64,4096]{1,0:T(8,128)(2,1)S(1)}, u32[]{:S(2)}, u32[]{:S(2)}) collective-permute-start(bf16[64,4096]{1,0:T(8,128)(2,1)S(1)} %get-tuple-element.119), channel_id=1, source_target_pairs={{0,16},{8,24},{16,0},{24,8},{1,17},{9,25},{17,1},{25,9},{2,18},{10... | collective-permute-start | bytes 1572872 | tf_op jit(solution)/shard_map/ppermute | solution.py:539
  89.8 1.6 %collective-permute-start.17 = (bf16[64,2048]{1,0:T(8,128)(2,1)S(1)}, bf16[64,2048]{1,0:T(8,128)(2,1)S(1)}, u32[]{:S(2)}, u32[]{:S(2)}) collective-permute-start(bf16[64,2048]{1,0:T(8,128)(2,1)S(1)} %get-tuple-element.117), channel_id=1, source_target_pairs={{0,8},{8,0},{16,24},{24,16},{1,9},{9,1},{17,25},{25,17},{2,10},{10... | collective-permute-start | bytes 786440 | tf_op jit(solution)/shard_map/ppermute | solution.py:534
  89.9 1.9 %collective-permute-start.18 = (bf16[64,2048]{1,0:T(8,128)(2,1)S(1)}, bf16[64,2048]{1,0:T(8,128)(2,1)S(1)}, u32[]{:S(2)}, u32[]{:S(2)}) collective-permute-start(bf16[64,2048]{1,0:T(8,128)(2,1)S(1)} %get-tuple-element.118), channel_id=1, source_target_pairs={{0,8},{8,0},{16,24},{24,16},{1,9},{9,1},{17,25},{25,17},{2,10},{10... | collective-permute-start | bytes 786440 | tf_op jit(solution)/shard_map/ppermute | solution.py:534
  92.5 14.0 %collective-permute-start.21 = (bf16[64,4096]{1,0:T(8,128)(2,1)S(1)}, bf16[64,4096]{1,0:T(8,128)(2,1)S(1)}, u32[]{:S(2)}, u32[]{:S(2)}) collective-permute-start(bf16[64,4096]{1,0:T(8,128)(2,1)S(1)} %get-tuple-element.124), channel_id=1, source_target_pairs={{0,16},{8,24},{16,0},{24,8},{1,17},{9,25},{17,1},{25,9},{2,18},{10... | collective-permute-start | bytes 1572872 | tf_op jit(solution)/shard_map/ppermute | solution.py:539
  98.6 9.8 %collective-permute-start.20 = (bf16[128,4096]{1,0:T(8,128)(2,1)S(1)}, bf16[128,4096]{1,0:T(8,128)(2,1)S(1)}, u32[]{:S(2)}, u32[]{:S(2)}) collective-permute-start(bf16[128,4096]{1,0:T(8,128)(2,1)S(1)} %get-tuple-element.123), channel_id=1, source_target_pairs={{0,8},{8,0},{16,24},{24,16},{1,9},{9,1},{17,25},{25,17},{2,10},{10... | collective-permute-start | bytes 3145736 | tf_op jit(solution)/shard_map/ppermute | solution.py:534
  98.7 8.5 %collective-permute-start.22 = (bf16[64,4096]{1,0:T(8,128)(2,1)S(1)}, bf16[64,4096]{1,0:T(8,128)(2,1)S(1)}, u32[]{:S(2)}, u32[]{:S(2)}) collective-permute-start(bf16[64,4096]{1,0:T(8,128)(2,1)S(1)} %collective-permute-done.19.refs_4_.refs_5_), channel_id=1, source_target_pairs={{0,8},{8,0},{16,24},{24,16},{1,9},{9,1},{17,25},{25,17},{2,10},{10... | collective-permute-start | bytes 1572872 | tf_op jit(solution)/shard_map/ppermute | solution.py:534
  106.5 1.9 %collective-permute-start.23 = (bf16[64,4096]{1,0:T(8,128)(2,1)S(1)}, bf16[64,4096]{1,0:T(8,128)(2,1)S(1)}, u32[]{:S(2)}, u32[]{:S(2)}) collective-permute-start(bf16[64,4096]{1,0:T(8,128)(2,1)S(1)} %collective-permute-done.21.refs_6_), channel_id=1, source_target_pairs={{0,8},{8,0},{16,24},{24,16},{1,9},{9,1},{17,25},{25,17},{2,10},{10... | collective-permute-start | bytes 1572872 | tf_op jit(solution)/shard_map/ppermute | solution.py:534
  (11 other events, 90.3 us)
